TPU v7x, 512 devices: a whole 4x8x8 slice. The times are simulated.
512 devices in a mesh: row: 16 (over y, core), col: 32 (over x, z).
Axes of the slice: x: 4, y: 8, z: 8, core: 2. Of those that a mesh axis runs over, the one named last changes fastest.
Arguments:
- tokens: bfloat16 [4096, 4096], P('row', 'col'), may hold values from -6 to 6
- gate_weight: bfloat16 [4096, 16384], P('row', 'col'), may hold values from -0.1875 to 0.1875
- up_weight: bfloat16 [4096, 16384], P('row', 'col'), may hold values from -0.1875 to 0.1875
- gate_mask: int32 [32, 128], P('row', 'col'), may hold values from 0 to 1, as said below
- up_mask: int32 [32, 128], P('row', 'col'), may hold values from 0 to 1, as said below
- cotangent: bfloat16 [4096, 16384], P('row', 'col'), may hold values from -6 to 6
Outputs:
- hidden: bfloat16 [4096, 16384], P('row', 'col')
- grad_tokens: bfloat16 [4096, 4096], P('row', 'col')
- grad_gate: bfloat16 [4096, 16384], P('row', 'col')
- grad_up: bfloat16 [4096, 16384], P('row', 'col')
Inputs may be any that keep to these rules, and one draw needn't show every extreme that they name: `gate_mask`: blocks are aligned 128 x 128 squares; each device's tile of 2 x 4 blocks keeps between 1 and 2 of them, and some tile keeps exactly 2. `up_mask`: as for gate_mask, drawn independently.
All inputs are finite; a program needn't handle non-finite values.
Results may differ from a plain program's by a relative error of at most 0.022.
Values may be sent and summed in bfloat16 or wider, within the bound.
No kernel may reach another device: no remote copies, remote signals or barrier semaphores. Data moves between devices by JAX's collectives and lax.ppermute only.
A program may use at most 128 MiB of HBM per device.

v0:
```python
import jax
import jax.numpy as jnp
from jax import lax
from jax.sharding import PartitionSpec as P

BLK = 128


def choose_slots(flat_mask, capacity):
    position = jnp.cumsum(flat_mask, axis=-1) - 1
    slot_ids = jnp.arange(capacity, dtype=jnp.int32)
    chosen = (flat_mask[..., None, :] == 1) & (position[..., None, :] == slot_ids[:, None])
    return chosen.astype(jnp.float32)


def unpack_slots(slot_data, selector, row_blocks, col_blocks):
    shards = selector.shape[0]
    dense_blocks = jnp.einsum(
        "nsp,nsab->npab",
        selector.astype(jnp.bfloat16),
        slot_data,
        preferred_element_type=jnp.float32,
    )
    dense_blocks = dense_blocks.astype(jnp.bfloat16).reshape(
        shards, row_blocks, col_blocks, BLK, BLK
    )
    return dense_blocks.transpose(0, 1, 3, 2, 4).reshape(
        shards * row_blocks * BLK, col_blocks * BLK
    )


def masked_tile(weight, block_mask):
    expanded = jnp.repeat(jnp.repeat(block_mask, BLK, axis=0), BLK, axis=1)
    return weight * expanded.astype(jnp.bfloat16)


def pack_grads(partial_value, selector, row_blocks, col_blocks):
    shards = selector.shape[0]
    blocks = partial_value.reshape(shards, row_blocks, BLK, col_blocks, BLK).transpose(
        0, 1, 3, 2, 4
    )
    blocks = blocks.reshape(shards, row_blocks * col_blocks, BLK, BLK)
    return jnp.einsum("nsp,npab->nsab", selector, blocks, precision=lax.Precision.HIGHEST)


def body(tokens, gate_weight, up_weight, gate_mask, up_mask, cotangent):
    row_count = lax.axis_size("row")
    row_blocks, col_blocks = gate_mask.shape
    per_tile = row_blocks * col_blocks
    capacity = per_tile // 4
    gathered = lax.all_gather(tokens, "col", axis=1, tiled=True)
    gate_send = gate_mask.astype(jnp.bfloat16)
    up_send = up_mask.astype(jnp.bfloat16)
    gate_full, up_full, gate_masks, up_masks = (
        lax.all_gather(masked_tile(gate_weight, gate_mask), "row", axis=0, tiled=True),
        lax.all_gather(masked_tile(up_weight, up_mask), "row", axis=0, tiled=True),
        lax.all_gather(gate_send, "row", axis=0, tiled=True),
        lax.all_gather(up_send, "row", axis=0, tiled=True),
    )
    gate_flat = gate_masks.astype(jnp.int32).reshape(row_count, per_tile)
    up_flat = up_masks.astype(jnp.int32).reshape(row_count, per_tile)
    gate_select = choose_slots(gate_flat, capacity)
    up_select = choose_slots(up_flat, capacity)
    gate_value = jnp.dot(gathered, gate_full, preferred_element_type=jnp.float32)
    up_value = jnp.dot(gathered, up_full, preferred_element_type=jnp.float32)
    sigma = jax.nn.sigmoid(gate_value)
    hidden = (gate_value * sigma * up_value).astype(jnp.bfloat16)
    cot = cotangent.astype(jnp.float32)
    grad_gval = (cot * up_value * sigma * (1.0 + gate_value * (1.0 - sigma))).astype(jnp.bfloat16)
    grad_uval = (cot * gate_value * sigma).astype(jnp.bfloat16)
    term = jnp.dot(gate_full, grad_gval.T, preferred_element_type=jnp.float32)
    own_rows = lax.psum_scatter(
        (term + jnp.dot(up_full, grad_uval.T, preferred_element_type=jnp.float32)).astype(
            jnp.bfloat16
        ),
        "col",
        scatter_dimension=0,
        tiled=True,
    ).astype(jnp.float32)
    grad_tokens = own_rows.T.astype(jnp.bfloat16)
    contract = (((0,), (0,)), ((), ()))
    partial_g = lax.dot_general(gathered, grad_gval, contract, preferred_element_type=jnp.float32)
    partial_u = lax.dot_general(gathered, grad_uval, contract, preferred_element_type=jnp.float32)
    packed_g = pack_grads(partial_g, gate_select, row_blocks, col_blocks)
    packed_u = pack_grads(partial_u, up_select, row_blocks, col_blocks)
    summed_g, summed_u = (
        lax.psum_scatter(
            packed_g.astype(jnp.bfloat16), "row", scatter_dimension=0, tiled=True
        ).astype(jnp.float32),
        lax.psum_scatter(
            packed_u.astype(jnp.bfloat16), "row", scatter_dimension=0, tiled=True
        ).astype(jnp.float32),
    )
    own_gate = choose_slots(gate_mask.reshape(1, per_tile), capacity)
    own_up = choose_slots(up_mask.reshape(1, per_tile), capacity)
    grad_gate = unpack_slots(summed_g.astype(jnp.bfloat16), own_gate, row_blocks, col_blocks)
    grad_up = unpack_slots(summed_u.astype(jnp.bfloat16), own_up, row_blocks, col_blocks)
    return (hidden, grad_tokens, grad_gate, grad_up)


def solution(mesh):
    return jax.shard_map(
        body,
        mesh=mesh,
        in_specs=(
            P("row", "col"),
            P("row", "col"),
            P("row", "col"),
            P("row", "col"),
            P("row", "col"),
            P("row", "col"),
        ),
        out_specs=(P("row", "col"), P("row", "col"), P("row", "col"), P("row", "col")),
        check_vma=False,
    )
```

profile of v0, /device:TPU:8, one launch (start us, length us, event | category | flops | bytes accessed | tf_op | source)
XLA Modules:
  0.0 546.8 jit_solution(16565639404005226371)
XLA Ops:
  7.2 0.0 all-gather.8.cloned.1.call-start
  7.2 0.7 all-gather.8.cloned.1.call-update
  7.9 0.0 all-gather.6.cloned.1.call-start
  7.9 0.7 convert_element_type.94
  8.6 0.3 broadcast_in_dim.17
  9.0 1.7 bitcast_multiply_fusion.1
  10.7 0.0 all-gather.6.cloned.1.call-update
  10.7 0.0 all-gather.10.cloned.1.call-start
  10.8 0.7 convert_element_type.97
  11.5 0.3 broadcast_in_dim.19
  11.8 1.7 bitcast_multiply_fusion
  13.5 0.0 all-gather.10.cloned.1.call-update
  13.5 0.0 reduce-scatter.8.cloned.1.call-start
  13.6 0.7 convert_bitcast_fusion
  14.3 19.8 %all-gather.1 = bf16[16,2,4]{2,1,0:T(2,128)(2,1)S(1)} all-gather(bf16[1,2,4]{2,1,0:T(2,128)(2,1)S(1)} %convert_bitcast_fusion), channel_id=1, replica_groups=mesh['row'=16,'col'=32] {'row'}, dimensions={0}, use_global_device_ids=true | all-gather | bytes 272 | tf_op jit(solution)/shard_map/all_gather | solution.py:58
  34.1 0.1 copy.48
  34.2 0.1 copy.49
  34.3 0.1 copy.50
  34.4 1.1 copy.40
  35.5 61.3 %all-gather.8.cloned.1.call-done = bf16[256,4096]{1,0:T(8,128)(2,1)} async-done(((bf16[256,128]{1,0:T(8,128)(2,1)}), bf16[256,4096]{1,0:T(8,128)(2,1)}) %all-gather.8.cloned.1.call-update) | async-done | bytes 2097168 | tf_op jit(solution)/shard_map/all_gather | solution.py:51
  96.8 45.9 %all-gather.6.cloned.1.call-done = bf16[4096,512]{1,0:T(8,128)(2,1)} async-done(((bf16[256,512]{1,0:T(8,128)(2,1)}), bf16[4096,512]{1,0:T(8,128)(2,1)}) %all-gather.6.cloned.1.call-update) | async-done | bytes 4194320 | tf_op jit(solution)/shard_map/all_gather | solution.py:55
  142.7 4.2 convolution_bitcast_fusion.3
  146.9 0.0 copy-done.1
  146.9 4.5 convolution_bitcast_fusion
  151.4 11.7 %reshape.233 = f32[16,2,128,4,128]{2,1,0,4,3:T(2,128)} reshape(f32[4096,512]{0,1:T(8,128)} %convolution_bitcast_fusion) | data formatting | bytes 16777216 | tf_op jit(solution)/shard_map/reshape | solution.py:39
  163.1 13.3 %copy.51 = f32[16,2,4,128,128]{4,2,1,3,0:T(4,128)} copy(f32[16,2,4,128,128]{3,1,0,4,2:T(2,128)} %bitcast.85) | data formatting | bytes 16777216 | tf_op jit(solution)/shard_map/transpose | solution.py:39
  176.4 7.7 %convolution_convert_fusion = bf16[16,2,128,128]{3,1,2,0:T(2,128)(2,1)S(1)} fusion(f32[16,8,128,128]{3,1,2,0:T(8,128)} %bitcast.83, pred[16,8]{1,0:T(8,128)(4,1)S(1)} %copy.49, s32[16,8]{1,0:T(8,128)S(1)} %copy.50), kind=kOutput, calls=%fused_computation.4 | convolution fusion | flops 50856448 | bytes 9437824 | tf_op jit(solution)/shard_map/nsp,npab->nsab/dot_general | solution.py:43
  184.1 1.3 copy.52
  185.4 0.0 reduce-scatter.8.cloned.1.call-update
  185.4 0.0 reduce-scatter.6.cloned.1.call-start
  185.5 0.0 copy-done.2
  185.5 14.9 %all-gather = bf16[16,2,4]{2,1,0:T(2,128)(2,1)S(1)} all-gather(bf16[1,2,4]{2,1,0:T(2,128)(2,1)S(1)} %convert_bitcast_fusion.1), channel_id=1, replica_groups=mesh['row'=16,'col'=32] {'row'}, dimensions={0}, use_global_device_ids=true | all-gather | bytes 272 | tf_op jit(solution)/shard_map/all_gather | solution.py:57
  200.5 0.1 copy.41
  200.6 0.1 copy.42
  200.7 0.1 copy.43
  200.8 3.6 fusion.3
  204.3 4.5 convolution_bitcast_fusion.1
  208.8 11.8 %reshape.227 = f32[16,2,128,4,128]{2,1,0,4,3:T(2,128)} reshape(f32[4096,512]{0,1:T(8,128)} %convolution_bitcast_fusion.1) | data formatting | bytes 16777216 | tf_op jit(solution)/shard_map/reshape | solution.py:39
  220.6 13.2 %copy.44 = f32[16,2,4,128,128]{4,2,1,3,0:T(4,128)} copy(f32[16,2,4,128,128]{3,1,0,4,2:T(2,128)} %bitcast.86) | data formatting | bytes 16777216 | tf_op jit(solution)/shard_map/transpose | solution.py:39
  233.8 7.6 %convolution_convert_fusion.1 = bf16[16,2,128,128]{3,1,2,0:T(2,128)(2,1)S(1)} fusion(f32[16,8,128,128]{3,1,2,0:T(8,128)} %bitcast.84, pred[16,8]{1,0:T(8,128)(4,1)S(1)} %copy.42, s32[16,8]{1,0:T(8,128)S(1)} %copy.43), kind=kOutput, calls=%fused_computation.5 | convolution fusion | flops 50856448 | bytes 9437824 | tf_op jit(solution)/shard_map/nsp,npab->nsab/dot_general | solution.py:43
  241.4 1.3 copy.45
  242.6 0.0 reduce-scatter.6.cloned.1.call-update
  242.7 0.3 reduce-scatter.4.cloned.1.call-start
  242.9 0.0 copy-start
  243.0 3.6 fusion.30
  246.6 0.0 copy-start.3
  246.6 2.7 fusion
  249.3 0.0 reduce-scatter.4.cloned.1.call-update
  249.3 0.1 reshape.226
  249.4 0.1 reshape.232
  249.5 0.2 reduce-window.14
  249.7 0.1 eq.99
  249.8 0.2 reduce-window.15
  250.0 0.1 eq.108
  250.1 0.8 copy.55
  250.9 1.1 convolution_convert_fusion.2
  252.0 0.1 copy.54
  252.1 0.7 copy.71
  252.9 56.8 %reduce-scatter.6.cloned.1.call-done = bf16[1,2,128,128]{3,2,1,0:T(8,128)(2,1)} async-done(((bf16[16,2,128,128]{3,2,1,0:T(8,128)(2,1)}), bf16[1,2,128,128]{3,2,1,0:T(8,128)(2,1)}) %reduce-scatter.6.cloned.1.call-update) | async-done | bytes 65552 | tf_op jit(solution)/shard_map/reduce_scatter | solution.py:87
  309.6 1.1 convolution_convert_fusion.3
  310.8 0.1 copy.47
  310.9 0.7 copy.72
  311.6 226.8 %reduce-scatter.4.cloned.1.call-done = bf16[128,256]{1,0:T(8,128)(2,1)} async-done(((bf16[4096,256]{1,0:T(8,128)(2,1)}), bf16[128,256]{1,0:T(8,128)(2,1)}) %reduce-scatter.4.cloned.1.call-update) | async-done | bytes 65552 | tf_op jit(solution)/shard_map/reduce_scatter | solution.py:72
  538.4 1.6 copy.56
  (21 shorter events, 0.1 us)
Async XLA Ops:
  7.2 89.6 %all-gather.8.cloned.1.call-start = ((), (), s32[]{:S(2)}) async-start(), calls=%async_computation.4 | async-start | bytes 2162688 | tf_op jit(solution)/shard_map/all_gather | solution.py:51
  7.9 134.8 %all-gather.6.cloned.1.call-start = ((), (), s32[]{:S(2)}) async-start(), calls=%async_computation.3 | async-start | bytes 4456448 | tf_op jit(solution)/shard_map/all_gather | solution.py:55
  10.7 190.1 %all-gather.10.cloned.1.call-start = ((), (), s32[]{:S(2)}) async-start(), calls=%async_computation.5 | async-start | bytes 4456448 | tf_op jit(solution)/shard_map/all_gather | solution.py:56
  13.5 237.4 %reduce-scatter.8.cloned.1.call-start = ((), (), s32[]{:S(2)}) async-start(), calls=%async_computation.8 | async-start | bytes 1114112 | tf_op jit(solution)/shard_map/reduce_scatter | solution.py:90
  96.8 50.0 %copy-start.1 = (bf16[256,4096]{1,0:T(8,128)(2,1)S(1)}, bf16[256,4096]{1,0:T(8,128)(2,1)}, u32[]{:S(2)}) copy-start(bf16[256,4096]{1,0:T(8,128)(2,1)} %all-gather.8.cloned.1.call-done) | copy-start | bytes 6291460
  176.4 9.1 %copy-start.2 = (s32[2,4]{1,0:T(2,128)S(1)}, s32[2,4]{1,0:T(2,128)}, u32[]{:S(2)}) copy-start(s32[2,4]{1,0:T(2,128)} %param.9) | copy-start | bytes 100
  185.4 124.2 %reduce-scatter.6.cloned.1.call-start = ((), (), s32[]{:S(2)}) async-start(), calls=%async_computation.7 | async-start | bytes 1114112 | tf_op jit(solution)/shard_map/reduce_scatter | solution.py:87
  242.7 295.7 %reduce-scatter.4.cloned.1.call-start = ((), (), s32[]{:S(2)}) async-start(), calls=%async_computation.6 | async-start | bytes 2162688 | tf_op jit(solution)/shard_map/reduce_scatter | solution.py:72
  242.9 3.6 copy-start
  246.6 2.8 copy-start.3
Sparse Core Ops, SparseCore 0:
  11.0 85.7 all-gather.7
  99.5 43.1 all-gather.5
  145.4 43.7 all-gather.9
  191.8 56.0 reduce-scatter.7
  250.8 58.7 reduce-scatter.5
  313.9 224.4 reduce-scatter.3
where the time goes:
time: 548 us; the launch traced here: 547 us
  waiting for transfers between devices  392 us (72%)
  local copies, waits for them, and re-layouts  59.3 us (11%)
  matrix products  40.6 us (7%)
  blocking collectives  34.8 us (6%)
  between operations  14.3 us (3%)
  other arithmetic  5.93 us (1%)
    reduce_scatter x1, waiting for transfers between devices, body(): lax.psum_scatter((term + jnp.dot(up_full, grad_uval.T, preferred_element_...  227 us
    all_gather x1, waiting for transfers between devices, body(): gathered = lax.all_gather(tokens, 'col', axis=1, tiled=True)  61.3 us
    reduce_scatter x1, waiting for transfers between devices, body(): lax.psum_scatter(packed_g.astype(jnp.bfloat16), 'row', scatter_dimension=...  56.8 us
    all_gather x1, waiting for transfers between devices, body(): lax.all_gather(masked_tile(gate_weight, gate_mask), 'row', axis=0, tiled=...  45.9 us
    transpose x2, local copies, waits for them, and re-layouts, pack_grads(): partial_value.reshape(shards, row_blocks, BLK, col_blocks, BLK)  26.5 us
    reshape x2, local copies, waits for them, and re-layouts, pack_grads(): partial_value.reshape(shards, row_blocks, BLK, col_blocks, BLK)  23.5 us
    all_gather x1, blocking collectives, body(): lax.all_gather(up_send, 'row', axis=0, tiled=True)  19.8 us
    dot_general x2, matrix products, pack_grads(): jnp.einsum('nsp,npab->nsab', selector, blocks, precision=lax.Precision.HI...  15.3 us
  transfers between devices with their start and end apart: 6, of which 4 were waited for; matrix products, arithmetic and copies ran while one was open for 19% of the time, Pallas kernels for 0%

commit v1 on v0

v1 whole, which is shorter than its diff:
```python
import jax
import jax.numpy as jnp
from jax import lax
from jax.experimental import pallas as pl
from jax.experimental.pallas import tpu as pltpu
from jax.sharding import PartitionSpec as P

BLK = 128
SLOTS = 4
META = SLOTS * BLK
BF = jnp.bfloat16
F32 = jnp.float32
VMEM = pl.BlockSpec(memory_space=pltpu.VMEM)
SMEM = pl.BlockSpec(memory_space=pltpu.SMEM)


def params():
    return pltpu.CompilerParams(vmem_limit_bytes=40 * 1024 * 1024)


def call(kernel, outs, in_specs, scratch=()):
    return pl.pallas_call(
        kernel,
        out_shape=outs,
        in_specs=in_specs,
        out_specs=jax.tree.map(lambda _: VMEM, outs),
        scratch_shapes=list(scratch),
        compiler_params=params(),
    )


def kept(mask_ref):
    cols = mask_ref.shape[1]
    first, second, count = jnp.int32(0), jnp.int32(0), jnp.int32(0)
    for p in range(mask_ref.shape[0] * cols):
        m = mask_ref[p // cols, p % cols]
        on = m == 1
        first = jnp.where(on & (count == 0), p, first)
        second = jnp.where(on & (count == 1), p, second)
        count = count + m
    return first, second, count


def block_of(ref, p, cols):
    r = pl.multiple_of((p // cols) * BLK, BLK)
    c = pl.multiple_of((p % cols) * BLK, BLK)
    return r, c


def pack_kernel(gm_ref, um_ref, gw_ref, uw_ref, out_ref):
    cols = gm_ref.shape[1]
    positions = []
    for t, (m_ref, w_ref) in enumerate(((gm_ref, gw_ref), (um_ref, uw_ref))):
        first, second, count = kept(m_ref)
        for s, (p, on) in enumerate(((first, count >= 1), (second, count >= 2))):
            r, c = block_of(w_ref, p, cols)
            block = w_ref[pl.ds(r, BLK), pl.ds(c, BLK)].astype(F32)
            out_ref[pl.ds((2 * t + s) * BLK, BLK), :] = jnp.where(on, block, 0.0).astype(BF)
            positions.append(p)
    lane = lax.broadcasted_iota(jnp.int32, (out_ref.shape[0] - META, BLK), 1)
    meta = jnp.zeros(lane.shape, jnp.int32)
    for s, p in enumerate(positions):
        meta = jnp.where(lane == s, p, meta)
    out_ref[pl.ds(META, lane.shape[0]), :] = meta.astype(F32).astype(BF)


def front_kernel(cols, idx_ref, x_ref, w_ref, cot_ref, hid_ref, g_ref, wg_ref, acc, gt):
    shards = w_ref.shape[0]
    acc[...] = jnp.zeros_like(acc)
    for n in range(shards):
        for s in range(SLOTS):
            p = idx_ref[n, s]
            a = p % cols + (s // 2) * cols
            acc[a] += jnp.dot(
                x_ref[2 * n + p // cols],
                w_ref[n, pl.ds(s * BLK, BLK), :],
                preferred_element_type=F32,
            )
    for c in range(cols):
        gate, up = acc[c], acc[cols + c]
        lanes = pl.ds(c * BLK, BLK)
        cot = cot_ref[:, lanes].astype(F32)
        sigma = jax.nn.sigmoid(gate)
        hid_ref[:, lanes] = (gate * sigma * up).astype(BF)
        gg = cot * up * sigma * (1.0 + gate * (1.0 - sigma))
        gu = cot * gate * sigma
        g_ref[c] = gg.astype(BF)
        g_ref[cols + c] = gu.astype(BF)
        gt[c] = gg.T.astype(BF)
        gt[cols + c] = gu.T.astype(BF)
    for n in range(shards):
        for s in range(SLOTS):
            p = idx_ref[n, s]
            a = p % cols + (s // 2) * cols
            wg_ref[n, pl.ds(s * BLK, BLK), :] = jnp.dot(
                gt[a], x_ref[2 * n + p // cols], preferred_element_type=F32
            ).astype(BF)


def term_kernel(cols, idx_ref, g_ref, w_ref, out_ref):
    for n in range(w_ref.shape[0]):
        sums = [None, None]
        for s in range(SLOTS):
            p = idx_ref[n, s]
            prod = lax.dot_general(
                g_ref[p % cols + (s // 2) * cols],
                w_ref[n, pl.ds(s * BLK, BLK), :],
                (((1,), (1,)), ((), ())),
                preferred_element_type=F32,
            )
            for r in range(2):
                part = jnp.where(p // cols == r, prod, 0.0)
                sums[r] = part if sums[r] is None else sums[r] + part
        for r in range(2):
            out_ref[2 * n + r] = sums[r].astype(BF)


def sum_kernel(t_ref, out_ref):
    total = t_ref[0].astype(F32)
    for j in range(1, t_ref.shape[0]):
        total = total + t_ref[j].astype(F32)
    out_ref[...] = total.astype(BF)


def unpack_kernel(gm_ref, um_ref, b_ref, gg_ref, gu_ref):
    cols = gm_ref.shape[1]
    for t, (m_ref, o_ref) in enumerate(((gm_ref, gg_ref), (um_ref, gu_ref))):
        o_ref[...] = jnp.zeros_like(o_ref)
        first, second, count = kept(m_ref)
        for s, (p, on) in enumerate(((first, count >= 1), (second, count >= 2))):

            @pl.when(on)
            def _(p=p, s=s):
                r, c = block_of(o_ref, p, cols)
                block = b_ref[pl.ds((2 * t + s) * BLK, BLK), :].astype(F32)
                o_ref[pl.ds(r, BLK), pl.ds(c, BLK)] = block.T.astype(BF)


def body(tokens, gate_weight, up_weight, gate_mask, up_mask, cotangent):
    rows, cols_n = lax.axis_size("row"), lax.axis_size("col")
    tok, width = cotangent.shape
    blocks = gate_mask.shape[1]
    shape = jax.ShapeDtypeStruct

    packed = call(pack_kernel, shape((META + 16, BLK), BF), [SMEM, SMEM, VMEM, VMEM])(
        gate_mask, up_mask, gate_weight, up_weight
    )
    tokens, packed = lax.optimization_barrier((tokens, packed))
    weights = lax.all_gather(packed, "row", axis=0)
    x = lax.all_to_all(jnp.broadcast_to(tokens, (cols_n, *tokens.shape)), "col", 0, 0)
    index = weights[:, META, :SLOTS].astype(jnp.int32)

    hidden, grads, wgrads = call(
        lambda *refs: front_kernel(blocks, *refs),
        (
            shape((tok, width), BF),
            shape((2 * blocks, tok, BLK), BF),
            shape((rows, META, BLK), BF),
        ),
        [SMEM, VMEM, VMEM, VMEM],
        [pltpu.VMEM((2 * blocks, tok, BLK), F32), pltpu.VMEM((2 * blocks, BLK, tok), BF)],
    )(index, x, weights, cotangent)
    summed = lax.psum_scatter(wgrads, "row", scatter_dimension=0)
    terms = call(
        lambda *refs: term_kernel(blocks, *refs),
        shape((cols_n, tok, BLK), BF),
        [SMEM, VMEM, VMEM],
    )(index, grads, weights)
    terms = lax.all_to_all(terms, "col", 0, 0)
    grad_tokens = call(sum_kernel, shape(tokens.shape, BF), [VMEM])(terms)
    grad_gate, grad_up = call(
        unpack_kernel,
        (shape(gate_weight.shape, BF), shape(up_weight.shape, BF)),
        [SMEM, SMEM, VMEM],
    )(gate_mask, up_mask, summed)
    return hidden, grad_tokens, grad_gate, grad_up


def solution(mesh):
    spec = P("row", "col")
    return jax.shard_map(
        body, mesh=mesh, in_specs=(spec,) * 6, out_specs=(spec,) * 4, check_vma=False
    )
```

time: 548 us -> 158 us (0.29)
  the two profiles are of different devices: /device:TPU:8 before, /device:TPU:25 now
where the time goes in v1:
time: 158 us
  blocking collectives  54 us (34%)
  waiting for transfers between devices  53.4 us (34%)
  between operations  14.1 us (9%)
  starting transfers between devices  13.1 us (8%)
  local copies, waits for them, and re-layouts  12.6 us (8%)
  Pallas kernels  10 us (6%)
    all_to_all x1, blocking collectives, body(): terms = lax.all_to_all(terms, 'col', 0, 0)  54 us
    all_gather x1, waiting for transfers between devices, body(): weights = lax.all_gather(packed, 'row', axis=0)  31 us
    all_to_all x1, waiting for transfers between devices, body(): lax.all_to_all(jnp.broadcast_to(tokens, (cols_n, *tokens.shape)), 'col',...  17.1 us
    all_to_all x1, starting transfers between devices, body(): lax.all_to_all(jnp.broadcast_to(tokens, (cols_n, *tokens.shape)), 'col',...  13 us
    unnamed x26, local copies, waits for them, and re-layouts  9.99 us
    reduce_scatter x1, waiting for transfers between devices, body(): summed = lax.psum_scatter(wgrads, 'row', scatter_dimension=0)  5.25 us
    pallas_call x1, Pallas kernels, body(): call(lambda *refs: front_kernel(blocks, *refs), (shape((tok, width), BF),...  4.07 us
  transfers between devices with their start and end apart: 3, of which 3 were waited for; matrix products, arithmetic and copies ran while one was open for 2% of the time, Pallas kernels for 2%

profile of v1, /device:TPU:25, one launch (start us, length us, event | category | flops | bytes accessed | tf_op | source)
XLA Modules:
  0.0 157.9 jit_solution(3968388223714451922)
XLA Ops:
  7.2 0.0 all-gather.3.cloned.1.call-start
  7.2 0.0 copy-start.6
  7.2 0.9 copy-done.6
  8.2 0.0 copy-start.7
  8.2 0.9 copy-done.7
  9.1 0.0 copy-start.9
  9.1 0.7 copy-done.9
  9.8 0.0 copy-start.11
  9.8 0.7 copy-done.11
  10.5 1.3 shard_map.93
  11.8 0.0 all-gather.3.cloned.1.call-update
  11.8 2.6 %broadcast_in_dim.3 = bf16[32,256,128]{2,1,0:T(8,128)(2,1)} broadcast(bf16[256,128]{1,0:T(8,128)(2,1)} %param.6), dimensions={1,2} | broadcast | bytes 2162688 | tf_op jit(solution)/shard_map/broadcast_in_dim | solution.py:150
  14.4 0.0 copy-start.5
  14.4 13.0 %all-to-all-start = ((bf16[32,256,128]{2,1,0:T(8,128)(2,1)}), bf16[32,256,128]{2,1,0:T(8,128)(2,1)S(1)}, u32[]{:S(2)}, u32[]{:S(2)}) async-start(bf16[32,256,128]{2,1,0:T(8,128)(2,1)} %broadcast_in_dim.3), calls=%async_computation | async-start | bytes 4194304 | tf_op jit(solution)/shard_map/all_to_all | solution.py:150
  27.4 0.0 reduce-scatter.2.cloned.1.call-start
  27.5 31.0 %all-gather.3.cloned.1.call-done = bf16[8448,128]{1,0:T(8,128)(2,1)} async-done(((bf16[528,128]{1,0:T(8,128)(2,1)}), bf16[8448,128]{1,0:T(8,128)(2,1)}) %all-gather.3.cloned.1.call-update) | async-done | bytes 2162704 | tf_op jit(solution)/shard_map/all_gather | solution.py:149
  58.5 0.8 slice_convert_fusion
  59.2 17.1 %all-to-all-done.refs_1_ = bf16[32,256,128]{2,1,0:T(8,128)(2,1)S(1)} async-done(((bf16[32,256,128]{2,1,0:T(8,128)(2,1)}), bf16[32,256,128]{2,1,0:T(8,128)(2,1)S(1)}, u32[]{:S(2)}, u32[]{:S(2)}) %all-to-all-start) | async-done | bytes 2097184 | tf_op jit(solution)/shard_map/all_to_all | solution.py:150
  76.3 0.0 copy-start.2
  76.3 1.3 copy-done.2
  77.6 0.0 copy-done.5
  77.6 0.0 copy-start
  77.6 1.6 %copy-done = bf16[8448,128]{1,0:T(8,128)(2,1)S(1)} copy-done((bf16[8448,128]{1,0:T(8,128)(2,1)S(1)}, bf16[8448,128]{1,0:T(8,128)(2,1)}, u32[]{:S(2)}) %copy-start) | copy-done | bytes 2162712
  79.2 0.0 copy-start.3
  79.3 1.6 %copy-done.3 = bf16[32,256,128]{2,1,0:T(8,128)(2,1)S(1)} copy-done((bf16[32,256,128]{2,1,0:T(8,128)(2,1)S(1)}, bf16[32,256,128]{2,1,0:T(8,128)(2,1)}, u32[]{:S(2)}) %copy-start.3) | copy-done | bytes 2097176
  80.8 0.0 copy-start.1
  80.8 4.1 %shard_map.94 = (bf16[256,512]{1,0:T(8,128)(2,1)}, bf16[8,256,128]{2,1,0:T(8,128)(2,1)S(1)}, bf16[16,512,128]{2,1,0:T(8,128)(2,1)S(1)}) custom-call(s32[16,4]{1,0:T(8,128)S(1)} %bitcast.7, bf16[32,256,128]{2,1,0:T(8,128)(2,1)S(1)} %copy-done.3, bf16[16,528,128]{2,1,0:T(8,128)(2,1)S(1)} %bitcast.4, bf16[256,512]{1,0:T(8,128)(2,1)S(1)} %copy-done.5), custom_call_target="tpu_custom_call" | custom-call | tf_op jit(solution)/shard_map/pallas_call | solution.py:153
  84.9 0.0 copy-start.4
  84.9 1.3 copy-done.4
  86.2 0.0 reduce-scatter.2.cloned.1.call-update
  86.2 0.0 copy-done.1
  86.3 2.0 %shard_map.95 = bf16[32,256,128]{2,1,0:T(8,128)(2,1)S(1)} custom-call(s32[16,4]{1,0:T(8,128)S(1)} %bitcast.8, bf16[8,256,128]{2,1,0:T(8,128)(2,1)S(1)} %get-tuple-element.14.refs_1_, bf16[16,528,128]{2,1,0:T(8,128)(2,1)S(1)} %bitcast.5), custom_call_target="tpu_custom_call" | custom-call | tf_op jit(solution)/shard_map/pallas_call | solution.py:164
  88.3 54.0 %all_to_all.10.t_ref = bf16[32,256,128]{2,1,0:T(8,128)(2,1)S(1)} all-to-all(bf16[32,256,128]{2,1,0:T(8,128)(2,1)S(1)} %shard_map.95), channel_id=1, replica_groups=mesh['row'=16,'col'=32] {'col'}, dimensions={0} | all-to-all | bytes 4194304 | tf_op jit(solution)/shard_map/all_to_all | solution.py:169
  142.3 0.0 copy-start.10
  142.3 0.0 copy-start.12
  142.3 0.9 shard_map.96
  143.2 5.2 %reduce-scatter.2.cloned.1.call-done = bf16[1,512,128]{2,1,0:T(8,128)(2,1)} async-done(((bf16[16,512,128]{2,1,0:T(8,128)(2,1)}), bf16[1,512,128]{2,1,0:T(8,128)(2,1)}) %reduce-scatter.2.cloned.1.call-update) | async-done | bytes 131088 | tf_op jit(solution)/shard_map/reduce_scatter | solution.py:163
  148.5 0.0 copy-done.10
  148.5 0.0 copy-done.12
  148.5 0.0 copy-start.8
  148.5 0.9 copy-done.8
  149.4 1.7 %shard_map.97 = (bf16[256,512]{1,0:T(8,128)(2,1)}, bf16[256,512]{1,0:T(8,128)(2,1)}) custom-call(s32[2,4]{1,0:T(2,128)S(1)} %copy-done.10, s32[2,4]{1,0:T(2,128)S(1)} %copy-done.12, bf16[512,128]{1,0:T(8,128)(2,1)S(1)} %bitcast.6), custom_call_target="tpu_custom_call" | custom-call | tf_op jit(solution)/shard_map/pallas_call | solution.py:171
Async XLA Ops:
  7.2 51.3 %all-gather.3.cloned.1.call-start = ((), (), s32[]{:S(2)}) async-start(), calls=%async_computation.4 | async-start | bytes 2297856 | tf_op jit(solution)/shard_map/all_gather | solution.py:149
  7.2 1.0 copy-start.6
  8.2 0.9 copy-start.7
  9.1 0.7 copy-start.9
  9.8 0.7 copy-start.11
  14.4 63.2 %copy-start.5 = (bf16[256,512]{1,0:T(8,128)(2,1)S(1)}, bf16[256,512]{1,0:T(8,128)(2,1)}, u32[]{:S(2)}) copy-start(bf16[256,512]{1,0:T(8,128)(2,1)} %refs_3_.1) | copy-start | bytes 786436
  14.4 61.9 %all-to-all-start = ((bf16[32,256,128]{2,1,0:T(8,128)(2,1)}), bf16[32,256,128]{2,1,0:T(8,128)(2,1)S(1)}, u32[]{:S(2)}, u32[]{:S(2)}) async-start(bf16[32,256,128]{2,1,0:T(8,128)(2,1)} %broadcast_in_dim.3), calls=%async_computation | async-start | bytes 4194304 | tf_op jit(solution)/shard_map/all_to_all | solution.py:150
  27.4 121.1 %reduce-scatter.2.cloned.1.call-start = ((), (), s32[]{:S(2)}) async-start(), calls=%async_computation.3 | async-start | bytes 2228224 | tf_op jit(solution)/shard_map/reduce_scatter | solution.py:163
  76.3 1.3 copy-start.2
  77.6 1.6 %copy-start = (bf16[8448,128]{1,0:T(8,128)(2,1)S(1)}, bf16[8448,128]{1,0:T(8,128)(2,1)}, u32[]{:S(2)}) copy-start(bf16[8448,128]{1,0:T(8,128)(2,1)} %all-gather.3.cloned.1.call-done) | copy-start | bytes 6488068
  79.2 1.6 %copy-start.3 = (bf16[32,256,128]{2,1,0:T(8,128)(2,1)S(1)}, bf16[32,256,128]{2,1,0:T(8,128)(2,1)}, u32[]{:S(2)}) copy-start(bf16[32,256,128]{2,1,0:T(8,128)(2,1)} %copy-done.2) | copy-start | bytes 6291460
  80.8 5.4 %copy-start.1 = (bf16[8448,128]{1,0:T(8,128)(2,1)S(1)}, bf16[8448,128]{1,0:T(8,128)(2,1)}, u32[]{:S(2)}) copy-start(bf16[8448,128]{1,0:T(8,128)(2,1)} %all-gather.3.cloned.1.call-done) | copy-start | bytes 6488068
  84.9 1.3 copy-start.4
  142.3 6.2 %copy-start.10 = (s32[2,4]{1,0:T(2,128)S(1)}, s32[2,4]{1,0:T(2,128)}, u32[]{:S(2)}) copy-start(s32[2,4]{1,0:T(2,128)} %gm_ref.3) | copy-start | bytes 100
  142.3 6.2 %copy-start.12 = (s32[2,4]{1,0:T(2,128)S(1)}, s32[2,4]{1,0:T(2,128)}, u32[]{:S(2)}) copy-start(s32[2,4]{1,0:T(2,128)} %um_ref.3) | copy-start | bytes 100
  148.5 0.9 copy-start.8
Sparse Core Ops, SparseCore 0:
  11.9 46.5 all-gather.2
  86.4 62.0 reduce-scatter.1

commit v2 on v1

v2 whole, which is shorter than its diff:
```python
import jax
import jax.numpy as jnp
from jax import lax
from jax.experimental import pallas as pl
from jax.experimental.pallas import tpu as pltpu
from jax.sharding import Mesh
from jax.sharding import PartitionSpec as P

BLK = 128
SLOTS = 4
META = SLOTS * BLK
ROWS_A = 176
BF = jnp.bfloat16
F32 = jnp.float32
VMEM = pl.BlockSpec(memory_space=pltpu.VMEM)
SMEM = pl.BlockSpec(memory_space=pltpu.SMEM)


def params():
    return pltpu.CompilerParams(vmem_limit_bytes=40 * 1024 * 1024)


def call(kernel, outs, in_specs, scratch=()):
    return pl.pallas_call(
        kernel,
        out_shape=outs,
        in_specs=in_specs,
        out_specs=jax.tree.map(lambda _: VMEM, outs),
        scratch_shapes=list(scratch),
        compiler_params=params(),
    )


def kept(mask_ref):
    cols = mask_ref.shape[1]
    first, second, count = jnp.int32(0), jnp.int32(0), jnp.int32(0)
    for p in range(mask_ref.shape[0] * cols):
        m = mask_ref[p // cols, p % cols]
        on = m == 1
        first = jnp.where(on & (count == 0), p, first)
        second = jnp.where(on & (count == 1), p, second)
        count = count + m
    return first, second, count


def block_of(ref, p, cols):
    r = pl.multiple_of((p // cols) * BLK, BLK)
    c = pl.multiple_of((p % cols) * BLK, BLK)
    return r, c


def pack_kernel(gm_ref, um_ref, tok_ref, gw_ref, uw_ref, out_ref, a_ref, b_ref):
    cols = gm_ref.shape[1]
    positions = []
    for t, (m_ref, w_ref) in enumerate(((gm_ref, gw_ref), (um_ref, uw_ref))):
        first, second, count = kept(m_ref)
        for s, (p, on) in enumerate(((first, count >= 1), (second, count >= 2))):
            r, c = block_of(w_ref, p, cols)
            block = w_ref[pl.ds(r, BLK), pl.ds(c, BLK)].astype(F32)
            out_ref[pl.ds((2 * t + s) * BLK, BLK), :] = jnp.where(on, block, 0.0).astype(BF)
            positions.append(p)
    lane = lax.broadcasted_iota(jnp.int32, (out_ref.shape[0] - META, BLK), 1)
    meta = jnp.zeros(lane.shape, jnp.int32)
    for s, p in enumerate(positions):
        meta = jnp.where(lane == s, p, meta)
    out_ref[pl.ds(META, lane.shape[0]), :] = meta.astype(F32).astype(BF)
    for z in range(a_ref.shape[0]):
        a_ref[z] = tok_ref[pl.ds(0, a_ref.shape[1]), :]
    b_ref[...] = tok_ref[pl.ds(a_ref.shape[1], b_ref.shape[0]), :]


def front_kernel(blocks, me_ref, idx_ref, xa0, xa1, xa2, xa3, xb_ref, w_ref, cot_ref, *rest):
    hid_ref, g_ref, keep_ref, send_ref, x_ref, acc, gt = rest
    my_x, my_c = me_ref[0], me_ref[1]
    shards = w_ref.shape[0]
    zs, xs = xb_ref.shape[:2]
    split = xa0.shape[1]
    for k, xa_ref in enumerate((xa0, xa1, xa2, xa3)):
        first = lax.rem(my_x - k + xs, xs) * zs
        for z in range(zs):
            x_ref[first + z, pl.ds(0, split), :] = xa_ref[z]
            x_ref[first + z, pl.ds(split, xb_ref.shape[2]), :] = xb_ref[z, k]
    acc[...] = jnp.zeros_like(acc)
    for n in range(shards):
        for s in range(SLOTS):
            p = idx_ref[n, s]
            a = p % blocks + (s // 2) * blocks
            acc[a] += jnp.dot(
                x_ref[2 * n + p // blocks],
                w_ref[n, pl.ds(s * BLK, BLK), :],
                preferred_element_type=F32,
            )
    for c in range(blocks):
        gate, up = acc[c], acc[blocks + c]
        lanes = pl.ds(c * BLK, BLK)
        cot = cot_ref[:, lanes].astype(F32)
        sigma = jax.nn.sigmoid(gate)
        hid_ref[:, lanes] = (gate * sigma * up).astype(BF)
        gg = cot * up * sigma * (1.0 + gate * (1.0 - sigma))
        gu = cot * gate * sigma
        g_ref[c] = gg.astype(BF)
        g_ref[blocks + c] = gu.astype(BF)
        gt[c] = gg.T.astype(BF)
        gt[blocks + c] = gu.T.astype(BF)
    for out_ref, core in ((send_ref, 1 - my_c), (keep_ref, my_c)):
        for y in range(shards // 2):
            n = 2 * y + core
            for s in range(SLOTS):
                p = idx_ref[n, s]
                a = p % blocks + (s // 2) * blocks
                out_ref[y, pl.ds(s * BLK, BLK), :] = jnp.dot(
                    gt[a], x_ref[2 * n + p // blocks], preferred_element_type=F32
                ).astype(BF)


def term_kernel(blocks, me_ref, idx_ref, g_ref, w_ref, ta0, ta1, ta2, ta3, tb_ref):
    my_x = me_ref[0]
    zs, xs = tb_ref.shape[:2]
    split = ta0.shape[1]
    for k, ta_ref in enumerate((ta0, ta1, ta2, ta3)):
        first = lax.rem(my_x + k, xs) * (zs // 2)
        for i in range(zs // 2):
            n = first + i
            sums = [None, None]
            for s in range(SLOTS):
                p = idx_ref[n, s]
                prod = lax.dot_general(
                    g_ref[p % blocks + (s // 2) * blocks],
                    w_ref[n, pl.ds(s * BLK, BLK), :],
                    (((1,), (1,)), ((), ())),
                    preferred_element_type=F32,
                )
                for r in range(2):
                    part = jnp.where(p // blocks == r, prod, 0.0)
                    sums[r] = part if sums[r] is None else sums[r] + part
            for r in range(2):
                ta_ref[2 * i + r] = sums[r][:split].astype(BF)
                tb_ref[2 * i + r, k] = sums[r][split:].astype(BF)


def total(parts):
    out = parts[0].astype(F32)
    for part in parts[1:]:
        out = out + part.astype(F32)
    return out


def pair_kernel(a_ref, b_ref, out_ref):
    for y in range(out_ref.shape[0]):
        out_ref[y] = total([a_ref[y], b_ref[y]]).astype(BF)


def middle_kernel(a0, a1, a2, a3, b_ref, oa_ref, ob0, ob1, ob2, ob3):
    for z in range(oa_ref.shape[0]):
        oa_ref[z] = total([a[z] for a in (a0, a1, a2, a3)]).astype(BF)
    for k, ob_ref in enumerate((ob0, ob1, ob2, ob3)):
        ob_ref[...] = total([b_ref[z, k] for z in range(b_ref.shape[0])]).astype(BF)


def last_kernel(a_ref, b0, b1, b2, b3, out_ref):
    split = a_ref.shape[1]
    out_ref[pl.ds(0, split), :] = total([a_ref[z] for z in range(a_ref.shape[0])]).astype(BF)
    out_ref[pl.ds(split, b0.shape[0]), :] = total([b[...] for b in (b0, b1, b2, b3)]).astype(BF)


def unpack_kernel(gm_ref, um_ref, b_ref, gg_ref, gu_ref):
    cols = gm_ref.shape[1]
    for t, (m_ref, o_ref) in enumerate(((gm_ref, gg_ref), (um_ref, gu_ref))):
        o_ref[...] = jnp.zeros_like(o_ref)
        first, second, count = kept(m_ref)
        for s, (p, on) in enumerate(((first, count >= 1), (second, count >= 2))):

            @pl.when(on)
            def _(p=p, s=s):
                r, c = block_of(o_ref, p, cols)
                block = b_ref[pl.ds((2 * t + s) * BLK, BLK), :].astype(F32)
                o_ref[pl.ds(r, BLK), pl.ds(c, BLK)] = block.T.astype(BF)


def shift(x, axis, k):
    size = lax.axis_size(axis)
    return lax.ppermute(x, axis, [(i, (i + k) % size) for i in range(size)])


def round_x(x):
    return [x] + [shift(x, "x", k) for k in (1, 2, 3)]


def body(tokens, gate_weight, up_weight, gate_mask, up_mask, cotangent):
    ys, cs, xs, zs = (lax.axis_size(a) for a in ("y", "c", "x", "z"))
    tok, width = cotangent.shape
    blocks = gate_mask.shape[1]
    split = ROWS_A
    left = tok - split
    shape = jax.ShapeDtypeStruct
    me = jnp.stack([lax.axis_index("x"), lax.axis_index("c")]).astype(jnp.int32)

    packed, half_a, half_b = call(
        pack_kernel,
        (shape((META + 16, BLK), BF), shape((zs, split, BLK), BF), shape((left, BLK), BF)),
        [SMEM, SMEM, VMEM, VMEM, VMEM],
    )(gate_mask, up_mask, tokens, gate_weight, up_weight)
    weights = lax.all_gather(packed, ("y", "c"), axis=0)
    x_b = jnp.stack(round_x(half_b))
    half_a = lax.all_to_all(half_a, "z", 0, 0)
    x_a = round_x(half_a)
    x_b = lax.all_to_all(jnp.broadcast_to(x_b, (zs, *x_b.shape)), "z", 0, 0)
    index = weights[:, META, :SLOTS].astype(jnp.int32)

    hidden, grads, keep, send = call(
        lambda *refs: front_kernel(blocks, *refs),
        (
            shape((tok, width), BF),
            shape((2 * blocks, tok, BLK), BF),
            shape((ys, META, BLK), BF),
            shape((ys, META, BLK), BF),
        ),
        [SMEM, SMEM] + [VMEM] * 7,
        [
            pltpu.VMEM((xs * zs, tok, BLK), BF),
            pltpu.VMEM((2 * blocks, tok, BLK), F32),
            pltpu.VMEM((2 * blocks, BLK, tok), BF),
        ],
    )(me, index, *x_a, x_b, weights, cotangent)
    other = shift(send, "c", 1)
    *t_a, t_b = call(
        lambda *refs: term_kernel(blocks, *refs),
        (shape((zs, split, BLK), BF),) * xs + (shape((zs, xs, left, BLK), BF),),
        [SMEM, SMEM, VMEM, VMEM],
    )(me, index, grads, weights)
    t_a = [t_a[0]] + [shift(t_a[k], "x", k) for k in range(1, xs)]
    wgrads = call(pair_kernel, shape((ys, META, BLK), BF), [VMEM] * 2)(keep, other)
    wgrads = lax.psum_scatter(wgrads, "y", scatter_dimension=0)
    t_b = lax.all_to_all(t_b, "z", 0, 0)
    t_a, *t_b = call(
        middle_kernel,
        (shape((zs, split, BLK), BF),) + (shape((left, BLK), BF),) * xs,
        [VMEM] * 5,
    )(*t_a, t_b)
    t_b = [t_b[0]] + [shift(t_b[k], "x", k) for k in range(1, xs)]
    t_a = lax.all_to_all(t_a, "z", 0, 0)
    grad_tokens = call(last_kernel, shape(tokens.shape, BF), [VMEM] * 5)(t_a, *t_b)
    grad_gate, grad_up = call(
        unpack_kernel,
        (shape(gate_weight.shape, BF), shape(up_weight.shape, BF)),
        [SMEM, SMEM, VMEM],
    )(gate_mask, up_mask, wgrads)
    return hidden, grad_tokens, grad_gate, grad_up


def solution(mesh):
    rows, cols = mesh.devices.shape
    cut = Mesh(mesh.devices.reshape(rows // 2, 2, 4, cols // 4), ("y", "c", "x", "z"))
    spec = P(("y", "c"), ("x", "z"))
    return jax.shard_map(
        body, mesh=cut, in_specs=(spec,) * 6, out_specs=(spec,) * 4, check_vma=False
    )
```

time: 158 us -> 147 us (0.930)
  the two profiles are of different devices: /device:TPU:25 before, /device:TPU:31 now
where the time goes in v2:
time: 147 us; the launch traced here: 146 us
  starting transfers between devices  63.9 us (43%)
  waiting for transfers between devices  44.5 us (30%)
  between operations  14.2 us (10%)
  Pallas kernels  13 us (9%)
  local copies, waits for them, and re-layouts  9.07 us (6%)
    ppermute x13, starting transfers between devices, shift(): return lax.ppermute(x, axis, [(i, (i + k) % size) for i in range(size)])  34.8 us
    ppermute x13, waiting for transfers between devices, shift(): return lax.ppermute(x, axis, [(i, (i + k) % size) for i in range(size)])  29.1 us
    all_to_all x1, starting transfers between devices, body(): half_a = lax.all_to_all(half_a, 'z', 0, 0)  10 us
    all_gather x1, waiting for transfers between devices, body(): weights = lax.all_gather(packed, ('y', 'c'), axis=0)  9.72 us
    unnamed x26, local copies, waits for them, and re-layouts  8.14 us
    all_to_all x1, starting transfers between devices, body(): t_b = lax.all_to_all(t_b, 'z', 0, 0)  6.72 us
    all_to_all x1, starting transfers between devices, body(): t_a = lax.all_to_all(t_a, 'z', 0, 0)  6.65 us
    all_to_all x1, starting transfers between devices, body(): x_b = lax.all_to_all(jnp.broadcast_to(x_b, (zs, *x_b.shape)), 'z', 0, 0)  5.65 us
  transfers between devices with their start and end apart: 19, of which 11 were waited for; matrix products, arithmetic and copies ran while one was open for 1% of the time, Pallas kernels for 3%

profile of v2, /device:TPU:31, one launch (start us, length us, event | category | flops | bytes accessed | tf_op | source)
XLA Modules:
  0.0 145.6 jit_solution(10470959822036044439)
XLA Ops:
  7.2 0.0 copy-start.2
  7.2 0.0 all-gather.3.cloned.1.call-start
  7.2 0.0 copy-start.3
  7.2 1.0 copy-done.3
  8.2 0.9 copy-done.4
  9.2 0.8 copy-done.6
  10.0 0.7 copy-done.7
  10.7 0.7 copy-done.9
  11.4 1.4 shard_map.93
  12.8 0.0 all-gather.3.cloned.1.call-update
  12.8 10.0 %all-to-all-start = ((bf16[8,176,128]{2,1,0:T(8,128)(2,1)}), bf16[8,176,128]{2,1,0:T(8,128)(2,1)S(1)}, u32[]{:S(2)}, u32[]{:S(2)}) async-start(bf16[8,176,128]{2,1,0:T(8,128)(2,1)} %get-tuple-element.24), calls=%async_computation | async-start | bytes 720896 | tf_op jit(solution)/shard_map/all_to_all | solution.py:205
  22.8 2.1 %collective-permute-start.3 = (bf16[80,128]{1,0:T(8,128)(2,1)S(1)}, bf16[80,128]{1,0:T(8,128)(2,1)S(1)}, u32[]{:S(2)}, u32[]{:S(2)}) collective-permute-start(bf16[80,128]{1,0:T(8,128)(2,1)S(1)} %get-tuple-element.25), channel_id=1, source_target_pairs={{0,8},{8,16},{16,24},{24,0},{1,9},{9,17},{17,25},{25,1},{2,10},{10... | collective-permute-start | bytes 61448 | tf_op jit(solution)/shard_map/ppermute | solution.py:182
  24.9 4.0 %collective-permute-start.4 = (bf16[80,128]{1,0:T(8,128)(2,1)S(1)}, bf16[80,128]{1,0:T(8,128)(2,1)S(1)}, u32[]{:S(2)}, u32[]{:S(2)}) collective-permute-start(bf16[80,128]{1,0:T(8,128)(2,1)S(1)} %get-tuple-element.25), channel_id=1, source_target_pairs={{0,16},{8,24},{16,0},{24,8},{1,17},{9,25},{17,1},{25,9},{2,18},{10... | collective-permute-start | bytes 61448 | tf_op jit(solution)/shard_map/ppermute | solution.py:182
  29.0 1.9 %collective-permute-start.5 = (bf16[80,128]{1,0:T(8,128)(2,1)S(1)}, bf16[80,128]{1,0:T(8,128)(2,1)S(1)}, u32[]{:S(2)}, u32[]{:S(2)}) collective-permute-start(bf16[80,128]{1,0:T(8,128)(2,1)S(1)} %get-tuple-element.25), channel_id=1, source_target_pairs={{0,24},{8,0},{16,8},{24,16},{1,25},{9,1},{17,9},{25,17},{2,26},{10... | collective-permute-start | bytes 61448 | tf_op jit(solution)/shard_map/ppermute | solution.py:182
  30.9 0.0 collective-permute-done.3
  30.9 0.3 collective-permute-done.4
  31.3 3.5 %collective-permute-done.5 = bf16[80,128]{1,0:T(8,128)(2,1)S(1)} collective-permute-done((bf16[80,128]{1,0:T(8,128)(2,1)S(1)}, bf16[80,128]{1,0:T(8,128)(2,1)S(1)}, u32[]{:S(2)}, u32[]{:S(2)}) %collective-permute-start.5) | collective-permute-done | bytes 20512 | tf_op jit(solution)/shard_map/ppermute | solution.py:182
  34.8 1.0 all-to-all-done.refs_2_
  35.8 0.9 broadcast_in_dim.3
  36.7 5.7 %all-to-all-start.1 = ((bf16[8,4,80,128]{3,2,1,0:T(8,128)(2,1)}), bf16[8,4,80,128]{3,2,1,0:T(8,128)(2,1)S(1)}, u32[]{:S(2)}, u32[]{:S(2)}) async-start(bf16[8,4,80,128]{3,2,1,0:T(8,128)(2,1)} %broadcast_in_dim.3), calls=%async_computation.1 | async-start | bytes 1310720 | tf_op jit(solution)/shard_map/all_to_all | solution.py:207
  42.3 0.0 reduce-scatter.2.cloned.1.call-start
  42.4 2.6 %collective-permute-start = (bf16[8,176,128]{2,1,0:T(8,128)(2,1)S(1)}, bf16[8,176,128]{2,1,0:T(8,128)(2,1)S(1)}, u32[]{:S(2)}, u32[]{:S(2)}) collective-permute-start(bf16[8,176,128]{2,1,0:T(8,128)(2,1)S(1)} %all-to-all-done.refs_2_), channel_id=1, source_target_pairs={{0,8},{8,16},{16,24},{24,0},{1,9},{9,17},{17,25},{25,1},{2,10},{10... | collective-permute-start | bytes 1081352 | tf_op jit(solution)/shard_map/ppermute | solution.py:182
  45.0 2.4 %collective-permute-start.1 = (bf16[8,176,128]{2,1,0:T(8,128)(2,1)S(1)}, bf16[8,176,128]{2,1,0:T(8,128)(2,1)S(1)}, u32[]{:S(2)}, u32[]{:S(2)}) collective-permute-start(bf16[8,176,128]{2,1,0:T(8,128)(2,1)S(1)} %all-to-all-done.refs_2_), channel_id=1, source_target_pairs={{0,16},{8,24},{16,0},{24,8},{1,17},{9,25},{17,1},{25,9},{2,18},{10... | collective-permute-start | bytes 1081352 | tf_op jit(solution)/shard_map/ppermute | solution.py:182
  47.4 2.2 %collective-permute-start.2 = (bf16[8,176,128]{2,1,0:T(8,128)(2,1)S(1)}, bf16[8,176,128]{2,1,0:T(8,128)(2,1)S(1)}, u32[]{:S(2)}, u32[]{:S(2)}) collective-permute-start(bf16[8,176,128]{2,1,0:T(8,128)(2,1)S(1)} %all-to-all-done.refs_2_), channel_id=1, source_target_pairs={{0,24},{8,0},{16,8},{24,16},{1,25},{9,1},{17,9},{25,17},{2,26},{10... | collective-permute-start | bytes 1081352 | tf_op jit(solution)/shard_map/ppermute | solution.py:182
  49.6 0.1 pad_add_fusion.refs_0_
  49.7 9.7 %all-gather.3.cloned.1.call-done = bf16[8448,128]{1,0:T(8,128)(2,1)} async-done(((bf16[528,128]{1,0:T(8,128)(2,1)}), bf16[8448,128]{1,0:T(8,128)(2,1)}) %all-gather.3.cloned.1.call-update) | async-done | bytes 2162704 | tf_op jit(solution)/shard_map/all_gather | solution.py:203
  59.4 0.8 slice_convert_fusion
  60.2 0.0 collective-permute-done.refs_3_
  60.2 0.0 collective-permute-done.1.refs_4_
  60.2 5.3 %collective-permute-done.2.refs_5_ = bf16[8,176,128]{2,1,0:T(8,128)(2,1)S(1)} collective-permute-done((bf16[8,176,128]{2,1,0:T(8,128)(2,1)S(1)}, bf16[8,176,128]{2,1,0:T(8,128)(2,1)S(1)}, u32[]{:S(2)}, u32[]{:S(2)}) %collective-permute-start.2) | collective-permute-done | bytes 360480 | tf_op jit(solution)/shard_map/ppermute | solution.py:182
  65.5 0.0 all-to-all-done.1.refs_6_
  65.5 0.0 copy-done.2
  65.5 1.6 %copy-done = bf16[8448,128]{1,0:T(8,128)(2,1)S(1)} copy-done((bf16[8448,128]{1,0:T(8,128)(2,1)S(1)}, bf16[8448,128]{1,0:T(8,128)(2,1)}, u32[]{:S(2)}) %copy-start) | copy-done | bytes 2162712
  67.1 4.3 %shard_map.94 = (bf16[256,512]{1,0:T(8,128)(2,1)}, bf16[8,256,128]{2,1,0:T(8,128)(2,1)S(1)}, bf16[8,512,128]{2,1,0:T(8,128)(2,1)S(1)}, bf16[8,512,128]{2,1,0:T(8,128)(2,1)S(1)}) custom-call(s32[2]{0:T(128)S(1)} %pad_add_fusion.refs_0_, s32[16,4]{1,0:T(8,128)S(1)} %bitcast.13, bf16[8,176,128]{2,1,0:T(8,128)(2,1)S(1)} %all-to-all-done.refs_2_, ...), custom_call_target="tpu_custom_call" | custom-call | tf_op jit(solution)/shard_map/pallas_call | solution.py:210
  71.4 3.5 %collective-permute-start.12 = (bf16[8,512,128]{2,1,0:T(8,128)(2,1)S(1)}, bf16[8,512,128]{2,1,0:T(8,128)(2,1)S(1)}, u32[]{:S(2)}, u32[]{:S(2)}) collective-permute-start(bf16[8,512,128]{2,1,0:T(8,128)(2,1)S(1)} %get-tuple-element.39), channel_id=1, source_target_pairs={{0,32},{32,0},{1,33},{33,1},{2,34},{34,2},{3,35},{35,3},{4,36},{36... | collective-permute-start | bytes 3145736 | tf_op jit(solution)/shard_map/ppermute | solution.py:182
  74.9 2.3 %collective-permute-done.12.b_ref = bf16[8,512,128]{2,1,0:T(8,128)(2,1)S(1)} collective-permute-done((bf16[8,512,128]{2,1,0:T(8,128)(2,1)S(1)}, bf16[8,512,128]{2,1,0:T(8,128)(2,1)S(1)}, u32[]{:S(2)}, u32[]{:S(2)}) %collective-permute-start.12) | collective-permute-done | bytes 1048608 | tf_op jit(solution)/shard_map/ppermute | solution.py:182
  77.2 1.2 shard_map.98
  78.4 0.0 reduce-scatter.2.cloned.1.call-update
  78.4 0.0 copy-done.1
  78.4 2.9 %shard_map.95 = (bf16[8,176,128]{2,1,0:T(8,128)(2,1)S(1)}, bf16[8,176,128]{2,1,0:T(8,128)(2,1)S(1)}, bf16[8,176,128]{2,1,0:T(8,128)(2,1)S(1)}, bf16[8,176,128]{2,1,0:T(8,128)(2,1)S(1)}, bf16[8,4,80,128]{3,2,1,0:T(8,128)(2,1)}) custom-call(s32[2]{0:T(128)S(1)} %pad_add_fusion.refs_0_, s32[16,4]{1,0:T(8,128)S(1)} %bitcast.14, ...), custom_call_target="tpu_custom_call" | custom-call | tf_op jit(solution)/shard_map/pallas_call | solution.py:226
  81.4 0.7 copy-done.11
  82.1 0.7 copy-done.12
  82.8 6.7 %all-to-all-start.2 = ((bf16[8,4,80,128]{3,2,1,0:T(8,128)(2,1)}), bf16[8,4,80,128]{3,2,1,0:T(8,128)(2,1)S(1)}, u32[]{:S(2)}, u32[]{:S(2)}) async-start(bf16[8,4,80,128]{3,2,1,0:T(8,128)(2,1)} %get-tuple-element.32), calls=%async_computation.2 | async-start | bytes 1310720 | tf_op jit(solution)/shard_map/all_to_all | solution.py:234
  89.6 2.2 %collective-permute-start.6 = (bf16[8,176,128]{2,1,0:T(8,128)(2,1)}, bf16[8,176,128]{2,1,0:T(8,128)(2,1)S(1)}, u32[]{:S(2)}, u32[]{:S(2)}) collective-permute-start(bf16[8,176,128]{2,1,0:T(8,128)(2,1)} %copy-done.12), channel_id=1, source_target_pairs={{0,8},{8,16},{16,24},{24,0},{1,9},{9,17},{17,25},{25,1},{2,10},{10... | collective-permute-start | bytes 1081352 | tf_op jit(solution)/shard_map/ppermute | solution.py:182
  91.8 2.3 %collective-permute-start.7 = (bf16[8,176,128]{2,1,0:T(8,128)(2,1)}, bf16[8,176,128]{2,1,0:T(8,128)(2,1)S(1)}, u32[]{:S(2)}, u32[]{:S(2)}) collective-permute-start(bf16[8,176,128]{2,1,0:T(8,128)(2,1)} %copy-done.11), channel_id=1, source_target_pairs={{0,16},{8,24},{16,0},{24,8},{1,17},{9,25},{17,1},{25,9},{2,18},{10... | collective-permute-start | bytes 1081352 | tf_op jit(solution)/shard_map/ppermute | solution.py:182
  94.1 2.7 %collective-permute-start.8 = (bf16[8,176,128]{2,1,0:T(8,128)(2,1)S(1)}, bf16[8,176,128]{2,1,0:T(8,128)(2,1)S(1)}, u32[]{:S(2)}, u32[]{:S(2)}) collective-permute-start(bf16[8,176,128]{2,1,0:T(8,128)(2,1)S(1)} %get-tuple-element.31), channel_id=1, source_target_pairs={{0,24},{8,0},{16,8},{24,16},{1,25},{9,1},{17,9},{25,17},{2,26},{10... | collective-permute-start | bytes 1081352 | tf_op jit(solution)/shard_map/ppermute | solution.py:182
  96.8 4.2 %collective-permute-done.6.a1 = bf16[8,176,128]{2,1,0:T(8,128)(2,1)S(1)} collective-permute-done((bf16[8,176,128]{2,1,0:T(8,128)(2,1)}, bf16[8,176,128]{2,1,0:T(8,128)(2,1)S(1)}, u32[]{:S(2)}, u32[]{:S(2)}) %collective-permute-start.6) | collective-permute-done | bytes 360480 | tf_op jit(solution)/shard_map/ppermute | solution.py:182
  101.0 3.5 %collective-permute-done.7.a2 = bf16[8,176,128]{2,1,0:T(8,128)(2,1)S(1)} collective-permute-done((bf16[8,176,128]{2,1,0:T(8,128)(2,1)}, bf16[8,176,128]{2,1,0:T(8,128)(2,1)S(1)}, u32[]{:S(2)}, u32[]{:S(2)}) %collective-permute-start.7) | collective-permute-done | bytes 360480 | tf_op jit(solution)/shard_map/ppermute | solution.py:182
  104.4 9.1 %collective-permute-done.8.a3 = bf16[8,176,128]{2,1,0:T(8,128)(2,1)S(1)} collective-permute-done((bf16[8,176,128]{2,1,0:T(8,128)(2,1)S(1)}, bf16[8,176,128]{2,1,0:T(8,128)(2,1)S(1)}, u32[]{:S(2)}, u32[]{:S(2)}) %collective-permute-start.8) | collective-permute-done | bytes 360480 | tf_op jit(solution)/shard_map/ppermute | solution.py:182
  113.6 0.0 all-to-all-done.2.b_ref
  113.6 0.9 shard_map.96
  114.5 6.6 %all-to-all-start.3 = ((bf16[8,176,128]{2,1,0:T(8,128)(2,1)}), bf16[8,176,128]{2,1,0:T(8,128)(2,1)S(1)}, u32[]{:S(2)}, u32[]{:S(2)}) async-start(bf16[8,176,128]{2,1,0:T(8,128)(2,1)} %get-tuple-element.33), calls=%async_computation.3 | async-start | bytes 720896 | tf_op jit(solution)/shard_map/all_to_all | solution.py:241
  121.1 2.3 %collective-permute-start.10 = (bf16[80,128]{1,0:T(8,128)(2,1)S(1)}, bf16[80,128]{1,0:T(8,128)(2,1)S(1)}, u32[]{:S(2)}, u32[]{:S(2)}) collective-permute-start(bf16[80,128]{1,0:T(8,128)(2,1)S(1)} %get-tuple-element.36), channel_id=1, source_target_pairs={{0,16},{8,24},{16,0},{24,8},{1,17},{9,25},{17,1},{25,9},{2,18},{10... | collective-permute-start | bytes 61448 | tf_op jit(solution)/shard_map/ppermute | solution.py:182
  123.5 1.9 %collective-permute-start.11 = (bf16[80,128]{1,0:T(8,128)(2,1)S(1)}, bf16[80,128]{1,0:T(8,128)(2,1)S(1)}, u32[]{:S(2)}, u32[]{:S(2)}) collective-permute-start(bf16[80,128]{1,0:T(8,128)(2,1)S(1)} %get-tuple-element.37), channel_id=1, source_target_pairs={{0,24},{8,0},{16,8},{24,16},{1,25},{9,1},{17,9},{25,17},{2,26},{10... | collective-permute-start | bytes 61448 | tf_op jit(solution)/shard_map/ppermute | solution.py:182
  125.4 4.6 %collective-permute-start.9 = (bf16[80,128]{1,0:T(8,128)(2,1)S(1)}, bf16[80,128]{1,0:T(8,128)(2,1)S(1)}, u32[]{:S(2)}, u32[]{:S(2)}) collective-permute-start(bf16[80,128]{1,0:T(8,128)(2,1)S(1)} %get-tuple-element.35), channel_id=1, source_target_pairs={{0,8},{8,16},{16,24},{24,0},{1,9},{9,17},{17,25},{25,1},{2,10},{10... | collective-permute-start | bytes 61448 | tf_op jit(solution)/shard_map/ppermute | solution.py:182
  130.0 0.0 collective-permute-done.10.b2
  130.0 0.0 collective-permute-done.11.b3
  130.0 1.0 collective-permute-done.9.b1
  131.0 4.6 %all-to-all-done.3.a_ref = bf16[8,176,128]{2,1,0:T(8,128)(2,1)S(1)} async-done(((bf16[8,176,128]{2,1,0:T(8,128)(2,1)}), bf16[8,176,128]{2,1,0:T(8,128)(2,1)S(1)}, u32[]{:S(2)}, u32[]{:S(2)}) %all-to-all-start.3) | async-done | bytes 360480 | tf_op jit(solution)/shard_map/all_to_all | solution.py:241
  135.5 0.7 shard_map.97
  136.2 0.0 copy-done.8
  136.2 0.0 copy-done.10
  136.2 0.9 copy-done.5
  137.1 1.6 %shard_map.99 = (bf16[256,512]{1,0:T(8,128)(2,1)}, bf16[256,512]{1,0:T(8,128)(2,1)}) custom-call(s32[2,4]{1,0:T(2,128)S(1)} %copy-done.8, s32[2,4]{1,0:T(2,128)S(1)} %copy-done.10, bf16[512,128]{1,0:T(8,128)(2,1)S(1)} %bitcast.12), custom_call_target="tpu_custom_call" | custom-call | tf_op jit(solution)/shard_map/pallas_call | solution.py:243
  (13 shorter events, 0.0 us)
Async XLA Ops:
  7.2 58.3 %copy-start.2 = (bf16[256,512]{1,0:T(8,128)(2,1)S(1)}, bf16[256,512]{1,0:T(8,128)(2,1)}, u32[]{:S(2)}) copy-start(bf16[256,512]{1,0:T(8,128)(2,1)} %refs_8_.1) | copy-start | bytes 786436
  7.2 52.2 %all-gather.3.cloned.1.call-start = ((), (), s32[]{:S(2)}) async-start(), calls=%async_computation.6 | async-start | bytes 2297856 | tf_op jit(solution)/shard_map/all_gather | solution.py:203
  7.2 1.0 copy-start.3
  8.2 0.9 copy-start.4
  9.2 0.8 copy-start.6
  10.0 0.7 copy-start.7
  10.7 0.7 copy-start.9
  12.8 23.0 %all-to-all-start = ((bf16[8,176,128]{2,1,0:T(8,128)(2,1)}), bf16[8,176,128]{2,1,0:T(8,128)(2,1)S(1)}, u32[]{:S(2)}, u32[]{:S(2)}) async-start(bf16[8,176,128]{2,1,0:T(8,128)(2,1)} %get-tuple-element.24), calls=%async_computation | async-start | bytes 720896 | tf_op jit(solution)/shard_map/all_to_all | solution.py:205
  22.8 8.1 %collective-permute-start.3 = (bf16[80,128]{1,0:T(8,128)(2,1)S(1)}, bf16[80,128]{1,0:T(8,128)(2,1)S(1)}, u32[]{:S(2)}, u32[]{:S(2)}) collective-permute-start(bf16[80,128]{1,0:T(8,128)(2,1)S(1)} %get-tuple-element.25), channel_id=1, source_target_pairs={{0,8},{8,16},{16,24},{24,0},{1,9},{9,17},{17,25},{25,1},{2,10},{10... | collective-permute-start | bytes 61448 | tf_op jit(solution)/shard_map/ppermute | solution.py:182
  24.9 6.3 %collective-permute-start.4 = (bf16[80,128]{1,0:T(8,128)(2,1)S(1)}, bf16[80,128]{1,0:T(8,128)(2,1)S(1)}, u32[]{:S(2)}, u32[]{:S(2)}) collective-permute-start(bf16[80,128]{1,0:T(8,128)(2,1)S(1)} %get-tuple-element.25), channel_id=1, source_target_pairs={{0,16},{8,24},{16,0},{24,8},{1,17},{9,25},{17,1},{25,9},{2,18},{10... | collective-permute-start | bytes 61448 | tf_op jit(solution)/shard_map/ppermute | solution.py:182
  29.0 5.7 %collective-permute-start.5 = (bf16[80,128]{1,0:T(8,128)(2,1)S(1)}, bf16[80,128]{1,0:T(8,128)(2,1)S(1)}, u32[]{:S(2)}, u32[]{:S(2)}) collective-permute-start(bf16[80,128]{1,0:T(8,128)(2,1)S(1)} %get-tuple-element.25), channel_id=1, source_target_pairs={{0,24},{8,0},{16,8},{24,16},{1,25},{9,1},{17,9},{25,17},{2,26},{10... | collective-permute-start | bytes 61448 | tf_op jit(solution)/shard_map/ppermute | solution.py:182
  36.7 28.8 %all-to-all-start.1 = ((bf16[8,4,80,128]{3,2,1,0:T(8,128)(2,1)}), bf16[8,4,80,128]{3,2,1,0:T(8,128)(2,1)S(1)}, u32[]{:S(2)}, u32[]{:S(2)}) async-start(bf16[8,4,80,128]{3,2,1,0:T(8,128)(2,1)} %broadcast_in_dim.3), calls=%async_computation.1 | async-start | bytes 1310720 | tf_op jit(solution)/shard_map/all_to_all | solution.py:207
  42.3 93.9 %reduce-scatter.2.cloned.1.call-start = ((), (), s32[]{:S(2)}) async-start(), calls=%async_computation.5 | async-start | bytes 1179648 | tf_op jit(solution)/shard_map/reduce_scatter | solution.py:233
  42.4 17.8 %collective-permute-start = (bf16[8,176,128]{2,1,0:T(8,128)(2,1)S(1)}, bf16[8,176,128]{2,1,0:T(8,128)(2,1)S(1)}, u32[]{:S(2)}, u32[]{:S(2)}) collective-permute-start(bf16[8,176,128]{2,1,0:T(8,128)(2,1)S(1)} %all-to-all-done.refs_2_), channel_id=1, source_target_pairs={{0,8},{8,16},{16,24},{24,0},{1,9},{9,17},{17,25},{25,1},{2,10},{10... | collective-permute-start | bytes 1081352 | tf_op jit(solution)/shard_map/ppermute | solution.py:182
  45.0 15.2 %collective-permute-start.1 = (bf16[8,176,128]{2,1,0:T(8,128)(2,1)S(1)}, bf16[8,176,128]{2,1,0:T(8,128)(2,1)S(1)}, u32[]{:S(2)}, u32[]{:S(2)}) collective-permute-start(bf16[8,176,128]{2,1,0:T(8,128)(2,1)S(1)} %all-to-all-done.refs_2_), channel_id=1, source_target_pairs={{0,16},{8,24},{16,0},{24,8},{1,17},{9,25},{17,1},{25,9},{2,18},{10... | collective-permute-start | bytes 1081352 | tf_op jit(solution)/shard_map/ppermute | solution.py:182
  47.4 18.1 %collective-permute-start.2 = (bf16[8,176,128]{2,1,0:T(8,128)(2,1)S(1)}, bf16[8,176,128]{2,1,0:T(8,128)(2,1)S(1)}, u32[]{:S(2)}, u32[]{:S(2)}) collective-permute-start(bf16[8,176,128]{2,1,0:T(8,128)(2,1)S(1)} %all-to-all-done.refs_2_), channel_id=1, source_target_pairs={{0,24},{8,0},{16,8},{24,16},{1,25},{9,1},{17,9},{25,17},{2,26},{10... | collective-permute-start | bytes 1081352 | tf_op jit(solution)/shard_map/ppermute | solution.py:182
  65.5 1.6 %copy-start = (bf16[8448,128]{1,0:T(8,128)(2,1)S(1)}, bf16[8448,128]{1,0:T(8,128)(2,1)}, u32[]{:S(2)}) copy-start(bf16[8448,128]{1,0:T(8,128)(2,1)} %all-gather.3.cloned.1.call-done) | copy-start | bytes 6488068
  71.4 7.0 %copy-start.1 = (bf16[8448,128]{1,0:T(8,128)(2,1)S(1)}, bf16[8448,128]{1,0:T(8,128)(2,1)}, u32[]{:S(2)}) copy-start(bf16[8448,128]{1,0:T(8,128)(2,1)} %all-gather.3.cloned.1.call-done) | copy-start | bytes 6488068
  71.4 5.8 %collective-permute-start.12 = (bf16[8,512,128]{2,1,0:T(8,128)(2,1)S(1)}, bf16[8,512,128]{2,1,0:T(8,128)(2,1)S(1)}, u32[]{:S(2)}, u32[]{:S(2)}) collective-permute-start(bf16[8,512,128]{2,1,0:T(8,128)(2,1)S(1)} %get-tuple-element.39), channel_id=1, source_target_pairs={{0,32},{32,0},{1,33},{33,1},{2,34},{34,2},{3,35},{35,3},{4,36},{36... | collective-permute-start | bytes 3145736 | tf_op jit(solution)/shard_map/ppermute | solution.py:182
  81.3 0.7 copy-start.11
  82.1 0.8 copy-start.12
  82.8 53.4 %copy-start.8 = (s32[2,4]{1,0:T(2,128)S(1)}, s32[2,4]{1,0:T(2,128)}, u32[]{:S(2)}) copy-start(s32[2,4]{1,0:T(2,128)} %gm_ref.3) | copy-start | bytes 100
  82.8 53.4 %copy-start.10 = (s32[2,4]{1,0:T(2,128)S(1)}, s32[2,4]{1,0:T(2,128)}, u32[]{:S(2)}) copy-start(s32[2,4]{1,0:T(2,128)} %um_ref.3) | copy-start | bytes 100
  82.8 30.7 %all-to-all-start.2 = ((bf16[8,4,80,128]{3,2,1,0:T(8,128)(2,1)}), bf16[8,4,80,128]{3,2,1,0:T(8,128)(2,1)S(1)}, u32[]{:S(2)}, u32[]{:S(2)}) async-start(bf16[8,4,80,128]{3,2,1,0:T(8,128)(2,1)} %get-tuple-element.32), calls=%async_computation.2 | async-start | bytes 1310720 | tf_op jit(solution)/shard_map/all_to_all | solution.py:234
  89.6 11.4 %collective-permute-start.6 = (bf16[8,176,128]{2,1,0:T(8,128)(2,1)}, bf16[8,176,128]{2,1,0:T(8,128)(2,1)S(1)}, u32[]{:S(2)}, u32[]{:S(2)}) collective-permute-start(bf16[8,176,128]{2,1,0:T(8,128)(2,1)} %copy-done.12), channel_id=1, source_target_pairs={{0,8},{8,16},{16,24},{24,0},{1,9},{9,17},{17,25},{25,1},{2,10},{10... | collective-permute-start | bytes 1081352 | tf_op jit(solution)/shard_map/ppermute | solution.py:182
  91.8 12.6 %collective-permute-start.7 = (bf16[8,176,128]{2,1,0:T(8,128)(2,1)}, bf16[8,176,128]{2,1,0:T(8,128)(2,1)S(1)}, u32[]{:S(2)}, u32[]{:S(2)}) collective-permute-start(bf16[8,176,128]{2,1,0:T(8,128)(2,1)} %copy-done.11), channel_id=1, source_target_pairs={{0,16},{8,24},{16,0},{24,8},{1,17},{9,25},{17,1},{25,9},{2,18},{10... | collective-permute-start | bytes 1081352 | tf_op jit(solution)/shard_map/ppermute | solution.py:182
  94.1 19.4 %collective-permute-start.8 = (bf16[8,176,128]{2,1,0:T(8,128)(2,1)S(1)}, bf16[8,176,128]{2,1,0:T(8,128)(2,1)S(1)}, u32[]{:S(2)}, u32[]{:S(2)}) collective-permute-start(bf16[8,176,128]{2,1,0:T(8,128)(2,1)S(1)} %get-tuple-element.31), channel_id=1, source_target_pairs={{0,24},{8,0},{16,8},{24,16},{1,25},{9,1},{17,9},{25,17},{2,26},{10... | collective-permute-start | bytes 1081352 | tf_op jit(solution)/shard_map/ppermute | solution.py:182
  114.5 21.0 %all-to-all-start.3 = ((bf16[8,176,128]{2,1,0:T(8,128)(2,1)}), bf16[8,176,128]{2,1,0:T(8,128)(2,1)S(1)}, u32[]{:S(2)}, u32[]{:S(2)}) async-start(bf16[8,176,128]{2,1,0:T(8,128)(2,1)} %get-tuple-element.33), calls=%async_computation.3 | async-start | bytes 720896 | tf_op jit(solution)/shard_map/all_to_all | solution.py:241
  121.1 8.8 %collective-permute-start.10 = (bf16[80,128]{1,0:T(8,128)(2,1)S(1)}, bf16[80,128]{1,0:T(8,128)(2,1)S(1)}, u32[]{:S(2)}, u32[]{:S(2)}) collective-permute-start(bf16[80,128]{1,0:T(8,128)(2,1)S(1)} %get-tuple-element.36), channel_id=1, source_target_pairs={{0,16},{8,24},{16,0},{24,8},{1,17},{9,25},{17,1},{25,9},{2,18},{10... | collective-permute-start | bytes 61448 | tf_op jit(solution)/shard_map/ppermute | solution.py:182
  123.5 6.5 %collective-permute-start.11 = (bf16[80,128]{1,0:T(8,128)(2,1)S(1)}, bf16[80,128]{1,0:T(8,128)(2,1)S(1)}, u32[]{:S(2)}, u32[]{:S(2)}) collective-permute-start(bf16[80,128]{1,0:T(8,128)(2,1)S(1)} %get-tuple-element.37), channel_id=1, source_target_pairs={{0,24},{8,0},{16,8},{24,16},{1,25},{9,1},{17,9},{25,17},{2,26},{10... | collective-permute-start | bytes 61448 | tf_op jit(solution)/shard_map/ppermute | solution.py:182
  125.4 5.6 %collective-permute-start.9 = (bf16[80,128]{1,0:T(8,128)(2,1)S(1)}, bf16[80,128]{1,0:T(8,128)(2,1)S(1)}, u32[]{:S(2)}, u32[]{:S(2)}) collective-permute-start(bf16[80,128]{1,0:T(8,128)(2,1)S(1)} %get-tuple-element.35), channel_id=1, source_target_pairs={{0,8},{8,16},{16,24},{24,0},{1,9},{9,17},{17,25},{25,1},{2,10},{10... | collective-permute-start | bytes 61448 | tf_op jit(solution)/shard_map/ppermute | solution.py:182
  136.2 0.9 copy-start.5
Sparse Core Ops, SparseCore 0:
  12.9 46.4 all-gather.2
  78.6 36.4 reduce-scatter.1

commit v3 on v2

v3 whole, which is shorter than its diff:
```python
import jax
import jax.numpy as jnp
from jax import lax
from jax.experimental import pallas as pl
from jax.experimental.pallas import tpu as pltpu
from jax.sharding import Mesh
from jax.sharding import PartitionSpec as P

BLK = 128
SLOTS = 4
META = SLOTS * BLK
BF = jnp.bfloat16
F32 = jnp.float32
VMEM = pl.BlockSpec(memory_space=pltpu.VMEM)
SMEM = pl.BlockSpec(memory_space=pltpu.SMEM)
HBM = pl.BlockSpec(memory_space=pltpu.HBM)


def call(kernel, outs, in_specs, scratch=(), out_spec=VMEM, limit=40):
    return pl.pallas_call(
        kernel,
        out_shape=outs,
        in_specs=in_specs,
        out_specs=jax.tree.map(lambda _: out_spec, outs),
        scratch_shapes=list(scratch),
        compiler_params=pltpu.CompilerParams(vmem_limit_bytes=limit * 1024 * 1024),
    )


def kept(mask_ref):
    cols = mask_ref.shape[1]
    first, second, count = jnp.int32(0), jnp.int32(0), jnp.int32(0)
    for p in range(mask_ref.shape[0] * cols):
        m = mask_ref[p // cols, p % cols]
        on = m == 1
        first = jnp.where(on & (count == 0), p, first)
        second = jnp.where(on & (count == 1), p, second)
        count = count + m
    return first, second, count


def block_of(ref, p, cols):
    r = pl.multiple_of((p // cols) * BLK, BLK)
    c = pl.multiple_of((p % cols) * BLK, BLK)
    return r, c


def pack_kernel(gm_ref, um_ref, tok_ref, gw_ref, uw_ref, out_ref, all_ref, gm, um, tail, zero, sems):
    cols = gm.shape[1]
    copies = [
        pltpu.make_async_copy(tok_ref, all_ref.at[z], sems.at[z]) for z in range(all_ref.shape[0])
    ]
    masks = [
        pltpu.make_async_copy(a, b, sems.at[len(copies) + t])
        for t, (a, b) in enumerate(((gm_ref, gm), (um_ref, um)))
    ]
    for copy in masks + copies:
        copy.start()
    zero[...] = jnp.zeros_like(zero)
    for copy in masks:
        copy.wait()
    sem = len(copies) + len(masks)
    positions = []
    for t, (m_ref, w_ref) in enumerate(((gm, gw_ref), (um, uw_ref))):
        first, second, count = kept(m_ref)
        for s, (p, on) in enumerate(((first, count >= 1), (second, count >= 2))):
            r, c = block_of(w_ref, p, cols)
            place = out_ref.at[pl.ds((2 * t + s) * BLK, BLK)]
            block = w_ref.at[pl.ds(r, BLK), pl.ds(c, BLK)]
            copy = pltpu.make_async_copy(block, place, sems.at[sem])
            empty = pltpu.make_async_copy(zero, place, sems.at[sem])
            pl.when(on)(copy.start)
            pl.when(jnp.logical_not(on))(empty.start)
            copies.append(copy)
            positions.append(p)
            sem += 1
    lane = lax.broadcasted_iota(jnp.int32, tail.shape, 1)
    meta = jnp.zeros(lane.shape, jnp.int32)
    for s, p in enumerate(positions):
        meta = jnp.where(lane == s, p, meta)
    tail[...] = meta.astype(F32).astype(BF)
    copy = pltpu.make_async_copy(tail, out_ref.at[pl.ds(META, tail.shape[0])], sems.at[sem])
    copy.start()
    for copy in copies + [copy]:
        copy.wait()


def front_kernel(blocks, me_ref, idx_ref, own, la, lb, ra, rb, oa, ob, w_hbm, cot_ref, *rest):
    hid_ref, g_ref, keep_ref, send_ref, x_ref, acc, gt, w_ref, sem = rest
    fetch = pltpu.make_async_copy(w_hbm, w_ref, sem)
    fetch.start()
    my_x, my_c = me_ref[0], me_ref[1]
    shards = w_ref.shape[0]
    half = la.shape[0]
    xs = x_ref.shape[0] // (2 * half)
    for part, k, z in (
        (own, 0, 0),
        (la, -1, 0),
        (lb, -1, half),
        (ra, 1, 0),
        (rb, 1, half),
        (oa, 2, 0),
        (ob, 2, half),
    ):
        first = lax.rem(my_x + k + xs, xs) * (2 * half) + z
        for i in range(part.shape[0]):
            x_ref[first + i] = part[i]
    fetch.wait()
    acc[...] = jnp.zeros_like(acc)
    for n in range(shards):
        for s in range(SLOTS):
            p = idx_ref[n, s]
            a = p % blocks + (s // 2) * blocks
            acc[a] += jnp.dot(
                x_ref[2 * n + p // blocks],
                w_ref[n, pl.ds(s * BLK, BLK), :],
                preferred_element_type=F32,
            )
    for c in range(blocks):
        gate, up = acc[c], acc[blocks + c]
        lanes = pl.ds(c * BLK, BLK)
        cot = cot_ref[:, lanes].astype(F32)
        sigma = jax.nn.sigmoid(gate)
        hid_ref[:, lanes] = (gate * sigma * up).astype(BF)
        gg = cot * up * sigma * (1.0 + gate * (1.0 - sigma))
        gu = cot * gate * sigma
        g_ref[c] = gg.astype(BF)
        g_ref[blocks + c] = gu.astype(BF)
        gt[c] = gg.T.astype(BF)
        gt[blocks + c] = gu.T.astype(BF)
    for out_ref, core in ((send_ref, 1 - my_c), (keep_ref, my_c)):
        for y in range(shards // 2):
            n = 2 * y + core
            for s in range(SLOTS):
                p = idx_ref[n, s]
                a = p % blocks + (s // 2) * blocks
                out_ref[y, pl.ds(s * BLK, BLK), :] = jnp.dot(
                    gt[a], x_ref[2 * n + p // blocks], preferred_element_type=F32
                ).astype(BF)


def term_kernel(blocks, me_ref, idx_ref, g_ref, w_ref, own, na, nb, pa, pb, oa, ob):
    my_x = me_ref[0]
    half = na.shape[0]
    xs = w_ref.shape[0] // half
    for part, k, z in (
        (oa, 2, 0),
        (ob, 2, half),
        (nb, 1, half),
        (pa, -1, 0),
        (na, 1, 0),
        (pb, -1, half),
        (own, 0, 0),
    ):
        first = lax.rem(my_x + k + xs, xs) * half + z // 2
        for i in range(part.shape[0] // 2):
            n = first + i
            sums = [None, None]
            for s in range(SLOTS):
                p = idx_ref[n, s]
                prod = lax.dot_general(
                    g_ref[p % blocks + (s // 2) * blocks],
                    w_ref[n, pl.ds(s * BLK, BLK), :],
                    (((1,), (1,)), ((), ())),
                    preferred_element_type=F32,
                )
                for r in range(2):
                    add = jnp.where(p // blocks == r, prod, 0.0)
                    sums[r] = add if sums[r] is None else sums[r] + add
            for r in range(2):
                part[2 * i + r] = sums[r].astype(BF)


def total(parts):
    out = parts[0].astype(F32)
    for part in parts[1:]:
        out = out + part.astype(F32)
    return out


def add_kernel(*refs):
    n = len(refs) // 3
    for a, b, out in zip(refs[:n], refs[n : 2 * n], refs[2 * n :], strict=True):
        for i in range(out.shape[0]):
            out[i] = total([a[i], b[i]]).astype(BF)


def middle_kernel(own, la, lb, ra, rb, out_ref):
    half = la.shape[0]
    for i in range(half):
        out_ref[i] = total([own[i], la[i], ra[i]]).astype(BF)
        out_ref[half + i] = total([own[half + i], lb[i], rb[i]]).astype(BF)


def last_kernel(a_ref, out_ref):
    out_ref[...] = total([a_ref[z] for z in range(a_ref.shape[0])]).astype(BF)


def unpack_kernel(gm_ref, um_ref, b_ref, gg_ref, gu_ref):
    cols = gm_ref.shape[1]
    for t, (m_ref, o_ref) in enumerate(((gm_ref, gg_ref), (um_ref, gu_ref))):
        o_ref[...] = jnp.zeros_like(o_ref)
        first, second, count = kept(m_ref)
        for s, (p, on) in enumerate(((first, count >= 1), (second, count >= 2))):

            @pl.when(on)
            def _(p=p, s=s):
                r, c = block_of(o_ref, p, cols)
                block = b_ref[pl.ds((2 * t + s) * BLK, BLK), :].astype(F32)
                o_ref[pl.ds(r, BLK), pl.ds(c, BLK)] = block.T.astype(BF)


def shift(x, axis, k):
    size = lax.axis_size(axis)
    return lax.ppermute(x, axis, [(i, (i + k) % size) for i in range(size)])


def body(tokens, gate_weight, up_weight, gate_mask, up_mask, cotangent):
    ys, cs, xs, zs = (lax.axis_size(a) for a in ("y", "c", "x", "z"))
    tok, width = cotangent.shape
    blocks = gate_mask.shape[1]
    half = zs // 2
    shape = jax.ShapeDtypeStruct
    me = jnp.stack([lax.axis_index("x"), lax.axis_index("c")]).astype(jnp.int32)

    packed, own = call(
        pack_kernel,
        (shape((META + 16, BLK), BF), shape((zs, tok, BLK), BF)),
        [HBM] * 5,
        [
            pltpu.SMEM(gate_mask.shape, jnp.int32),
            pltpu.SMEM(up_mask.shape, jnp.int32),
            pltpu.VMEM((16, BLK), BF),
            pltpu.VMEM((BLK, BLK), BF),
            pltpu.SemaphoreType.DMA((zs + 2 + SLOTS + 1,)),
        ],
        HBM,
        60,
    )(gate_mask, up_mask, tokens, gate_weight, up_weight)
    weights = lax.all_gather(packed, ("y", "c"), axis=0)
    own = lax.all_to_all(own, "z", 0, 0)
    own_a, own_b = own[:half], own[half:]
    la, rb = shift(own_a, "x", 1), shift(own_b, "x", -1)
    lb, ra = shift(own_b, "x", 1), shift(own_a, "x", -1)
    oa, ob = shift(la, "x", 1), shift(rb, "x", -1)
    index = weights[:, META, :SLOTS].astype(jnp.int32)

    hidden, grads, keep, send = call(
        lambda *refs: front_kernel(blocks, *refs),
        (
            shape((tok, width), BF),
            shape((2 * blocks, tok, BLK), BF),
            shape((ys, META, BLK), BF),
            shape((ys, META, BLK), BF),
        ),
        [SMEM, SMEM] + [VMEM] * 7 + [HBM, VMEM],
        [
            pltpu.VMEM((xs * zs, tok, BLK), BF),
            pltpu.VMEM((2 * blocks, tok, BLK), F32),
            pltpu.VMEM((2 * blocks, BLK, tok), BF),
            pltpu.VMEM(weights.shape, BF),
            pltpu.SemaphoreType.DMA(()),
        ],
    )(me, index, own, la, lb, ra, rb, oa, ob, weights, cotangent)
    other = shift(send, "c", 1)
    piece = shape((half, tok, BLK), BF)
    own, na, nb, pa, pb, oa, ob = call(
        lambda *refs: term_kernel(blocks, *refs),
        (shape((zs, tok, BLK), BF),) + (piece,) * 6,
        [SMEM, SMEM, VMEM, VMEM],
    )(me, index, grads, weights)
    oa, ob = shift(oa, "x", 1), shift(ob, "x", -1)
    lb, ra = shift(nb, "x", 1), shift(pa, "x", -1)
    (wgrads,) = call(add_kernel, (shape(keep.shape, BF),), [VMEM] * 2)(keep, other)
    wgrads = lax.psum_scatter(wgrads, "y", scatter_dimension=0)
    na, pb = call(add_kernel, (piece,) * 2, [VMEM] * 4)(na, pb, oa, ob)
    la, rb = shift(na, "x", 1), shift(pb, "x", -1)
    own = call(middle_kernel, shape(own.shape, BF), [VMEM] * 5)(own, la, lb, ra, rb)
    own = lax.all_to_all(own, "z", 0, 0)
    grad_tokens = call(last_kernel, shape(tokens.shape, BF), [VMEM])(own)
    grad_gate, grad_up = call(
        unpack_kernel,
        (shape(gate_weight.shape, BF), shape(up_weight.shape, BF)),
        [SMEM, SMEM, VMEM],
    )(gate_mask, up_mask, wgrads)
    return hidden, grad_tokens, grad_gate, grad_up


def solution(mesh):
    rows, cols = mesh.devices.shape
    cut = Mesh(mesh.devices.reshape(rows // 2, 2, 4, cols // 4), ("y", "c", "x", "z"))
    spec = P(("y", "c"), ("x", "z"))
    return jax.shard_map(
        body, mesh=cut, in_specs=(spec,) * 6, out_specs=(spec,) * 4, check_vma=False
    )
```

time: 147 us -> 154 us (1.048)
  the two profiles are of different devices: /device:TPU:31 before, /device:TPU:24 now
where the time goes in v3:
time: 154 us
  blocking collectives  46.6 us (30%)
  starting transfers between devices  44.2 us (29%)
  Pallas kernels  30.6 us (20%)
  waiting for transfers between devices  14.6 us (9%)
  between operations  14.3 us (9%)
  local copies, waits for them, and re-layouts  2.56 us (2%)
    all_to_all x2, blocking collectives, body(): own = lax.all_to_all(own, 'z', 0, 0)  46.6 us
    ppermute x13, starting transfers between devices, shift(): return lax.ppermute(x, axis, [(i, (i + k) % size) for i in range(size)])  44.1 us
    pallas_call x1, Pallas kernels, body(): call(pack_kernel, (shape((META + 16, BLK), BF), shape((zs, tok, BLK), BF)...  20.1 us
    ppermute x13, waiting for transfers between devices, shift(): return lax.ppermute(x, axis, [(i, (i + k) % size) for i in range(size)])  14.5 us
    pallas_call x1, Pallas kernels, body(): call(lambda *refs: front_kernel(blocks, *refs), (shape((tok, width), BF),...  4.43 us
  transfers between devices with their start and end apart: 15, of which 7 were waited for; matrix products, arithmetic and copies ran while one was open for 1% of the time, Pallas kernels for 2%

profile of v3, /device:TPU:24, one launch (start us, length us, event | category | flops | bytes accessed | tf_op | source)
XLA Modules:
  0.0 153.5 jit_solution(6938000589240915632)
XLA Ops:
  7.2 0.0 copy-start.2
  7.2 0.0 all-gather.3.cloned.1.call-start
  7.2 20.1 %shard_map.93 = (bf16[528,128]{1,0:T(8,128)(2,1)}, bf16[8,256,128]{2,1,0:T(8,128)(2,1)}) custom-call(s32[2,4]{1,0:T(2,128)} %gm_ref.3, s32[2,4]{1,0:T(2,128)} %um_ref.3, bf16[256,128]{1,0:T(8,128)(2,1)} %tok_ref.1, bf16[256,512]{1,0:T(8,128)(2,1)} %gw_ref.1, bf16[256,512]{1,0:T(8,128)(2,1)} %uw_ref.1), custom_call_target="tpu_custom_call" | custom-call | tf_op jit(solution)/shard_map/pallas_call | solution.py:226
  27.3 0.0 all-gather.3.cloned.1.call-update
  27.4 0.0 reduce-scatter.2.cloned.1.call-start
  27.4 28.8 %all_to_all.10.refs_2_ = bf16[8,256,128]{2,1,0:T(8,128)(2,1)S(1)} all-to-all(bf16[8,256,128]{2,1,0:T(8,128)(2,1)} %get-tuple-element.22), channel_id=1, replica_groups=mesh['y'=8,'c'=2,'x'=4,'z'=8] {'z'}, dimensions={0} | all-to-all | bytes 1048576 | tf_op jit(solution)/shard_map/all_to_all | solution.py:241
  56.3 3.4 %collective-permute-start = (bf16[4,256,128]{2,1,0:T(8,128)(2,1)S(1)}, bf16[4,256,128]{2,1,0:T(8,128)(2,1)S(1)}, u32[]{:S(2)}, u32[]{:S(2)}) collective-permute-start(bf16[4,256,128]{2,1,0:T(8,128)(2,1)S(1)} %get-tuple-element.39), channel_id=1, source_target_pairs={{0,8},{8,16},{16,24},{24,0},{1,9},{9,17},{17,25},{25,1},{2,10},{10... | collective-permute-start | bytes 786440 | tf_op jit(solution)/shard_map/ppermute | solution.py:215
  59.7 3.7 %collective-permute-start.3 = (bf16[4,256,128]{2,1,0:T(8,128)(2,1)S(1)}, bf16[4,256,128]{2,1,0:T(8,128)(2,1)S(1)}, u32[]{:S(2)}, u32[]{:S(2)}) collective-permute-start(bf16[4,256,128]{2,1,0:T(8,128)(2,1)S(1)} %get-tuple-element.38), channel_id=1, source_target_pairs={{0,24},{8,0},{16,8},{24,16},{1,25},{9,1},{17,9},{25,17},{2,26},{10... | collective-permute-start | bytes 786440 | tf_op jit(solution)/shard_map/ppermute | solution.py:215
  63.3 2.2 %collective-permute-start.1 = (bf16[4,256,128]{2,1,0:T(8,128)(2,1)S(1)}, bf16[4,256,128]{2,1,0:T(8,128)(2,1)S(1)}, u32[]{:S(2)}, u32[]{:S(2)}) collective-permute-start(bf16[4,256,128]{2,1,0:T(8,128)(2,1)S(1)} %get-tuple-element.38), channel_id=1, source_target_pairs={{0,8},{8,16},{16,24},{24,0},{1,9},{9,17},{17,25},{25,1},{2,10},{10... | collective-permute-start | bytes 786440 | tf_op jit(solution)/shard_map/ppermute | solution.py:215
  65.5 4.9 %collective-permute-start.2 = (bf16[4,256,128]{2,1,0:T(8,128)(2,1)S(1)}, bf16[4,256,128]{2,1,0:T(8,128)(2,1)S(1)}, u32[]{:S(2)}, u32[]{:S(2)}) collective-permute-start(bf16[4,256,128]{2,1,0:T(8,128)(2,1)S(1)} %get-tuple-element.39), channel_id=1, source_target_pairs={{0,24},{8,0},{16,8},{24,16},{1,25},{9,1},{17,9},{25,17},{2,26},{10... | collective-permute-start | bytes 786440 | tf_op jit(solution)/shard_map/ppermute | solution.py:215
  70.4 0.0 collective-permute-done.refs_3_
  70.4 1.9 %collective-permute-start.4 = (bf16[4,256,128]{2,1,0:T(8,128)(2,1)S(1)}, bf16[4,256,128]{2,1,0:T(8,128)(2,1)S(1)}, u32[]{:S(2)}, u32[]{:S(2)}) collective-permute-start(bf16[4,256,128]{2,1,0:T(8,128)(2,1)S(1)} %collective-permute-done.refs_3_), channel_id=1, source_target_pairs={{0,8},{8,16},{16,24},{24,0},{1,9},{9,17},{17,25},{25,1},{2,10},{10... | collective-permute-start | bytes 786440 | tf_op jit(solution)/shard_map/ppermute | solution.py:215
  72.3 0.0 collective-permute-done.3.refs_6_
  72.3 5.1 %collective-permute-start.5 = (bf16[4,256,128]{2,1,0:T(8,128)(2,1)S(1)}, bf16[4,256,128]{2,1,0:T(8,128)(2,1)S(1)}, u32[]{:S(2)}, u32[]{:S(2)}) collective-permute-start(bf16[4,256,128]{2,1,0:T(8,128)(2,1)S(1)} %collective-permute-done.3.refs_6_), channel_id=1, source_target_pairs={{0,24},{8,0},{16,8},{24,16},{1,25},{9,1},{17,9},{25,17},{2,26},{10... | collective-permute-start | bytes 786440 | tf_op jit(solution)/shard_map/ppermute | solution.py:215
  77.5 0.1 pad_add_fusion.refs_0_
  77.6 0.0 all-gather.3.cloned.1.call-done
  77.6 0.8 slice_convert_fusion
  78.3 0.0 collective-permute-done.1.refs_4_
  78.3 0.0 collective-permute-done.2.refs_5_
  78.3 2.3 %collective-permute-done.4.refs_7_ = bf16[4,256,128]{2,1,0:T(8,128)(2,1)S(1)} collective-permute-done((bf16[4,256,128]{2,1,0:T(8,128)(2,1)S(1)}, bf16[4,256,128]{2,1,0:T(8,128)(2,1)S(1)}, u32[]{:S(2)}, u32[]{:S(2)}) %collective-permute-start.4) | collective-permute-done | bytes 262176 | tf_op jit(solution)/shard_map/ppermute | solution.py:215
  80.7 1.2 collective-permute-done.5.refs_8_
  81.9 0.0 copy-done.2
  81.9 0.0 copy-start
  81.9 1.6 %copy-done = bf16[8448,128]{1,0:T(8,128)(2,1)S(1)} copy-done((bf16[8448,128]{1,0:T(8,128)(2,1)S(1)}, bf16[8448,128]{1,0:T(8,128)(2,1)}, u32[]{:S(2)}) %copy-start) | copy-done | bytes 2162712
  83.5 4.4 %shard_map.94 = (bf16[256,512]{1,0:T(8,128)(2,1)}, bf16[8,256,128]{2,1,0:T(8,128)(2,1)S(1)}, bf16[8,512,128]{2,1,0:T(8,128)(2,1)S(1)}, bf16[8,512,128]{2,1,0:T(8,128)(2,1)S(1)}) custom-call(s32[2]{0:T(128)S(1)} %pad_add_fusion.refs_0_, s32[16,4]{1,0:T(8,128)S(1)} %bitcast.9, bf16[8,256,128]{2,1,0:T(8,128)(2,1)S(1)} %all_to_all.10.refs_2_, ...), custom_call_target="tpu_custom_call" | custom-call | tf_op jit(solution)/shard_map/pallas_call | solution.py:248
  87.9 0.0 copy-start.1
  87.9 2.1 %collective-permute-start.12 = (bf16[8,512,128]{2,1,0:T(8,128)(2,1)S(1)}, bf16[8,512,128]{2,1,0:T(8,128)(2,1)S(1)}, u32[]{:S(2)}, u32[]{:S(2)}) collective-permute-start(bf16[8,512,128]{2,1,0:T(8,128)(2,1)S(1)} %get-tuple-element.35), channel_id=1, source_target_pairs={{0,32},{32,0},{1,33},{33,1},{2,34},{34,2},{3,35},{35,3},{4,36},{36... | collective-permute-start | bytes 3145736 | tf_op jit(solution)/shard_map/ppermute | solution.py:215
  90.0 2.6 %collective-permute-done.12.refs_1_ = bf16[8,512,128]{2,1,0:T(8,128)(2,1)S(1)} collective-permute-done((bf16[8,512,128]{2,1,0:T(8,128)(2,1)S(1)}, bf16[8,512,128]{2,1,0:T(8,128)(2,1)S(1)}, u32[]{:S(2)}, u32[]{:S(2)}) %collective-permute-start.12) | collective-permute-done | bytes 1048608 | tf_op jit(solution)/shard_map/ppermute | solution.py:215
  92.6 1.3 shard_map.99
  93.9 0.0 reduce-scatter.2.cloned.1.call-update
  93.9 0.0 copy-done.1
  93.9 2.0 %shard_map.95 = (bf16[8,256,128]{2,1,0:T(8,128)(2,1)S(1)}, bf16[4,256,128]{2,1,0:T(8,128)(2,1)S(1)}, bf16[4,256,128]{2,1,0:T(8,128)(2,1)S(1)}, bf16[4,256,128]{2...) custom-call(s32[2]{0:T(128)S(1)} %pad_add_fusion.refs_0_, ...), custom_call_target="tpu_custom_call" | custom-call | tf_op jit(solution)/shard_map/pallas_call | solution.py:267
  96.0 1.9 %collective-permute-start.6 = (bf16[4,256,128]{2,1,0:T(8,128)(2,1)S(1)}, bf16[4,256,128]{2,1,0:T(8,128)(2,1)S(1)}, u32[]{:S(2)}, u32[]{:S(2)}) collective-permute-start(bf16[4,256,128]{2,1,0:T(8,128)(2,1)S(1)} %get-tuple-element.28), channel_id=1, source_target_pairs={{0,8},{8,16},{16,24},{24,0},{1,9},{9,17},{17,25},{25,1},{2,10},{10... | collective-permute-start | bytes 786440 | tf_op jit(solution)/shard_map/ppermute | solution.py:215
  97.9 5.6 %collective-permute-start.7 = (bf16[4,256,128]{2,1,0:T(8,128)(2,1)S(1)}, bf16[4,256,128]{2,1,0:T(8,128)(2,1)S(1)}, u32[]{:S(2)}, u32[]{:S(2)}) collective-permute-start(bf16[4,256,128]{2,1,0:T(8,128)(2,1)S(1)} %get-tuple-element.29), channel_id=1, source_target_pairs={{0,24},{8,0},{16,8},{24,16},{1,25},{9,1},{17,9},{25,17},{2,26},{10... | collective-permute-start | bytes 786440 | tf_op jit(solution)/shard_map/ppermute | solution.py:215
  103.5 3.9 %collective-permute-start.10 = (bf16[4,256,128]{2,1,0:T(8,128)(2,1)S(1)}, bf16[4,256,128]{2,1,0:T(8,128)(2,1)S(1)}, u32[]{:S(2)}, u32[]{:S(2)}) collective-permute-start(bf16[4,256,128]{2,1,0:T(8,128)(2,1)S(1)} %get-tuple-element.32), channel_id=1, source_target_pairs={{0,24},{8,0},{16,8},{24,16},{1,25},{9,1},{17,9},{25,17},{2,26},{10... | collective-permute-start | bytes 786440 | tf_op jit(solution)/shard_map/ppermute | solution.py:215
  107.4 1.9 %collective-permute-start.9 = (bf16[4,256,128]{2,1,0:T(8,128)(2,1)S(1)}, bf16[4,256,128]{2,1,0:T(8,128)(2,1)S(1)}, u32[]{:S(2)}, u32[]{:S(2)}) collective-permute-start(bf16[4,256,128]{2,1,0:T(8,128)(2,1)S(1)} %get-tuple-element.31), channel_id=1, source_target_pairs={{0,8},{8,16},{16,24},{24,0},{1,9},{9,17},{17,25},{25,1},{2,10},{10... | collective-permute-start | bytes 786440 | tf_op jit(solution)/shard_map/ppermute | solution.py:215
  109.4 0.0 collective-permute-done.6.refs_2_
  109.4 0.8 collective-permute-done.7.refs_3_
  110.1 0.0 copy-start.4
  110.1 0.0 copy-start.5
  110.1 0.1 shard_map.96
  110.3 5.6 %collective-permute-start.11 = (bf16[4,256,128]{2,1,0:T(8,128)(2,1)S(1)}, bf16[4,256,128]{2,1,0:T(8,128)(2,1)S(1)}, u32[]{:S(2)}, u32[]{:S(2)}) collective-permute-start(bf16[4,256,128]{2,1,0:T(8,128)(2,1)S(1)} %get-tuple-element.33), channel_id=1, source_target_pairs={{0,24},{8,0},{16,8},{24,16},{1,25},{9,1},{17,9},{25,17},{2,26},{10... | collective-permute-start | bytes 786440 | tf_op jit(solution)/shard_map/ppermute | solution.py:215
  115.9 1.9 %collective-permute-start.8 = (bf16[4,256,128]{2,1,0:T(8,128)(2,1)S(1)}, bf16[4,256,128]{2,1,0:T(8,128)(2,1)S(1)}, u32[]{:S(2)}, u32[]{:S(2)}) collective-permute-start(bf16[4,256,128]{2,1,0:T(8,128)(2,1)S(1)} %get-tuple-element.30), channel_id=1, source_target_pairs={{0,8},{8,16},{16,24},{24,0},{1,9},{9,17},{17,25},{25,1},{2,10},{10... | collective-permute-start | bytes 786440 | tf_op jit(solution)/shard_map/ppermute | solution.py:215
  117.8 0.0 collective-permute-done.10.ra
  117.8 0.2 collective-permute-done.9.lb
  118.0 2.5 %collective-permute-done.11.rb = bf16[4,256,128]{2,1,0:T(8,128)(2,1)S(1)} collective-permute-done((bf16[4,256,128]{2,1,0:T(8,128)(2,1)S(1)}, bf16[4,256,128]{2,1,0:T(8,128)(2,1)S(1)}, u32[]{:S(2)}, u32[]{:S(2)}) %collective-permute-start.11) | collective-permute-done | bytes 262176 | tf_op jit(solution)/shard_map/ppermute | solution.py:215
  120.6 4.9 %collective-permute-done.8.la = bf16[4,256,128]{2,1,0:T(8,128)(2,1)S(1)} collective-permute-done((bf16[4,256,128]{2,1,0:T(8,128)(2,1)S(1)}, bf16[4,256,128]{2,1,0:T(8,128)(2,1)S(1)}, u32[]{:S(2)}, u32[]{:S(2)}) %collective-permute-start.8) | collective-permute-done | bytes 262176 | tf_op jit(solution)/shard_map/ppermute | solution.py:215
  125.4 0.2 shard_map.97
  125.6 17.8 %all_to_all.11.a_ref = bf16[8,256,128]{2,1,0:T(8,128)(2,1)S(1)} all-to-all(bf16[8,256,128]{2,1,0:T(8,128)(2,1)S(1)} %shard_map.97), channel_id=1, replica_groups=mesh['y'=8,'c'=2,'x'=4,'z'=8] {'z'}, dimensions={0} | all-to-all | bytes 1048576 | tf_op jit(solution)/shard_map/all_to_all | solution.py:279
  143.4 0.7 shard_map.98
  144.1 0.0 reduce-scatter.2.cloned.1.call-done
  144.1 0.0 copy-done.4
  144.1 0.0 copy-done.5
  144.1 0.0 copy-start.3
  144.1 0.9 copy-done.3
  145.0 1.7 %shard_map.100 = (bf16[256,512]{1,0:T(8,128)(2,1)}, bf16[256,512]{1,0:T(8,128)(2,1)}) custom-call(s32[2,4]{1,0:T(2,128)S(1)} %copy-done.4, s32[2,4]{1,0:T(2,128)S(1)} %copy-done.5, bf16[512,128]{1,0:T(8,128)(2,1)S(1)} %bitcast.8), custom_call_target="tpu_custom_call" | custom-call | tf_op jit(solution)/shard_map/pallas_call | solution.py:281
  (1 shorter events, 0.0 us)
Async XLA Ops:
  7.2 74.7 %copy-start.2 = (bf16[256,512]{1,0:T(8,128)(2,1)S(1)}, bf16[256,512]{1,0:T(8,128)(2,1)}, u32[]{:S(2)}) copy-start(bf16[256,512]{1,0:T(8,128)(2,1)} %refs_10_.1) | copy-start | bytes 786436
  7.2 70.4 %all-gather.3.cloned.1.call-start = ((), (), s32[]{:S(2)}) async-start(), calls=%async_computation.4 | async-start | bytes 2297856 | tf_op jit(solution)/shard_map/all_gather | solution.py:240
  27.4 116.7 %reduce-scatter.2.cloned.1.call-start = ((), (), s32[]{:S(2)}) async-start(), calls=%async_computation.3 | async-start | bytes 1179648 | tf_op jit(solution)/shard_map/reduce_scatter | solution.py:275
  56.3 14.1 %collective-permute-start = (bf16[4,256,128]{2,1,0:T(8,128)(2,1)S(1)}, bf16[4,256,128]{2,1,0:T(8,128)(2,1)S(1)}, u32[]{:S(2)}, u32[]{:S(2)}) collective-permute-start(bf16[4,256,128]{2,1,0:T(8,128)(2,1)S(1)} %get-tuple-element.39), channel_id=1, source_target_pairs={{0,8},{8,16},{16,24},{24,0},{1,9},{9,17},{17,25},{25,1},{2,10},{10... | collective-permute-start | bytes 786440 | tf_op jit(solution)/shard_map/ppermute | solution.py:215
  59.7 12.7 %collective-permute-start.3 = (bf16[4,256,128]{2,1,0:T(8,128)(2,1)S(1)}, bf16[4,256,128]{2,1,0:T(8,128)(2,1)S(1)}, u32[]{:S(2)}, u32[]{:S(2)}) collective-permute-start(bf16[4,256,128]{2,1,0:T(8,128)(2,1)S(1)} %get-tuple-element.38), channel_id=1, source_target_pairs={{0,24},{8,0},{16,8},{24,16},{1,25},{9,1},{17,9},{25,17},{2,26},{10... | collective-permute-start | bytes 786440 | tf_op jit(solution)/shard_map/ppermute | solution.py:215
  63.3 15.0 %collective-permute-start.1 = (bf16[4,256,128]{2,1,0:T(8,128)(2,1)S(1)}, bf16[4,256,128]{2,1,0:T(8,128)(2,1)S(1)}, u32[]{:S(2)}, u32[]{:S(2)}) collective-permute-start(bf16[4,256,128]{2,1,0:T(8,128)(2,1)S(1)} %get-tuple-element.38), channel_id=1, source_target_pairs={{0,8},{8,16},{16,24},{24,0},{1,9},{9,17},{17,25},{25,1},{2,10},{10... | collective-permute-start | bytes 786440 | tf_op jit(solution)/shard_map/ppermute | solution.py:215
  65.5 12.8 %collective-permute-start.2 = (bf16[4,256,128]{2,1,0:T(8,128)(2,1)S(1)}, bf16[4,256,128]{2,1,0:T(8,128)(2,1)S(1)}, u32[]{:S(2)}, u32[]{:S(2)}) collective-permute-start(bf16[4,256,128]{2,1,0:T(8,128)(2,1)S(1)} %get-tuple-element.39), channel_id=1, source_target_pairs={{0,24},{8,0},{16,8},{24,16},{1,25},{9,1},{17,9},{25,17},{2,26},{10... | collective-permute-start | bytes 786440 | tf_op jit(solution)/shard_map/ppermute | solution.py:215
  70.4 10.3 %collective-permute-start.4 = (bf16[4,256,128]{2,1,0:T(8,128)(2,1)S(1)}, bf16[4,256,128]{2,1,0:T(8,128)(2,1)S(1)}, u32[]{:S(2)}, u32[]{:S(2)}) collective-permute-start(bf16[4,256,128]{2,1,0:T(8,128)(2,1)S(1)} %collective-permute-done.refs_3_), channel_id=1, source_target_pairs={{0,8},{8,16},{16,24},{24,0},{1,9},{9,17},{17,25},{25,1},{2,10},{10... | collective-permute-start | bytes 786440 | tf_op jit(solution)/shard_map/ppermute | solution.py:215
  72.3 9.5 %collective-permute-start.5 = (bf16[4,256,128]{2,1,0:T(8,128)(2,1)S(1)}, bf16[4,256,128]{2,1,0:T(8,128)(2,1)S(1)}, u32[]{:S(2)}, u32[]{:S(2)}) collective-permute-start(bf16[4,256,128]{2,1,0:T(8,128)(2,1)S(1)} %collective-permute-done.3.refs_6_), channel_id=1, source_target_pairs={{0,24},{8,0},{16,8},{24,16},{1,25},{9,1},{17,9},{25,17},{2,26},{10... | collective-permute-start | bytes 786440 | tf_op jit(solution)/shard_map/ppermute | solution.py:215
  81.9 1.6 %copy-start = (bf16[8448,128]{1,0:T(8,128)(2,1)S(1)}, bf16[8448,128]{1,0:T(8,128)(2,1)}, u32[]{:S(2)}) copy-start(bf16[8448,128]{1,0:T(8,128)(2,1)} %all-gather.3.cloned.1.call-done) | copy-start | bytes 6488068
  87.9 6.0 %copy-start.1 = (bf16[8448,128]{1,0:T(8,128)(2,1)S(1)}, bf16[8448,128]{1,0:T(8,128)(2,1)}, u32[]{:S(2)}) copy-start(bf16[8448,128]{1,0:T(8,128)(2,1)} %all-gather.3.cloned.1.call-done) | copy-start | bytes 6488068
  87.9 4.7 %collective-permute-start.12 = (bf16[8,512,128]{2,1,0:T(8,128)(2,1)S(1)}, bf16[8,512,128]{2,1,0:T(8,128)(2,1)S(1)}, u32[]{:S(2)}, u32[]{:S(2)}) collective-permute-start(bf16[8,512,128]{2,1,0:T(8,128)(2,1)S(1)} %get-tuple-element.35), channel_id=1, source_target_pairs={{0,32},{32,0},{1,33},{33,1},{2,34},{34,2},{3,35},{35,3},{4,36},{36... | collective-permute-start | bytes 3145736 | tf_op jit(solution)/shard_map/ppermute | solution.py:215
  96.0 13.4 %collective-permute-start.6 = (bf16[4,256,128]{2,1,0:T(8,128)(2,1)S(1)}, bf16[4,256,128]{2,1,0:T(8,128)(2,1)S(1)}, u32[]{:S(2)}, u32[]{:S(2)}) collective-permute-start(bf16[4,256,128]{2,1,0:T(8,128)(2,1)S(1)} %get-tuple-element.28), channel_id=1, source_target_pairs={{0,8},{8,16},{16,24},{24,0},{1,9},{9,17},{17,25},{25,1},{2,10},{10... | collective-permute-start | bytes 786440 | tf_op jit(solution)/shard_map/ppermute | solution.py:215
  97.9 12.2 %collective-permute-start.7 = (bf16[4,256,128]{2,1,0:T(8,128)(2,1)S(1)}, bf16[4,256,128]{2,1,0:T(8,128)(2,1)S(1)}, u32[]{:S(2)}, u32[]{:S(2)}) collective-permute-start(bf16[4,256,128]{2,1,0:T(8,128)(2,1)S(1)} %get-tuple-element.29), channel_id=1, source_target_pairs={{0,24},{8,0},{16,8},{24,16},{1,25},{9,1},{17,9},{25,17},{2,26},{10... | collective-permute-start | bytes 786440 | tf_op jit(solution)/shard_map/ppermute | solution.py:215
  103.5 14.3 %collective-permute-start.10 = (bf16[4,256,128]{2,1,0:T(8,128)(2,1)S(1)}, bf16[4,256,128]{2,1,0:T(8,128)(2,1)S(1)}, u32[]{:S(2)}, u32[]{:S(2)}) collective-permute-start(bf16[4,256,128]{2,1,0:T(8,128)(2,1)S(1)} %get-tuple-element.32), channel_id=1, source_target_pairs={{0,24},{8,0},{16,8},{24,16},{1,25},{9,1},{17,9},{25,17},{2,26},{10... | collective-permute-start | bytes 786440 | tf_op jit(solution)/shard_map/ppermute | solution.py:215
  107.4 10.6 %collective-permute-start.9 = (bf16[4,256,128]{2,1,0:T(8,128)(2,1)S(1)}, bf16[4,256,128]{2,1,0:T(8,128)(2,1)S(1)}, u32[]{:S(2)}, u32[]{:S(2)}) collective-permute-start(bf16[4,256,128]{2,1,0:T(8,128)(2,1)S(1)} %get-tuple-element.31), channel_id=1, source_target_pairs={{0,8},{8,16},{16,24},{24,0},{1,9},{9,17},{17,25},{25,1},{2,10},{10... | collective-permute-start | bytes 786440 | tf_op jit(solution)/shard_map/ppermute | solution.py:215
  110.1 33.9 %copy-start.4 = (s32[2,4]{1,0:T(2,128)S(1)}, s32[2,4]{1,0:T(2,128)}, u32[]{:S(2)}) copy-start(s32[2,4]{1,0:T(2,128)} %gm_ref.3) | copy-start | bytes 100
  110.1 33.9 %copy-start.5 = (s32[2,4]{1,0:T(2,128)S(1)}, s32[2,4]{1,0:T(2,128)}, u32[]{:S(2)}) copy-start(s32[2,4]{1,0:T(2,128)} %um_ref.3) | copy-start | bytes 100
  110.3 10.3 %collective-permute-start.11 = (bf16[4,256,128]{2,1,0:T(8,128)(2,1)S(1)}, bf16[4,256,128]{2,1,0:T(8,128)(2,1)S(1)}, u32[]{:S(2)}, u32[]{:S(2)}) collective-permute-start(bf16[4,256,128]{2,1,0:T(8,128)(2,1)S(1)} %get-tuple-element.33), channel_id=1, source_target_pairs={{0,24},{8,0},{16,8},{24,16},{1,25},{9,1},{17,9},{25,17},{2,26},{10... | collective-permute-start | bytes 786440 | tf_op jit(solution)/shard_map/ppermute | solution.py:215
  115.9 9.5 %collective-permute-start.8 = (bf16[4,256,128]{2,1,0:T(8,128)(2,1)S(1)}, bf16[4,256,128]{2,1,0:T(8,128)(2,1)S(1)}, u32[]{:S(2)}, u32[]{:S(2)}) collective-permute-start(bf16[4,256,128]{2,1,0:T(8,128)(2,1)S(1)} %get-tuple-element.30), channel_id=1, source_target_pairs={{0,8},{8,16},{16,24},{24,0},{1,9},{9,17},{17,25},{25,1},{2,10},{10... | collective-permute-start | bytes 786440 | tf_op jit(solution)/shard_map/ppermute | solution.py:215
  144.1 0.9 copy-start.3
Sparse Core Ops, SparseCore 0:
  27.5 47.1 all-gather.2
  94.0 36.4 reduce-scatter.1

commit v4 on v3

v4 whole, which is shorter than its diff:
```python
import jax
import jax.numpy as jnp
from jax import lax
from jax.experimental import pallas as pl
from jax.experimental.pallas import tpu as pltpu
from jax.sharding import Mesh
from jax.sharding import PartitionSpec as P

BLK = 128
SLOTS = 4
META = SLOTS * BLK
BF = jnp.bfloat16
F32 = jnp.float32
VMEM = pl.BlockSpec(memory_space=pltpu.VMEM)
SMEM = pl.BlockSpec(memory_space=pltpu.SMEM)
HBM = pl.BlockSpec(memory_space=pltpu.HBM)


def call(kernel, outs, in_specs, scratch=(), out_spec=VMEM, limit=40):
    return pl.pallas_call(
        kernel,
        out_shape=outs,
        in_specs=in_specs,
        out_specs=jax.tree.map(lambda _: out_spec, outs),
        scratch_shapes=list(scratch),
        compiler_params=pltpu.CompilerParams(vmem_limit_bytes=limit * 1024 * 1024),
    )


def kept(mask_ref):
    cols = mask_ref.shape[1]
    first, second, count = jnp.int32(0), jnp.int32(0), jnp.int32(0)
    for p in range(mask_ref.shape[0] * cols):
        m = mask_ref[p // cols, p % cols]
        on = m == 1
        first = jnp.where(on & (count == 0), p, first)
        second = jnp.where(on & (count == 1), p, second)
        count = count + m
    return first, second, count


def block_of(ref, p, cols):
    r = pl.multiple_of((p // cols) * BLK, BLK)
    c = pl.multiple_of((p % cols) * BLK, BLK)
    return r, c


def turn(i, stage, size):
    if stage == "far":
        return (i + size // 2) % size
    if stage == "one":
        return i + 1 - 2 * (i % 2)
    return (i + size - 1 + 2 * (i % 2)) % size


def stages(size):
    return (["far"] if size > 4 else []) + ["one", "two"]


def swap(x, axis, stage):
    size = lax.axis_size(axis)
    return lax.ppermute(x, axis, [(i, turn(i, stage, size)) for i in range(size)])


def origin(i, j, size):
    for bit, stage in reversed(list(enumerate(stages(size)))):
        if j >> bit & 1:
            i = turn(i, stage, size)
    return i


def pack_kernel(gm_ref, um_ref, tok_ref, gw_ref, uw_ref, out_ref, all_ref, gm, um, sems):
    cols = gm.shape[1]
    tokens = pltpu.make_async_copy(tok_ref, all_ref.at[0], sems.at[0])
    masks = [
        pltpu.make_async_copy(a, b, sems.at[1 + t])
        for t, (a, b) in enumerate(((gm_ref, gm), (um_ref, um)))
    ]
    for copy in masks + [tokens]:
        copy.start()
    for copy in masks:
        copy.wait()
    chosen = []
    for t, (m_ref, w_ref) in enumerate(((gm, gw_ref), (um, uw_ref))):
        first, second, count = kept(m_ref)
        for s, (p, on) in enumerate(((first, count >= 1), (second, count >= 2))):
            r, c = block_of(w_ref, p, cols)
            place = pl.ds((2 * t + s) * BLK, BLK)
            copy = pltpu.make_async_copy(
                w_ref.at[pl.ds(r, BLK), pl.ds(c, BLK)], out_ref.at[place], sems.at[3 + 2 * t + s]
            )
            copy.start()
            chosen.append((p, on, place, copy))
    lane = lax.broadcasted_iota(jnp.int32, (out_ref.shape[0] - META, BLK), 1)
    meta = jnp.zeros(lane.shape, jnp.int32)
    for s, (p, _, _, _) in enumerate(chosen):
        meta = jnp.where(lane == s, p, meta)
    out_ref[pl.ds(META, lane.shape[0]), :] = meta.astype(F32).astype(BF)
    tokens.wait()
    for z in range(1, all_ref.shape[0]):
        all_ref[z] = all_ref[0]
    for _, on, place, copy in chosen:
        copy.wait()

        @pl.when(jnp.logical_not(on))
        def _(place=place):
            out_ref[place, :] = jnp.zeros((BLK, BLK), BF)


def main_kernel(blocks, me_ref, own, r1, r2, oa, ob, w0, w1, w2, w3, cot_ref, *rest):
    hid_ref, keep_ref, send_ref, t0, t1, t2, ta, tb = rest[:8]
    x_ref, w_ref, at_vec, at_ref, idx_ref, acc, g_ref, gt, sem = rest[8:]
    count = w0.shape[0]
    for g, part in enumerate((w0, w1, w2, w3)):
        for i in range(count):
            meta = part[i, pl.ds(META, 16), :].astype(F32).astype(jnp.int32)
            at_vec[pl.ds(g * count + i, 1), :] = meta[:1]
    scalars = pltpu.make_async_copy(at_vec, at_ref, sem)
    scalars.start()
    my_x, my_c, my_y = me_ref[0], me_ref[1], me_ref[2]
    shards = w_ref.shape[0]
    ys, zs, half = shards // 2, own.shape[0], oa.shape[0]
    xs = 2 * shards // zs
    far, one, two = ((turn(my_x, stage, xs)) for stage in ("far", "one", "two"))
    for part, x, z in ((own, my_x, 0), (r1, one, 0), (r2, two, 0), (oa, far, 0), (ob, far, half)):
        for i in range(part.shape[0]):
            x_ref[x * zs + z + i] = part[i]
    scalars.wait()
    for g, part in enumerate((w0, w1, w2, w3)):
        for i in range(count):
            y = origin(my_y, (g % 2) * count + i, ys)
            n = 2 * y + (my_c if g < 2 else 1 - my_c)
            w_ref[n] = part[i, pl.ds(0, META), :]
            for s in range(SLOTS):
                idx_ref[n, s] = at_ref[g * count + i, s]

    acc[...] = jnp.zeros_like(acc)
    for n in range(shards):
        for s in range(SLOTS):
            p = idx_ref[n, s]
            a = p % blocks + (s // 2) * blocks
            acc[a] += jnp.dot(
                x_ref[2 * n + p // blocks],
                w_ref[n, pl.ds(s * BLK, BLK), :],
                preferred_element_type=F32,
            )
    for c in range(blocks):
        gate, up = acc[c], acc[blocks + c]
        lanes = pl.ds(c * BLK, BLK)
        cot = cot_ref[:, lanes].astype(F32)
        sigma = jax.nn.sigmoid(gate)
        hid_ref[:, lanes] = (gate * sigma * up).astype(BF)
        gg = cot * up * sigma * (1.0 + gate * (1.0 - sigma))
        gu = cot * gate * sigma
        g_ref[c] = gg.astype(BF)
        g_ref[blocks + c] = gu.astype(BF)
        gt[c] = gg.T.astype(BF)
        gt[blocks + c] = gu.T.astype(BF)
    for out_ref, core in ((send_ref, 1 - my_c), (keep_ref, my_c)):
        for j in range(ys):
            n = 2 * origin(my_y, j, ys) + core
            for s in range(SLOTS):
                p = idx_ref[n, s]
                a = p % blocks + (s // 2) * blocks
                out_ref[j, pl.ds(s * BLK, BLK), :] = jnp.dot(
                    gt[a], x_ref[2 * n + p // blocks], preferred_element_type=F32
                ).astype(BF)
    for part, x, z in ((ta, far, 0), (tb, far, half), (t1, one, 0), (t2, two, 0), (t0, my_x, 0)):
        for i in range(part.shape[0] // 2):
            n = x * (zs // 2) + z // 2 + i
            sums = [None, None]
            for s in range(SLOTS):
                p = idx_ref[n, s]
                prod = lax.dot_general(
                    g_ref[p % blocks + (s // 2) * blocks],
                    w_ref[n, pl.ds(s * BLK, BLK), :],
                    (((1,), (1,)), ((), ())),
                    preferred_element_type=F32,
                )
                for r in range(2):
                    add = jnp.where(p // blocks == r, prod, 0.0)
                    sums[r] = add if sums[r] is None else sums[r] + add
            for r in range(2):
                part[2 * i + r] = sums[r].astype(BF)


def total(parts):
    out = parts[0].astype(F32)
    for part in parts[1:]:
        out = out + part.astype(F32)
    return out


def halves_kernel(a_ref, b_ref, lo_ref, hi_ref):
    half = lo_ref.shape[0]
    for i in range(half):
        lo_ref[i] = total([a_ref[i], b_ref[i]]).astype(BF)
        hi_ref[i] = total([a_ref[half + i], b_ref[half + i]]).astype(BF)


def forward_kernel(t1, t2, ra, rb, o1, o2):
    half = ra.shape[0]
    for i in range(half):
        o1[i] = total([t1[i], ra[i]]).astype(BF)
        o1[half + i] = t1[half + i]
        o2[i] = t2[i]
        o2[half + i] = total([t2[half + i], rb[i]]).astype(BF)


def middle_kernel(t0, r1, r2, out_ref):
    for i in range(out_ref.shape[0]):
        out_ref[i] = total([t0[i], r1[i], r2[i]]).astype(BF)


def last_kernel(a_ref, out_ref):
    out_ref[...] = total([a_ref[z] for z in range(a_ref.shape[0])]).astype(BF)


def unpack_kernel(gm_ref, um_ref, a_ref, b_ref, gg_ref, gu_ref):
    cols = gm_ref.shape[1]
    for t, (m_ref, o_ref) in enumerate(((gm_ref, gg_ref), (um_ref, gu_ref))):
        o_ref[...] = jnp.zeros_like(o_ref)
        first, second, count = kept(m_ref)
        for s, (p, on) in enumerate(((first, count >= 1), (second, count >= 2))):

            @pl.when(on)
            def _(p=p, s=s):
                r, c = block_of(o_ref, p, cols)
                rows = pl.ds((2 * t + s) * BLK, BLK)
                block = total([a_ref[0, rows, :], b_ref[0, rows, :]])
                o_ref[pl.ds(r, BLK), pl.ds(c, BLK)] = block.T.astype(BF)


def body(tokens, gate_weight, up_weight, gate_mask, up_mask, cotangent):
    ys, xs, zs = (lax.axis_size(a) for a in ("y", "x", "z"))
    tok, width = cotangent.shape
    blocks = gate_mask.shape[1]
    half = zs // 2
    shape = jax.ShapeDtypeStruct
    me = jnp.stack([lax.axis_index(a) for a in ("x", "c", "y")]).astype(jnp.int32)

    packed, own = call(
        pack_kernel,
        (shape((META + 16, BLK), BF), shape((zs, tok, BLK), BF)),
        [HBM] * 5,
        [
            pltpu.SMEM(gate_mask.shape, jnp.int32),
            pltpu.SMEM(up_mask.shape, jnp.int32),
            pltpu.SemaphoreType.DMA((3 + SLOTS,)),
        ],
        limit=60,
    )(gate_mask, up_mask, tokens, gate_weight, up_weight)
    own = lax.all_to_all(own, "z", 0, 0)
    w = packed[None]
    *early, late = stages(ys)
    for stage in early:
        w = jnp.concatenate([w, swap(w, "y", stage)])
    w_late = swap(w, "y", late)
    r1, r2 = swap(own, "x", "one"), swap(own, "x", "two")
    w = [w, w_late, swap(w, "c", "one"), swap(w_late, "c", "one")]
    oa, ob = swap(r1[:half], "x", "two"), swap(r2[half:], "x", "one")

    whole, piece = shape((zs, tok, BLK), BF), shape((half, tok, BLK), BF)
    hidden, keep, send, t0, t1, t2, ta, tb = call(
        lambda *refs: main_kernel(blocks, *refs),
        (
            shape((tok, width), BF),
            shape((ys, META, BLK), BF),
            shape((ys, META, BLK), BF),
            whole,
            whole,
            whole,
            piece,
            piece,
        ),
        [SMEM] + [VMEM] * 10,
        [
            pltpu.VMEM((xs * zs, tok, BLK), BF),
            pltpu.VMEM((2 * ys, META, BLK), BF),
            pltpu.VMEM((2 * ys, BLK), jnp.int32),
            pltpu.SMEM((2 * ys, BLK), jnp.int32),
            pltpu.SMEM((2 * ys, SLOTS), jnp.int32),
            pltpu.VMEM((2 * blocks, tok, BLK), F32),
            pltpu.VMEM((2 * blocks, tok, BLK), BF),
            pltpu.VMEM((2 * blocks, BLK, tok), BF),
            pltpu.SemaphoreType.DMA(()),
        ],
    )(me, own, r1, r2, oa, ob, *w, cotangent)
    other = swap(send, "c", "one")
    ra, rb = swap(ta, "x", "two"), swap(tb, "x", "one")
    lo = keep
    for stage in reversed(stages(ys)):
        part = shape((lo.shape[0] // 2, *lo.shape[1:]), BF)
        lo, hi = call(halves_kernel, (part, part), [VMEM] * 2)(lo, other)
        other = swap(hi, "y", stage)
    t1, t2 = call(forward_kernel, (whole, whole), [VMEM] * 4)(t1, t2, ra, rb)
    r1, r2 = swap(t1, "x", "one"), swap(t2, "x", "two")
    own = call(middle_kernel, whole, [VMEM] * 3)(t0, r1, r2)
    own = lax.all_to_all(own, "z", 0, 0)
    grad_tokens = call(last_kernel, shape(tokens.shape, BF), [VMEM])(own)
    grad_gate, grad_up = call(
        unpack_kernel,
        (shape(gate_weight.shape, BF), shape(up_weight.shape, BF)),
        [SMEM, SMEM, VMEM, VMEM],
    )(gate_mask, up_mask, lo, other)
    return hidden, grad_tokens, grad_gate, grad_up


def solution(mesh):
    rows, cols = mesh.devices.shape
    cut = Mesh(mesh.devices.reshape(rows // 2, 2, 4, cols // 4), ("y", "c", "x", "z"))
    spec = P(("y", "c"), ("x", "z"))
    return jax.shard_map(
        body, mesh=cut, in_specs=(spec,) * 6, out_specs=(spec,) * 4, check_vma=False
    )
```

time: 154 us -> 138 us (0.90)
  the two profiles are of different devices: /device:TPU:24 before, /device:TPU:16 now
where the time goes in v4:
time: 138 us; the launch traced here: 137 us
  starting transfers between devices  69.6 us (50%)
  waiting for transfers between devices  51.7 us (37%)
  Pallas kernels  13.3 us (10%)
  local copies, waits for them, and re-layouts  1.46 us (1%)
    ppermute x17, starting transfers between devices, swap(): lax.ppermute(x, axis, [(i, turn(i, stage, size)) for i in range(size)])  53.7 us
    ppermute x17, waiting for transfers between devices, swap(): lax.ppermute(x, axis, [(i, turn(i, stage, size)) for i in range(size)])  44.5 us
    all_to_all x2, starting transfers between devices, body(): own = lax.all_to_all(own, 'z', 0, 0)  15.9 us
    all_to_all x2, waiting for transfers between devices, body(): own = lax.all_to_all(own, 'z', 0, 0)  7.27 us
    pallas_call x1, Pallas kernels, body(): call(lambda *refs: main_kernel(blocks, *refs), (shape((tok, width), BF),...  6.92 us
  transfers between devices with their start and end apart: 19, of which 13 were waited for; matrix products, arithmetic and copies ran while one was open for 1% of the time, Pallas kernels for 2%

profile of v4, /device:TPU:16, one launch (start us, length us, event | category | flops | bytes accessed | tf_op | source)
XLA Modules:
  0.0 137.1 jit_solution(7078334577353595696)
XLA Ops:
  0.6 2.5 %shard_map.93 = (bf16[528,128]{1,0:T(8,128)(2,1)}, bf16[8,256,128]{2,1,0:T(8,128)(2,1)}) custom-call(s32[2,4]{1,0:T(2,128)} %gm_ref.3, s32[2,4]{1,0:T(2,128)} %um_ref.3, bf16[256,128]{1,0:T(8,128)(2,1)} %tok_ref.1, bf16[256,512]{1,0:T(8,128)(2,1)} %gw_ref.1, bf16[256,512]{1,0:T(8,128)(2,1)} %uw_ref.1), custom_call_target="tpu_custom_call" | custom-call | tf_op jit(solution)/shard_map/pallas_call | solution.py:242
  3.2 5.9 %collective-permute-start.4 = (bf16[1,528,128]{2,1,0:T(8,128)(2,1)}, bf16[1,528,128]{2,1,0:T(8,128)(2,1)S(1)}, u32[]{:S(2)}, u32[]{:S(2)}) collective-permute-start(bf16[1,528,128]{2,1,0:T(8,128)(2,1)} %bitcast.4), channel_id=1, source_target_pairs={{0,256},{64,320},{128,384},{192,448},{256,0},{320,64},{384,128},{4... | collective-permute-start | bytes 405512 | tf_op jit(solution)/shard_map/ppermute | solution.py:62
  9.1 0.0 copy-start.3
  9.1 10.5 %all-to-all-start = ((bf16[8,256,128]{2,1,0:T(8,128)(2,1)}), bf16[8,256,128]{2,1,0:T(8,128)(2,1)S(1)}, u32[]{:S(2)}, u32[]{:S(2)}) async-start(bf16[8,256,128]{2,1,0:T(8,128)(2,1)} %get-tuple-element.24), calls=%async_computation | async-start | bytes 1048576 | tf_op jit(solution)/shard_map/all_to_all | solution.py:253
  19.6 0.0 collective-permute-done.4
  19.6 0.0 copy-done.3
  19.6 2.6 %collective-permute-start.5 = (bf16[2,528,128]{2,1,0:T(8,128)(2,1)S(1)}, bf16[2,528,128]{2,1,0:T(8,128)(2,1)S(1)}, u32[]{:S(2)}, u32[]{:S(2)}) collective-permute-start(bf16[2,528,128]{2,1,0:T(8,128)(2,1)S(1)} %pad_maximum_fusion.1), channel_id=1, source_target_pairs={{0,64},{64,0},{128,192},{192,128},{256,320},{320,256},{384,448},{4... | collective-permute-start | bytes 811016 | tf_op jit(solution)/shard_map/ppermute | solution.py:62
  22.2 6.9 %collective-permute-done.5 = bf16[2,528,128]{2,1,0:T(8,128)(2,1)S(1)} collective-permute-done((bf16[2,528,128]{2,1,0:T(8,128)(2,1)S(1)}, bf16[2,528,128]{2,1,0:T(8,128)(2,1)S(1)}, u32[]{:S(2)}, u32[]{:S(2)}) %collective-permute-start.5) | collective-permute-done | bytes 270368 | tf_op jit(solution)/shard_map/ppermute | solution.py:62
  29.1 0.1 pad_maximum_fusion.refs_6_
  29.2 3.3 %collective-permute-start.6 = (bf16[4,528,128]{2,1,0:T(8,128)(2,1)S(1)}, bf16[4,528,128]{2,1,0:T(8,128)(2,1)S(1)}, u32[]{:S(2)}, u32[]{:S(2)}) collective-permute-start(bf16[4,528,128]{2,1,0:T(8,128)(2,1)S(1)} %pad_maximum_fusion.refs_6_), channel_id=1, source_target_pairs={{0,448},{64,128},{128,64},{192,256},{256,192},{320,384},{384,320},... | collective-permute-start | bytes 1622024 | tf_op jit(solution)/shard_map/ppermute | solution.py:62
  32.5 4.3 %all-to-all-done.refs_1_ = bf16[8,256,128]{2,1,0:T(8,128)(2,1)S(1)} async-done(((bf16[8,256,128]{2,1,0:T(8,128)(2,1)}), bf16[8,256,128]{2,1,0:T(8,128)(2,1)S(1)}, u32[]{:S(2)}, u32[]{:S(2)}) %all-to-all-start) | async-done | bytes 524320 | tf_op jit(solution)/shard_map/all_to_all | solution.py:253
  36.7 4.7 %collective-permute-start.1 = (bf16[8,256,128]{2,1,0:T(8,128)(2,1)S(1)}, bf16[8,256,128]{2,1,0:T(8,128)(2,1)S(1)}, u32[]{:S(2)}, u32[]{:S(2)}) collective-permute-start(bf16[8,256,128]{2,1,0:T(8,128)(2,1)S(1)} %all-to-all-done.refs_1_), channel_id=1, source_target_pairs={{0,24},{8,16},{16,8},{24,0},{1,25},{9,17},{17,9},{25,1},{2,26},{10... | collective-permute-start | bytes 1572872 | tf_op jit(solution)/shard_map/ppermute | solution.py:62
  41.4 2.1 %collective-permute-start = (bf16[8,256,128]{2,1,0:T(8,128)(2,1)S(1)}, bf16[8,256,128]{2,1,0:T(8,128)(2,1)S(1)}, u32[]{:S(2)}, u32[]{:S(2)}) collective-permute-start(bf16[8,256,128]{2,1,0:T(8,128)(2,1)S(1)} %all-to-all-done.refs_1_), channel_id=1, source_target_pairs={{0,8},{8,0},{16,24},{24,16},{1,9},{9,1},{17,25},{25,17},{2,10},{10... | collective-permute-start | bytes 1572872 | tf_op jit(solution)/shard_map/ppermute | solution.py:62
  43.5 1.9 %collective-permute-start.7 = (bf16[4,528,128]{2,1,0:T(8,128)(2,1)S(1)}, bf16[4,528,128]{2,1,0:T(8,128)(2,1)S(1)}, u32[]{:S(2)}, u32[]{:S(2)}) collective-permute-start(bf16[4,528,128]{2,1,0:T(8,128)(2,1)S(1)} %pad_maximum_fusion.refs_6_), channel_id=1, source_target_pairs={{0,32},{32,0},{1,33},{33,1},{2,34},{34,2},{3,35},{35,3},{4,36},{36... | collective-permute-start | bytes 1622024 | tf_op jit(solution)/shard_map/ppermute | solution.py:62
  45.5 0.0 collective-permute-done.6.refs_7_
  45.5 2.4 %collective-permute-start.8 = (bf16[4,528,128]{2,1,0:T(8,128)(2,1)S(1)}, bf16[4,528,128]{2,1,0:T(8,128)(2,1)}, u32[]{:S(2)}, u32[]{:S(2)}) collective-permute-start(bf16[4,528,128]{2,1,0:T(8,128)(2,1)S(1)} %collective-permute-done.6.refs_7_), channel_id=1, source_target_pairs={{0,32},{32,0},{1,33},{33,1},{2,34},{34,2},{3,35},{35,3},{4,36},{36... | collective-permute-start | bytes 1622024 | tf_op jit(solution)/shard_map/ppermute | solution.py:62
  47.9 4.7 %collective-permute-done.1.refs_3_ = bf16[8,256,128]{2,1,0:T(8,128)(2,1)S(1)} collective-permute-done((bf16[8,256,128]{2,1,0:T(8,128)(2,1)S(1)}, bf16[8,256,128]{2,1,0:T(8,128)(2,1)S(1)}, u32[]{:S(2)}, u32[]{:S(2)}) %collective-permute-start.1) | collective-permute-done | bytes 524320 | tf_op jit(solution)/shard_map/ppermute | solution.py:62
  52.6 0.7 slice.9
  53.3 0.0 copy-start
  53.3 2.5 %collective-permute-start.3 = (bf16[4,256,128]{2,1,0:T(8,128)(2,1)}, bf16[4,256,128]{2,1,0:T(8,128)(2,1)}, u32[]{:S(2)}, u32[]{:S(2)}) collective-permute-start(bf16[4,256,128]{2,1,0:T(8,128)(2,1)} %slice.9), channel_id=1, source_target_pairs={{0,8},{8,0},{16,24},{24,16},{1,9},{9,1},{17,25},{25,17},{2,10},{10... | collective-permute-start | bytes 786440 | tf_op jit(solution)/shard_map/ppermute | solution.py:62
  55.8 0.1 collective-permute-done.refs_2_
  55.9 0.7 slice.8
  56.7 4.3 %collective-permute-start.2 = (bf16[4,256,128]{2,1,0:T(8,128)(2,1)}, bf16[4,256,128]{2,1,0:T(8,128)(2,1)}, u32[]{:S(2)}, u32[]{:S(2)}) collective-permute-start(bf16[4,256,128]{2,1,0:T(8,128)(2,1)} %slice.8), channel_id=1, source_target_pairs={{0,24},{8,16},{16,8},{24,0},{1,25},{9,17},{17,9},{25,1},{2,26},{10... | collective-permute-start | bytes 786440 | tf_op jit(solution)/shard_map/ppermute | solution.py:62
  60.9 0.1 pad_add_fusion.refs_0_
  61.0 0.0 collective-permute-done.7.refs_8_
  61.0 0.0 collective-permute-done.8.refs_9_
  61.0 1.0 collective-permute-done.3.refs_5_
  62.0 4.4 %collective-permute-done.2.refs_4_ = bf16[4,256,128]{2,1,0:T(8,128)(2,1)} collective-permute-done((bf16[4,256,128]{2,1,0:T(8,128)(2,1)}, bf16[4,256,128]{2,1,0:T(8,128)(2,1)}, u32[]{:S(2)}, u32[]{:S(2)}) %collective-permute-start.2) | collective-permute-done | bytes 262176 | tf_op jit(solution)/shard_map/ppermute | solution.py:62
  66.4 0.0 copy-done
  66.4 6.9 %shard_map.94 = (bf16[256,512]{1,0:T(8,128)(2,1)}, bf16[8,512,128]{2,1,0:T(8,128)(2,1)S(1)}, bf16[8,512,128]{2,1,0:T(8,128)(2,1)S(1)}, bf16[8,256,128]{2,1,0:T(8...) custom-call(s32[3]{0:T(128)S(1)} %pad_add_fusion.refs_0_, ...), custom_call_target="tpu_custom_call" | custom-call | tf_op jit(solution)/shard_map/pallas_call | solution.py:264
  73.4 1.9 %collective-permute-start.13 = (bf16[8,512,128]{2,1,0:T(8,128)(2,1)S(1)}, bf16[8,512,128]{2,1,0:T(8,128)(2,1)S(1)}, u32[]{:S(2)}, u32[]{:S(2)}) collective-permute-start(bf16[8,512,128]{2,1,0:T(8,128)(2,1)S(1)} %get-tuple-element.35), channel_id=1, source_target_pairs={{0,32},{32,0},{1,33},{33,1},{2,34},{34,2},{3,35},{35,3},{4,36},{36... | collective-permute-start | bytes 3145736 | tf_op jit(solution)/shard_map/ppermute | solution.py:62
  75.3 4.3 %collective-permute-start.9 = (bf16[4,256,128]{2,1,0:T(8,128)(2,1)S(1)}, bf16[4,256,128]{2,1,0:T(8,128)(2,1)S(1)}, u32[]{:S(2)}, u32[]{:S(2)}) collective-permute-start(bf16[4,256,128]{2,1,0:T(8,128)(2,1)S(1)} %get-tuple-element.30), channel_id=1, source_target_pairs={{0,24},{8,16},{16,8},{24,0},{1,25},{9,17},{17,9},{25,1},{2,26},{10... | collective-permute-start | bytes 786440 | tf_op jit(solution)/shard_map/ppermute | solution.py:62
  79.6 2.1 %collective-permute-start.10 = (bf16[4,256,128]{2,1,0:T(8,128)(2,1)S(1)}, bf16[4,256,128]{2,1,0:T(8,128)(2,1)S(1)}, u32[]{:S(2)}, u32[]{:S(2)}) collective-permute-start(bf16[4,256,128]{2,1,0:T(8,128)(2,1)S(1)} %get-tuple-element.31), channel_id=1, source_target_pairs={{0,8},{8,0},{16,24},{24,16},{1,9},{9,1},{17,25},{25,17},{2,10},{10... | collective-permute-start | bytes 786440 | tf_op jit(solution)/shard_map/ppermute | solution.py:62
  81.7 5.4 %collective-permute-done.9.ra = bf16[4,256,128]{2,1,0:T(8,128)(2,1)S(1)} collective-permute-done((bf16[4,256,128]{2,1,0:T(8,128)(2,1)S(1)}, bf16[4,256,128]{2,1,0:T(8,128)(2,1)S(1)}, u32[]{:S(2)}, u32[]{:S(2)}) %collective-permute-start.9) | collective-permute-done | bytes 262176 | tf_op jit(solution)/shard_map/ppermute | solution.py:62
  87.1 2.8 %collective-permute-done.10.rb = bf16[4,256,128]{2,1,0:T(8,128)(2,1)S(1)} collective-permute-done((bf16[4,256,128]{2,1,0:T(8,128)(2,1)S(1)}, bf16[4,256,128]{2,1,0:T(8,128)(2,1)S(1)}, u32[]{:S(2)}, u32[]{:S(2)}) %collective-permute-start.10) | collective-permute-done | bytes 262176 | tf_op jit(solution)/shard_map/ppermute | solution.py:62
  89.9 0.1 shard_map.95
  90.0 2.2 %collective-permute-start.11 = (bf16[8,256,128]{2,1,0:T(8,128)(2,1)S(1)}, bf16[8,256,128]{2,1,0:T(8,128)(2,1)S(1)}, u32[]{:S(2)}, u32[]{:S(2)}) collective-permute-start(bf16[8,256,128]{2,1,0:T(8,128)(2,1)S(1)} %get-tuple-element.32), channel_id=1, source_target_pairs={{0,8},{8,0},{16,24},{24,16},{1,9},{9,1},{17,25},{25,17},{2,10},{10... | collective-permute-start | bytes 1572872 | tf_op jit(solution)/shard_map/ppermute | solution.py:62
  92.2 2.8 %collective-permute-start.12 = (bf16[8,256,128]{2,1,0:T(8,128)(2,1)S(1)}, bf16[8,256,128]{2,1,0:T(8,128)(2,1)S(1)}, u32[]{:S(2)}, u32[]{:S(2)}) collective-permute-start(bf16[8,256,128]{2,1,0:T(8,128)(2,1)S(1)} %get-tuple-element.33), channel_id=1, source_target_pairs={{0,24},{8,16},{16,8},{24,0},{1,25},{9,17},{17,9},{25,1},{2,26},{10... | collective-permute-start | bytes 1572872 | tf_op jit(solution)/shard_map/ppermute | solution.py:62
  95.0 0.0 collective-permute-done.13.b_ref
  95.0 0.2 shard_map.98
  95.3 3.6 %collective-permute-start.14 = (bf16[4,512,128]{2,1,0:T(8,128)(2,1)S(1)}, bf16[4,512,128]{2,1,0:T(8,128)(2,1)S(1)}, u32[]{:S(2)}, u32[]{:S(2)}) collective-permute-start(bf16[4,512,128]{2,1,0:T(8,128)(2,1)S(1)} %get-tuple-element.37), channel_id=1, source_target_pairs={{0,448},{64,128},{128,64},{192,256},{256,192},{320,384},{384,320},... | collective-permute-start | bytes 1572872 | tf_op jit(solution)/shard_map/ppermute | solution.py:62
  98.9 6.3 %collective-permute-done.11.r1 = bf16[8,256,128]{2,1,0:T(8,128)(2,1)S(1)} collective-permute-done((bf16[8,256,128]{2,1,0:T(8,128)(2,1)S(1)}, bf16[8,256,128]{2,1,0:T(8,128)(2,1)S(1)}, u32[]{:S(2)}, u32[]{:S(2)}) %collective-permute-start.11) | collective-permute-done | bytes 524320 | tf_op jit(solution)/shard_map/ppermute | solution.py:62
  105.2 3.3 %collective-permute-done.12.r2 = bf16[8,256,128]{2,1,0:T(8,128)(2,1)S(1)} collective-permute-done((bf16[8,256,128]{2,1,0:T(8,128)(2,1)S(1)}, bf16[8,256,128]{2,1,0:T(8,128)(2,1)S(1)}, u32[]{:S(2)}, u32[]{:S(2)}) %collective-permute-start.12) | collective-permute-done | bytes 524320 | tf_op jit(solution)/shard_map/ppermute | solution.py:62
  108.4 1.0 shard_map.96
  109.4 5.4 %all-to-all-start.1 = ((bf16[8,256,128]{2,1,0:T(8,128)(2,1)}), bf16[8,256,128]{2,1,0:T(8,128)(2,1)S(1)}, u32[]{:S(2)}, u32[]{:S(2)}) async-start(bf16[8,256,128]{2,1,0:T(8,128)(2,1)} %shard_map.96), calls=%async_computation.1 | async-start | bytes 1048576 | tf_op jit(solution)/shard_map/all_to_all | solution.py:299
  114.8 0.0 collective-permute-done.14.b_ref
  114.8 0.1 shard_map.99
  114.9 2.7 %collective-permute-start.15 = (bf16[2,512,128]{2,1,0:T(8,128)(2,1)S(1)}, bf16[2,512,128]{2,1,0:T(8,128)(2,1)S(1)}, u32[]{:S(2)}, u32[]{:S(2)}) collective-permute-start(bf16[2,512,128]{2,1,0:T(8,128)(2,1)S(1)} %get-tuple-element.39), channel_id=1, source_target_pairs={{0,64},{64,0},{128,192},{192,128},{256,320},{320,256},{384,448},{4... | collective-permute-start | bytes 786440 | tf_op jit(solution)/shard_map/ppermute | solution.py:62
  117.6 5.7 %collective-permute-done.15.b_ref = bf16[2,512,128]{2,1,0:T(8,128)(2,1)S(1)} collective-permute-done((bf16[2,512,128]{2,1,0:T(8,128)(2,1)S(1)}, bf16[2,512,128]{2,1,0:T(8,128)(2,1)S(1)}, u32[]{:S(2)}, u32[]{:S(2)}) %collective-permute-start.15) | collective-permute-done | bytes 262176 | tf_op jit(solution)/shard_map/ppermute | solution.py:62
  123.3 0.1 shard_map.100
  123.3 4.6 %collective-permute-start.16 = (bf16[1,512,128]{2,1,0:T(8,128)(2,1)S(1)}, bf16[1,512,128]{2,1,0:T(8,128)(2,1)S(1)}, u32[]{:S(2)}, u32[]{:S(2)}) collective-permute-start(bf16[1,512,128]{2,1,0:T(8,128)(2,1)S(1)} %get-tuple-element.41), channel_id=1, source_target_pairs={{0,256},{64,320},{128,384},{192,448},{256,0},{320,64},{384,128},{4... | collective-permute-start | bytes 393224 | tf_op jit(solution)/shard_map/ppermute | solution.py:62
  128.0 3.0 %all-to-all-done.1.a_ref = bf16[8,256,128]{2,1,0:T(8,128)(2,1)S(1)} async-done(((bf16[8,256,128]{2,1,0:T(8,128)(2,1)}), bf16[8,256,128]{2,1,0:T(8,128)(2,1)S(1)}, u32[]{:S(2)}, u32[]{:S(2)}) %all-to-all-start.1) | async-done | bytes 524320 | tf_op jit(solution)/shard_map/all_to_all | solution.py:299
  131.0 0.0 copy-start.2
  131.0 0.7 shard_map.97
  131.7 0.0 copy-start.1
  131.7 3.8 %collective-permute-done.16.b_ref = bf16[1,512,128]{2,1,0:T(8,128)(2,1)S(1)} collective-permute-done((bf16[1,512,128]{2,1,0:T(8,128)(2,1)S(1)}, bf16[1,512,128]{2,1,0:T(8,128)(2,1)S(1)}, u32[]{:S(2)}, u32[]{:S(2)}) %collective-permute-start.16) | collective-permute-done | bytes 131104 | tf_op jit(solution)/shard_map/ppermute | solution.py:62
  135.5 0.0 copy-done.2
  135.5 0.0 copy-done.1
  135.5 1.6 %shard_map.101 = (bf16[256,512]{1,0:T(8,128)(2,1)}, bf16[256,512]{1,0:T(8,128)(2,1)}) custom-call(s32[2,4]{1,0:T(2,128)S(1)} %copy-done.1, s32[2,4]{1,0:T(2,128)S(1)} %copy-done.2, bf16[1,512,128]{2,1,0:T(8,128)(2,1)S(1)} %get-tuple-element.40.a_ref, bf16[1,512,128]{2,1,0:T(8,128)(2,1)S(1)} %collective-permute-done.16.b_ref), custom_call_target="tpu_custom_call" | custom-call | tf_op jit(solution)/shard_map/pallas_call | solution.py:301
  (1 shorter events, 0.0 us)
Async XLA Ops:
  3.2 16.4 %collective-permute-start.4 = (bf16[1,528,128]{2,1,0:T(8,128)(2,1)}, bf16[1,528,128]{2,1,0:T(8,128)(2,1)S(1)}, u32[]{:S(2)}, u32[]{:S(2)}) collective-permute-start(bf16[1,528,128]{2,1,0:T(8,128)(2,1)} %bitcast.4), channel_id=1, source_target_pairs={{0,256},{64,320},{128,384},{192,448},{256,0},{320,64},{384,128},{4... | collective-permute-start | bytes 405512 | tf_op jit(solution)/shard_map/ppermute | solution.py:62
  9.1 10.5 %copy-start.3 = (bf16[528,128]{1,0:T(8,128)(2,1)S(1)}, bf16[528,128]{1,0:T(8,128)(2,1)}, u32[]{:S(2)}) copy-start(bf16[528,128]{1,0:T(8,128)(2,1)} %get-tuple-element.25) | copy-start | bytes 405508
  9.1 27.7 %all-to-all-start = ((bf16[8,256,128]{2,1,0:T(8,128)(2,1)}), bf16[8,256,128]{2,1,0:T(8,128)(2,1)S(1)}, u32[]{:S(2)}, u32[]{:S(2)}) async-start(bf16[8,256,128]{2,1,0:T(8,128)(2,1)} %get-tuple-element.24), calls=%async_computation | async-start | bytes 1048576 | tf_op jit(solution)/shard_map/all_to_all | solution.py:253
  19.6 9.5 %collective-permute-start.5 = (bf16[2,528,128]{2,1,0:T(8,128)(2,1)S(1)}, bf16[2,528,128]{2,1,0:T(8,128)(2,1)S(1)}, u32[]{:S(2)}, u32[]{:S(2)}) collective-permute-start(bf16[2,528,128]{2,1,0:T(8,128)(2,1)S(1)} %pad_maximum_fusion.1), channel_id=1, source_target_pairs={{0,64},{64,0},{128,192},{192,128},{256,320},{320,256},{384,448},{4... | collective-permute-start | bytes 811016 | tf_op jit(solution)/shard_map/ppermute | solution.py:62
  29.2 16.3 %collective-permute-start.6 = (bf16[4,528,128]{2,1,0:T(8,128)(2,1)S(1)}, bf16[4,528,128]{2,1,0:T(8,128)(2,1)S(1)}, u32[]{:S(2)}, u32[]{:S(2)}) collective-permute-start(bf16[4,528,128]{2,1,0:T(8,128)(2,1)S(1)} %pad_maximum_fusion.refs_6_), channel_id=1, source_target_pairs={{0,448},{64,128},{128,64},{192,256},{256,192},{320,384},{384,320},... | collective-permute-start | bytes 1622024 | tf_op jit(solution)/shard_map/ppermute | solution.py:62
  36.7 15.8 %collective-permute-start.1 = (bf16[8,256,128]{2,1,0:T(8,128)(2,1)S(1)}, bf16[8,256,128]{2,1,0:T(8,128)(2,1)S(1)}, u32[]{:S(2)}, u32[]{:S(2)}) collective-permute-start(bf16[8,256,128]{2,1,0:T(8,128)(2,1)S(1)} %all-to-all-done.refs_1_), channel_id=1, source_target_pairs={{0,24},{8,16},{16,8},{24,0},{1,25},{9,17},{17,9},{25,1},{2,26},{10... | collective-permute-start | bytes 1572872 | tf_op jit(solution)/shard_map/ppermute | solution.py:62
  41.4 14.5 %collective-permute-start = (bf16[8,256,128]{2,1,0:T(8,128)(2,1)S(1)}, bf16[8,256,128]{2,1,0:T(8,128)(2,1)S(1)}, u32[]{:S(2)}, u32[]{:S(2)}) collective-permute-start(bf16[8,256,128]{2,1,0:T(8,128)(2,1)S(1)} %all-to-all-done.refs_1_), channel_id=1, source_target_pairs={{0,8},{8,0},{16,24},{24,16},{1,9},{9,1},{17,25},{25,17},{2,10},{10... | collective-permute-start | bytes 1572872 | tf_op jit(solution)/shard_map/ppermute | solution.py:62
  43.5 17.5 %collective-permute-start.7 = (bf16[4,528,128]{2,1,0:T(8,128)(2,1)S(1)}, bf16[4,528,128]{2,1,0:T(8,128)(2,1)S(1)}, u32[]{:S(2)}, u32[]{:S(2)}) collective-permute-start(bf16[4,528,128]{2,1,0:T(8,128)(2,1)S(1)} %pad_maximum_fusion.refs_6_), channel_id=1, source_target_pairs={{0,32},{32,0},{1,33},{33,1},{2,34},{34,2},{3,35},{35,3},{4,36},{36... | collective-permute-start | bytes 1622024 | tf_op jit(solution)/shard_map/ppermute | solution.py:62
  45.5 15.5 %collective-permute-start.8 = (bf16[4,528,128]{2,1,0:T(8,128)(2,1)S(1)}, bf16[4,528,128]{2,1,0:T(8,128)(2,1)}, u32[]{:S(2)}, u32[]{:S(2)}) collective-permute-start(bf16[4,528,128]{2,1,0:T(8,128)(2,1)S(1)} %collective-permute-done.6.refs_7_), channel_id=1, source_target_pairs={{0,32},{32,0},{1,33},{33,1},{2,34},{34,2},{3,35},{35,3},{4,36},{36... | collective-permute-start | bytes 1622024 | tf_op jit(solution)/shard_map/ppermute | solution.py:62
  53.3 13.2 %copy-start = (bf16[256,512]{1,0:T(8,128)(2,1)S(1)}, bf16[256,512]{1,0:T(8,128)(2,1)}, u32[]{:S(2)}) copy-start(bf16[256,512]{1,0:T(8,128)(2,1)} %refs_10_.1) | copy-start | bytes 786436
  53.3 8.7 %collective-permute-start.3 = (bf16[4,256,128]{2,1,0:T(8,128)(2,1)}, bf16[4,256,128]{2,1,0:T(8,128)(2,1)}, u32[]{:S(2)}, u32[]{:S(2)}) collective-permute-start(bf16[4,256,128]{2,1,0:T(8,128)(2,1)} %slice.9), channel_id=1, source_target_pairs={{0,8},{8,0},{16,24},{24,16},{1,9},{9,1},{17,25},{25,17},{2,10},{10... | collective-permute-start | bytes 786440 | tf_op jit(solution)/shard_map/ppermute | solution.py:62
  56.7 9.8 %collective-permute-start.2 = (bf16[4,256,128]{2,1,0:T(8,128)(2,1)}, bf16[4,256,128]{2,1,0:T(8,128)(2,1)}, u32[]{:S(2)}, u32[]{:S(2)}) collective-permute-start(bf16[4,256,128]{2,1,0:T(8,128)(2,1)} %slice.8), channel_id=1, source_target_pairs={{0,24},{8,16},{16,8},{24,0},{1,25},{9,17},{17,9},{25,1},{2,26},{10... | collective-permute-start | bytes 786440 | tf_op jit(solution)/shard_map/ppermute | solution.py:62
  73.4 21.7 %collective-permute-start.13 = (bf16[8,512,128]{2,1,0:T(8,128)(2,1)S(1)}, bf16[8,512,128]{2,1,0:T(8,128)(2,1)S(1)}, u32[]{:S(2)}, u32[]{:S(2)}) collective-permute-start(bf16[8,512,128]{2,1,0:T(8,128)(2,1)S(1)} %get-tuple-element.35), channel_id=1, source_target_pairs={{0,32},{32,0},{1,33},{33,1},{2,34},{34,2},{3,35},{35,3},{4,36},{36... | collective-permute-start | bytes 3145736 | tf_op jit(solution)/shard_map/ppermute | solution.py:62
  75.3 11.8 %collective-permute-start.9 = (bf16[4,256,128]{2,1,0:T(8,128)(2,1)S(1)}, bf16[4,256,128]{2,1,0:T(8,128)(2,1)S(1)}, u32[]{:S(2)}, u32[]{:S(2)}) collective-permute-start(bf16[4,256,128]{2,1,0:T(8,128)(2,1)S(1)} %get-tuple-element.30), channel_id=1, source_target_pairs={{0,24},{8,16},{16,8},{24,0},{1,25},{9,17},{17,9},{25,1},{2,26},{10... | collective-permute-start | bytes 786440 | tf_op jit(solution)/shard_map/ppermute | solution.py:62
  79.6 10.3 %collective-permute-start.10 = (bf16[4,256,128]{2,1,0:T(8,128)(2,1)S(1)}, bf16[4,256,128]{2,1,0:T(8,128)(2,1)S(1)}, u32[]{:S(2)}, u32[]{:S(2)}) collective-permute-start(bf16[4,256,128]{2,1,0:T(8,128)(2,1)S(1)} %get-tuple-element.31), channel_id=1, source_target_pairs={{0,8},{8,0},{16,24},{24,16},{1,9},{9,1},{17,25},{25,17},{2,10},{10... | collective-permute-start | bytes 786440 | tf_op jit(solution)/shard_map/ppermute | solution.py:62
  90.0 15.1 %collective-permute-start.11 = (bf16[8,256,128]{2,1,0:T(8,128)(2,1)S(1)}, bf16[8,256,128]{2,1,0:T(8,128)(2,1)S(1)}, u32[]{:S(2)}, u32[]{:S(2)}) collective-permute-start(bf16[8,256,128]{2,1,0:T(8,128)(2,1)S(1)} %get-tuple-element.32), channel_id=1, source_target_pairs={{0,8},{8,0},{16,24},{24,16},{1,9},{9,1},{17,25},{25,17},{2,10},{10... | collective-permute-start | bytes 1572872 | tf_op jit(solution)/shard_map/ppermute | solution.py:62
  92.2 16.2 %collective-permute-start.12 = (bf16[8,256,128]{2,1,0:T(8,128)(2,1)S(1)}, bf16[8,256,128]{2,1,0:T(8,128)(2,1)S(1)}, u32[]{:S(2)}, u32[]{:S(2)}) collective-permute-start(bf16[8,256,128]{2,1,0:T(8,128)(2,1)S(1)} %get-tuple-element.33), channel_id=1, source_target_pairs={{0,24},{8,16},{16,8},{24,0},{1,25},{9,17},{17,9},{25,1},{2,26},{10... | collective-permute-start | bytes 1572872 | tf_op jit(solution)/shard_map/ppermute | solution.py:62
  95.3 19.5 %collective-permute-start.14 = (bf16[4,512,128]{2,1,0:T(8,128)(2,1)S(1)}, bf16[4,512,128]{2,1,0:T(8,128)(2,1)S(1)}, u32[]{:S(2)}, u32[]{:S(2)}) collective-permute-start(bf16[4,512,128]{2,1,0:T(8,128)(2,1)S(1)} %get-tuple-element.37), channel_id=1, source_target_pairs={{0,448},{64,128},{128,64},{192,256},{256,192},{320,384},{384,320},... | collective-permute-start | bytes 1572872 | tf_op jit(solution)/shard_map/ppermute | solution.py:62
  109.4 21.5 %all-to-all-start.1 = ((bf16[8,256,128]{2,1,0:T(8,128)(2,1)}), bf16[8,256,128]{2,1,0:T(8,128)(2,1)S(1)}, u32[]{:S(2)}, u32[]{:S(2)}) async-start(bf16[8,256,128]{2,1,0:T(8,128)(2,1)} %shard_map.96), calls=%async_computation.1 | async-start | bytes 1048576 | tf_op jit(solution)/shard_map/all_to_all | solution.py:299
  114.9 8.3 %collective-permute-start.15 = (bf16[2,512,128]{2,1,0:T(8,128)(2,1)S(1)}, bf16[2,512,128]{2,1,0:T(8,128)(2,1)S(1)}, u32[]{:S(2)}, u32[]{:S(2)}) collective-permute-start(bf16[2,512,128]{2,1,0:T(8,128)(2,1)S(1)} %get-tuple-element.39), channel_id=1, source_target_pairs={{0,64},{64,0},{128,192},{192,128},{256,320},{320,256},{384,448},{4... | collective-permute-start | bytes 786440 | tf_op jit(solution)/shard_map/ppermute | solution.py:62
  123.3 12.2 %collective-permute-start.16 = (bf16[1,512,128]{2,1,0:T(8,128)(2,1)S(1)}, bf16[1,512,128]{2,1,0:T(8,128)(2,1)S(1)}, u32[]{:S(2)}, u32[]{:S(2)}) collective-permute-start(bf16[1,512,128]{2,1,0:T(8,128)(2,1)S(1)} %get-tuple-element.41), channel_id=1, source_target_pairs={{0,256},{64,320},{128,384},{192,448},{256,0},{320,64},{384,128},{4... | collective-permute-start | bytes 393224 | tf_op jit(solution)/shard_map/ppermute | solution.py:62
  131.0 4.5 %copy-start.2 = (s32[2,4]{1,0:T(2,128)S(1)}, s32[2,4]{1,0:T(2,128)}, u32[]{:S(2)}) copy-start(s32[2,4]{1,0:T(2,128)} %um_ref.3) | copy-start | bytes 100
  131.7 3.8 %copy-start.1 = (s32[2,4]{1,0:T(2,128)S(1)}, s32[2,4]{1,0:T(2,128)}, u32[]{:S(2)}) copy-start(s32[2,4]{1,0:T(2,128)} %gm_ref.3) | copy-start | bytes 100

commit v5 on v4

--- a/solution.py
+++ b/solution.py
@@ -16,7 +16,7 @@
 HBM = pl.BlockSpec(memory_space=pltpu.HBM)
 
 
-def call(kernel, outs, in_specs, scratch=(), out_spec=VMEM, limit=40):
+def call(kernel, outs, in_specs, scratch=(), out_spec=VMEM, limit=24):
     return pl.pallas_call(
         kernel,
         out_shape=outs,
@@ -108,8 +108,8 @@
 
 
 def main_kernel(blocks, me_ref, own, r1, r2, oa, ob, w0, w1, w2, w3, cot_ref, *rest):
-    hid_ref, keep_ref, send_ref, t0, t1, t2, ta, tb = rest[:8]
-    x_ref, w_ref, at_vec, at_ref, idx_ref, acc, g_ref, gt, sem = rest[8:]
+    hid_ref, keep_ref, send_ref, t_ref = rest[:4]
+    x_ref, w_ref, at_vec, at_ref, idx_ref, acc, g_ref, gt, sem = rest[4:]
     count = w0.shape[0]
     for g, part in enumerate((w0, w1, w2, w3)):
         for i in range(count):
@@ -165,23 +165,22 @@
                 out_ref[j, pl.ds(s * BLK, BLK), :] = jnp.dot(
                     gt[a], x_ref[2 * n + p // blocks], preferred_element_type=F32
                 ).astype(BF)
-    for part, x, z in ((ta, far, 0), (tb, far, half), (t1, one, 0), (t2, two, 0), (t0, my_x, 0)):
-        for i in range(part.shape[0] // 2):
-            n = x * (zs // 2) + z // 2 + i
-            sums = [None, None]
-            for s in range(SLOTS):
-                p = idx_ref[n, s]
-                prod = lax.dot_general(
-                    g_ref[p % blocks + (s // 2) * blocks],
-                    w_ref[n, pl.ds(s * BLK, BLK), :],
-                    (((1,), (1,)), ((), ())),
-                    preferred_element_type=F32,
-                )
-                for r in range(2):
-                    add = jnp.where(p // blocks == r, prod, 0.0)
-                    sums[r] = add if sums[r] is None else sums[r] + add
+    for n in range(shards):
+        sums = [None, None]
+        for s in range(SLOTS):
+            p = idx_ref[n, s]
+            prod = lax.dot_general(
+                g_ref[p % blocks + (s // 2) * blocks],
+                w_ref[n, pl.ds(s * BLK, BLK), :],
+                (((1,), (1,)), ((), ())),
+                preferred_element_type=F32,
+            )
             for r in range(2):
-                part[2 * i + r] = sums[r].astype(BF)
+                add = jnp.where(p // blocks == r, prod, 0.0)
+                sums[r] = add if sums[r] is None else sums[r] + add
+        for r in range(2):
+            k = 2 * n + r
+            t_ref[k // zs, k % zs] = sums[r].astype(BF)
 
 
 def total(parts):
@@ -198,18 +197,9 @@
         hi_ref[i] = total([a_ref[half + i], b_ref[half + i]]).astype(BF)
 
 
-def forward_kernel(t1, t2, ra, rb, o1, o2):
-    half = ra.shape[0]
-    for i in range(half):
-        o1[i] = total([t1[i], ra[i]]).astype(BF)
-        o1[half + i] = t1[half + i]
-        o2[i] = t2[i]
-        o2[half + i] = total([t2[half + i], rb[i]]).astype(BF)
-
-
-def middle_kernel(t0, r1, r2, out_ref):
-    for i in range(out_ref.shape[0]):
-        out_ref[i] = total([t0[i], r1[i], r2[i]]).astype(BF)
+def middle_kernel(t_ref, _, out_ref):
+    for z in range(out_ref.shape[0]):
+        out_ref[z] = total([t_ref[x, z] for x in range(t_ref.shape[0])]).astype(BF)
 
 
 def last_kernel(a_ref, out_ref):
@@ -260,18 +250,13 @@
     w = [w, w_late, swap(w, "c", "one"), swap(w_late, "c", "one")]
     oa, ob = swap(r1[:half], "x", "two"), swap(r2[half:], "x", "one")
 
-    whole, piece = shape((zs, tok, BLK), BF), shape((half, tok, BLK), BF)
-    hidden, keep, send, t0, t1, t2, ta, tb = call(
+    hidden, keep, send, terms = call(
         lambda *refs: main_kernel(blocks, *refs),
         (
             shape((tok, width), BF),
             shape((ys, META, BLK), BF),
             shape((ys, META, BLK), BF),
-            whole,
-            whole,
-            whole,
-            piece,
-            piece,
+            shape((xs, zs, tok, BLK), BF),
         ),
         [SMEM] + [VMEM] * 10,
         [
@@ -287,15 +272,13 @@
         ],
     )(me, own, r1, r2, oa, ob, *w, cotangent)
     other = swap(send, "c", "one")
-    ra, rb = swap(ta, "x", "two"), swap(tb, "x", "one")
+    terms = lax.all_to_all(terms, "x", 0, 0)
     lo = keep
     for stage in reversed(stages(ys)):
         part = shape((lo.shape[0] // 2, *lo.shape[1:]), BF)
         lo, hi = call(halves_kernel, (part, part), [VMEM] * 2)(lo, other)
         other = swap(hi, "y", stage)
-    t1, t2 = call(forward_kernel, (whole, whole), [VMEM] * 4)(t1, t2, ra, rb)
-    r1, r2 = swap(t1, "x", "one"), swap(t2, "x", "two")
-    own = call(middle_kernel, whole, [VMEM] * 3)(t0, r1, r2)
+    own = call(middle_kernel, shape(own.shape, BF), [VMEM, HBM])(terms, lo)
     own = lax.all_to_all(own, "z", 0, 0)
     grad_tokens = call(last_kernel, shape(tokens.shape, BF), [VMEM])(own)
     grad_gate, grad_up = call(

time: 138 us -> 138 us (level)
  the two profiles are of different devices: /device:TPU:16 before, /device:TPU:2 now
where the time goes in v5:
time: 138 us; the launch traced here: 137 us
  starting transfers between devices  63.2 us (46%)
  waiting for transfers between devices  50 us (36%)
  Pallas kernels  15 us (11%)
  local copies, waits for them, and re-layouts  5.71 us (4%)
  other arithmetic  1.97 us (1%)
    ppermute x13, waiting for transfers between devices, swap(): lax.ppermute(x, axis, [(i, turn(i, stage, size)) for i in range(size)])  44.4 us
    ppermute x13, starting transfers between devices, swap(): lax.ppermute(x, axis, [(i, turn(i, stage, size)) for i in range(size)])  42 us
    all_to_all x2, starting transfers between devices, body(): own = lax.all_to_all(own, 'z', 0, 0)  15.9 us
    pallas_call x1, Pallas kernels, body(): call(lambda *refs: main_kernel(blocks, *refs), (shape((tok, width), BF),...  7.25 us
    all_to_all x2, waiting for transfers between devices, body(): own = lax.all_to_all(own, 'z', 0, 0)  5.6 us
    all_to_all x1, starting transfers between devices, body(): terms = lax.all_to_all(terms, 'x', 0, 0)  5.33 us
    unnamed x16, local copies, waits for them, and re-layouts  4.27 us
  transfers between devices with their start and end apart: 16, of which 9 were waited for; matrix products, arithmetic and copies ran while one was open for 2% of the time, Pallas kernels for 2%

profile of v5, /device:TPU:2, one launch (start us, length us, event | category | flops | bytes accessed | tf_op | source)
XLA Modules:
  0.0 136.7 jit_solution(3671589483649188060)
XLA Ops:
  0.6 0.0 copy-start.5
  0.6 2.6 %shard_map.93 = (bf16[528,128]{1,0:T(8,128)(2,1)}, bf16[8,256,128]{2,1,0:T(8,128)(2,1)}) custom-call(s32[2,4]{1,0:T(2,128)} %gm_ref.3, s32[2,4]{1,0:T(2,128)} %um_ref.3, bf16[256,128]{1,0:T(8,128)(2,1)} %tok_ref.1, bf16[256,512]{1,0:T(8,128)(2,1)} %gw_ref.1, bf16[256,512]{1,0:T(8,128)(2,1)} %uw_ref.1), custom_call_target="tpu_custom_call" | custom-call | tf_op jit(solution)/shard_map/pallas_call | solution.py:232
  3.2 7.7 %collective-permute-start.4 = (bf16[1,528,128]{2,1,0:T(8,128)(2,1)}, bf16[1,528,128]{2,1,0:T(8,128)(2,1)S(1)}, u32[]{:S(2)}, u32[]{:S(2)}) collective-permute-start(bf16[1,528,128]{2,1,0:T(8,128)(2,1)} %bitcast.4), channel_id=1, source_target_pairs={{0,256},{64,320},{128,384},{192,448},{256,0},{320,64},{384,128},{4... | collective-permute-start | bytes 405512 | tf_op jit(solution)/shard_map/ppermute | solution.py:62
  11.0 10.3 %all-to-all-start = ((bf16[8,256,128]{2,1,0:T(8,128)(2,1)}), bf16[8,256,128]{2,1,0:T(8,128)(2,1)S(1)}, u32[]{:S(2)}, u32[]{:S(2)}) async-start(bf16[8,256,128]{2,1,0:T(8,128)(2,1)} %get-tuple-element.18), calls=%async_computation | async-start | bytes 1048576 | tf_op jit(solution)/shard_map/all_to_all | solution.py:243
  21.3 0.0 collective-permute-done.4
  21.3 0.9 pad_maximum_fusion.1
  22.3 2.6 %collective-permute-start.5 = (bf16[2,528,128]{2,1,0:T(8,128)(2,1)S(1)}, bf16[2,528,128]{2,1,0:T(8,128)(2,1)S(1)}, u32[]{:S(2)}, u32[]{:S(2)}) collective-permute-start(bf16[2,528,128]{2,1,0:T(8,128)(2,1)S(1)} %pad_maximum_fusion.1), channel_id=1, source_target_pairs={{0,64},{64,0},{128,192},{192,128},{256,320},{320,256},{384,448},{4... | collective-permute-start | bytes 811016 | tf_op jit(solution)/shard_map/ppermute | solution.py:62
  24.9 6.9 %collective-permute-done.5 = bf16[2,528,128]{2,1,0:T(8,128)(2,1)S(1)} collective-permute-done((bf16[2,528,128]{2,1,0:T(8,128)(2,1)S(1)}, bf16[2,528,128]{2,1,0:T(8,128)(2,1)S(1)}, u32[]{:S(2)}, u32[]{:S(2)}) %collective-permute-start.5) | collective-permute-done | bytes 270368 | tf_op jit(solution)/shard_map/ppermute | solution.py:62
  31.8 1.0 pad_maximum_fusion.refs_6_
  32.8 2.4 %collective-permute-start.6 = (bf16[4,528,128]{2,1,0:T(8,128)(2,1)S(1)}, bf16[4,528,128]{2,1,0:T(8,128)(2,1)S(1)}, u32[]{:S(2)}, u32[]{:S(2)}) collective-permute-start(bf16[4,528,128]{2,1,0:T(8,128)(2,1)S(1)} %pad_maximum_fusion.refs_6_), channel_id=1, source_target_pairs={{0,448},{64,128},{128,64},{192,256},{256,192},{320,384},{384,320},... | collective-permute-start | bytes 1622024 | tf_op jit(solution)/shard_map/ppermute | solution.py:62
  35.1 3.4 %all-to-all-done.refs_1_ = bf16[8,256,128]{2,1,0:T(8,128)(2,1)S(1)} async-done(((bf16[8,256,128]{2,1,0:T(8,128)(2,1)}), bf16[8,256,128]{2,1,0:T(8,128)(2,1)S(1)}, u32[]{:S(2)}, u32[]{:S(2)}) %all-to-all-start) | async-done | bytes 524320 | tf_op jit(solution)/shard_map/all_to_all | solution.py:243
  38.5 3.4 %collective-permute-start.1 = (bf16[8,256,128]{2,1,0:T(8,128)(2,1)S(1)}, bf16[8,256,128]{2,1,0:T(8,128)(2,1)S(1)}, u32[]{:S(2)}, u32[]{:S(2)}) collective-permute-start(bf16[8,256,128]{2,1,0:T(8,128)(2,1)S(1)} %all-to-all-done.refs_1_), channel_id=1, source_target_pairs={{0,24},{8,16},{16,8},{24,0},{1,25},{9,17},{17,9},{25,1},{2,26},{10... | collective-permute-start | bytes 1572872 | tf_op jit(solution)/shard_map/ppermute | solution.py:62
  42.0 3.7 %collective-permute-start = (bf16[8,256,128]{2,1,0:T(8,128)(2,1)S(1)}, bf16[8,256,128]{2,1,0:T(8,128)(2,1)S(1)}, u32[]{:S(2)}, u32[]{:S(2)}) collective-permute-start(bf16[8,256,128]{2,1,0:T(8,128)(2,1)S(1)} %all-to-all-done.refs_1_), channel_id=1, source_target_pairs={{0,8},{8,0},{16,24},{24,16},{1,9},{9,1},{17,25},{25,17},{2,10},{10... | collective-permute-start | bytes 1572872 | tf_op jit(solution)/shard_map/ppermute | solution.py:62
  45.7 1.9 %collective-permute-start.7 = (bf16[4,528,128]{2,1,0:T(8,128)(2,1)S(1)}, bf16[4,528,128]{2,1,0:T(8,128)(2,1)S(1)}, u32[]{:S(2)}, u32[]{:S(2)}) collective-permute-start(bf16[4,528,128]{2,1,0:T(8,128)(2,1)S(1)} %pad_maximum_fusion.refs_6_), channel_id=1, source_target_pairs={{0,32},{32,0},{1,33},{33,1},{2,34},{34,2},{3,35},{35,3},{4,36},{36... | collective-permute-start | bytes 1622024 | tf_op jit(solution)/shard_map/ppermute | solution.py:62
  47.6 0.8 collective-permute-done.6.refs_7_
  48.4 0.0 copy-start.1
  48.4 1.9 %collective-permute-start.8 = (bf16[4,528,128]{2,1,0:T(8,128)(2,1)S(1)}, bf16[4,528,128]{2,1,0:T(8,128)(2,1)}, u32[]{:S(2)}, u32[]{:S(2)}) collective-permute-start(bf16[4,528,128]{2,1,0:T(8,128)(2,1)S(1)} %collective-permute-done.6.refs_7_), channel_id=1, source_target_pairs={{0,32},{32,0},{1,33},{33,1},{2,34},{34,2},{3,35},{35,3},{4,36},{36... | collective-permute-start | bytes 1622024 | tf_op jit(solution)/shard_map/ppermute | solution.py:62
  50.3 3.0 %collective-permute-done.1.refs_3_ = bf16[8,256,128]{2,1,0:T(8,128)(2,1)S(1)} collective-permute-done((bf16[8,256,128]{2,1,0:T(8,128)(2,1)S(1)}, bf16[8,256,128]{2,1,0:T(8,128)(2,1)S(1)}, u32[]{:S(2)}, u32[]{:S(2)}) %collective-permute-start.1) | collective-permute-done | bytes 524320 | tf_op jit(solution)/shard_map/ppermute | solution.py:62
  53.3 0.7 slice.9
  54.1 3.7 %collective-permute-start.3 = (bf16[4,256,128]{2,1,0:T(8,128)(2,1)}, bf16[4,256,128]{2,1,0:T(8,128)(2,1)}, u32[]{:S(2)}, u32[]{:S(2)}) collective-permute-start(bf16[4,256,128]{2,1,0:T(8,128)(2,1)} %slice.9), channel_id=1, source_target_pairs={{0,8},{8,0},{16,24},{24,16},{1,9},{9,1},{17,25},{25,17},{2,10},{10... | collective-permute-start | bytes 786440 | tf_op jit(solution)/shard_map/ppermute | solution.py:62
  57.7 0.0 collective-permute-done.refs_2_
  57.7 0.7 slice.8
  58.4 4.1 %collective-permute-start.2 = (bf16[4,256,128]{2,1,0:T(8,128)(2,1)}, bf16[4,256,128]{2,1,0:T(8,128)(2,1)}, u32[]{:S(2)}, u32[]{:S(2)}) collective-permute-start(bf16[4,256,128]{2,1,0:T(8,128)(2,1)} %slice.8), channel_id=1, source_target_pairs={{0,24},{8,16},{16,8},{24,0},{1,25},{9,17},{17,9},{25,1},{2,26},{10... | collective-permute-start | bytes 786440 | tf_op jit(solution)/shard_map/ppermute | solution.py:62
  62.6 0.1 pad_add_fusion.refs_0_
  62.7 0.0 collective-permute-done.7.refs_8_
  62.7 0.0 copy-start.3
  62.7 0.8 copy-done.3
  63.5 0.0 collective-permute-done.8.refs_9_
  63.5 0.0 collective-permute-done.3.refs_5_
  63.5 0.0 copy-done.1
  63.5 3.8 %collective-permute-done.2.refs_4_ = bf16[4,256,128]{2,1,0:T(8,128)(2,1)} collective-permute-done((bf16[4,256,128]{2,1,0:T(8,128)(2,1)}, bf16[4,256,128]{2,1,0:T(8,128)(2,1)}, u32[]{:S(2)}, u32[]{:S(2)}) %collective-permute-start.2) | collective-permute-done | bytes 262176 | tf_op jit(solution)/shard_map/ppermute | solution.py:62
  67.2 0.0 copy-done.5
  67.3 0.0 copy-start.2
  67.3 1.0 copy-done.2
  68.3 0.0 copy-start.4
  68.3 1.0 copy-done.4
  69.3 7.3 %shard_map.94 = (bf16[256,512]{1,0:T(8,128)(2,1)}, bf16[8,512,128]{2,1,0:T(8,128)(2,1)S(1)}, bf16[8,512,128]{2,1,0:T(8,128)(2,1)}, bf16[4,8,256,128]{3,2,1,0:T(8,128)(2,1)S(1)}) custom-call(s32[3]{0:T(128)S(1)} %pad_add_fusion.refs_0_, bf16[8,256,128]{2,1,0:T(8,128)(2,1)S(1)} %all-to-all-done.refs_1_, bf16[8,256,128]{2,1,0:T(8,128)(2,1)S(1)} %collective-permute-done.refs_2_, ...), custom_call_target="tpu_custom_call" | custom-call | tf_op jit(solution)/shard_map/pallas_call | solution.py:253
  76.6 0.0 copy-start
  76.6 1.4 copy-done
  78.0 1.9 %collective-permute-start.9 = (bf16[8,512,128]{2,1,0:T(8,128)(2,1)}, bf16[8,512,128]{2,1,0:T(8,128)(2,1)}, u32[]{:S(2)}, u32[]{:S(2)}) collective-permute-start(bf16[8,512,128]{2,1,0:T(8,128)(2,1)} %get-tuple-element.23), channel_id=1, source_target_pairs={{0,32},{32,0},{1,33},{33,1},{2,34},{34,2},{3,35},{35,3},{4,36},{36... | collective-permute-start | bytes 3145736 | tf_op jit(solution)/shard_map/ppermute | solution.py:62
  79.9 5.3 %all-to-all-start.1 = ((bf16[4,8,256,128]{3,2,1,0:T(8,128)(2,1)}), bf16[4,8,256,128]{3,2,1,0:T(8,128)(2,1)S(1)}, u32[]{:S(2)}, u32[]{:S(2)}) async-start(bf16[4,8,256,128]{3,2,1,0:T(8,128)(2,1)} %copy-done), calls=%async_computation.1 | async-start | bytes 4194304 | tf_op jit(solution)/shard_map/all_to_all | solution.py:275
  85.2 0.0 collective-permute-done.9.b_ref
  85.2 1.5 %shard_map.95 = (bf16[4,512,128]{2,1,0:T(8,128)(2,1)S(1)}, bf16[4,512,128]{2,1,0:T(8,128)(2,1)S(1)}) custom-call(bf16[8,512,128]{2,1,0:T(8,128)(2,1)S(1)} %get-tuple-element.22.a_ref, bf16[8,512,128]{2,1,0:T(8,128)(2,1)} %collective-permute-done.9.b_ref), custom_call_target="tpu_custom_call" | custom-call | tf_op jit(solution)/shard_map/pallas_call | solution.py:279
  86.7 2.3 %collective-permute-start.10 = (bf16[4,512,128]{2,1,0:T(8,128)(2,1)S(1)}, bf16[4,512,128]{2,1,0:T(8,128)(2,1)S(1)}, u32[]{:S(2)}, u32[]{:S(2)}) collective-permute-start(bf16[4,512,128]{2,1,0:T(8,128)(2,1)S(1)} %get-tuple-element.25), channel_id=1, source_target_pairs={{0,448},{64,128},{128,64},{192,256},{256,192},{320,384},{384,320},... | collective-permute-start | bytes 1572872 | tf_op jit(solution)/shard_map/ppermute | solution.py:62
  89.0 14.7 %collective-permute-done.10.b_ref = bf16[4,512,128]{2,1,0:T(8,128)(2,1)S(1)} collective-permute-done((bf16[4,512,128]{2,1,0:T(8,128)(2,1)S(1)}, bf16[4,512,128]{2,1,0:T(8,128)(2,1)S(1)}, u32[]{:S(2)}, u32[]{:S(2)}) %collective-permute-start.10) | collective-permute-done | bytes 524320 | tf_op jit(solution)/shard_map/ppermute | solution.py:62
  103.7 0.1 shard_map.96
  103.8 1.9 %collective-permute-start.11 = (bf16[2,512,128]{2,1,0:T(8,128)(2,1)S(1)}, bf16[2,512,128]{2,1,0:T(8,128)(2,1)S(1)}, u32[]{:S(2)}, u32[]{:S(2)}) collective-permute-start(bf16[2,512,128]{2,1,0:T(8,128)(2,1)S(1)} %get-tuple-element.27), channel_id=1, source_target_pairs={{0,64},{64,0},{128,192},{192,128},{256,320},{320,256},{384,448},{4... | collective-permute-start | bytes 786440 | tf_op jit(solution)/shard_map/ppermute | solution.py:62
  105.7 7.4 %collective-permute-done.11.b_ref = bf16[2,512,128]{2,1,0:T(8,128)(2,1)S(1)} collective-permute-done((bf16[2,512,128]{2,1,0:T(8,128)(2,1)S(1)}, bf16[2,512,128]{2,1,0:T(8,128)(2,1)S(1)}, u32[]{:S(2)}, u32[]{:S(2)}) %collective-permute-start.11) | collective-permute-done | bytes 262176 | tf_op jit(solution)/shard_map/ppermute | solution.py:62
  113.1 0.0 copy-start.6
  113.1 0.0 copy-start.7
  113.1 0.1 shard_map.97
  113.2 0.0 all-to-all-done.1.t_ref
  113.2 1.1 shard_map.98
  114.3 5.5 %all-to-all-start.2 = ((bf16[8,256,128]{2,1,0:T(8,128)(2,1)}), bf16[8,256,128]{2,1,0:T(8,128)(2,1)S(1)}, u32[]{:S(2)}, u32[]{:S(2)}) async-start(bf16[8,256,128]{2,1,0:T(8,128)(2,1)} %shard_map.98), calls=%async_computation.2 | async-start | bytes 1048576 | tf_op jit(solution)/shard_map/all_to_all | solution.py:282
  119.8 4.4 %collective-permute-start.12 = (bf16[1,512,128]{2,1,0:T(8,128)(2,1)S(1)}, bf16[1,512,128]{2,1,0:T(8,128)(2,1)S(1)}, u32[]{:S(2)}, u32[]{:S(2)}) collective-permute-start(bf16[1,512,128]{2,1,0:T(8,128)(2,1)S(1)} %get-tuple-element.29), channel_id=1, source_target_pairs={{0,256},{64,320},{128,384},{192,448},{256,0},{320,64},{384,128},{4... | collective-permute-start | bytes 393224 | tf_op jit(solution)/shard_map/ppermute | solution.py:62
  124.3 7.8 %collective-permute-done.12.b_ref = bf16[1,512,128]{2,1,0:T(8,128)(2,1)S(1)} collective-permute-done((bf16[1,512,128]{2,1,0:T(8,128)(2,1)S(1)}, bf16[1,512,128]{2,1,0:T(8,128)(2,1)S(1)}, u32[]{:S(2)}, u32[]{:S(2)}) %collective-permute-start.12) | collective-permute-done | bytes 131104 | tf_op jit(solution)/shard_map/ppermute | solution.py:62
  132.0 0.0 copy-done.6
  132.0 0.0 copy-done.7
  132.1 1.7 %shard_map.100 = (bf16[256,512]{1,0:T(8,128)(2,1)}, bf16[256,512]{1,0:T(8,128)(2,1)}) custom-call(s32[2,4]{1,0:T(2,128)S(1)} %copy-done.6, s32[2,4]{1,0:T(2,128)S(1)} %copy-done.7, bf16[1,512,128]{2,1,0:T(8,128)(2,1)S(1)} %get-tuple-element.28._.a_ref, bf16[1,512,128]{2,1,0:T(8,128)(2,1)S(1)} %collective-permute-done.12.b_ref), custom_call_target="tpu_custom_call" | custom-call | tf_op jit(solution)/shard_map/pallas_call | solution.py:284
  133.7 2.2 %all-to-all-done.2.a_ref = bf16[8,256,128]{2,1,0:T(8,128)(2,1)S(1)} async-done(((bf16[8,256,128]{2,1,0:T(8,128)(2,1)}), bf16[8,256,128]{2,1,0:T(8,128)(2,1)S(1)}, u32[]{:S(2)}, u32[]{:S(2)}) %all-to-all-start.2) | async-done | bytes 524320 | tf_op jit(solution)/shard_map/all_to_all | solution.py:282
  136.0 0.7 shard_map.99
Async XLA Ops:
  0.6 66.6 %copy-start.5 = (bf16[256,512]{1,0:T(8,128)(2,1)S(1)}, bf16[256,512]{1,0:T(8,128)(2,1)}, u32[]{:S(2)}) copy-start(bf16[256,512]{1,0:T(8,128)(2,1)} %refs_10_.1) | copy-start | bytes 786436
  3.2 18.1 %collective-permute-start.4 = (bf16[1,528,128]{2,1,0:T(8,128)(2,1)}, bf16[1,528,128]{2,1,0:T(8,128)(2,1)S(1)}, u32[]{:S(2)}, u32[]{:S(2)}) collective-permute-start(bf16[1,528,128]{2,1,0:T(8,128)(2,1)} %bitcast.4), channel_id=1, source_target_pairs={{0,256},{64,320},{128,384},{192,448},{256,0},{320,64},{384,128},{4... | collective-permute-start | bytes 405512 | tf_op jit(solution)/shard_map/ppermute | solution.py:62
  11.0 27.5 %all-to-all-start = ((bf16[8,256,128]{2,1,0:T(8,128)(2,1)}), bf16[8,256,128]{2,1,0:T(8,128)(2,1)S(1)}, u32[]{:S(2)}, u32[]{:S(2)}) async-start(bf16[8,256,128]{2,1,0:T(8,128)(2,1)} %get-tuple-element.18), calls=%async_computation | async-start | bytes 1048576 | tf_op jit(solution)/shard_map/all_to_all | solution.py:243
  22.3 9.6 %collective-permute-start.5 = (bf16[2,528,128]{2,1,0:T(8,128)(2,1)S(1)}, bf16[2,528,128]{2,1,0:T(8,128)(2,1)S(1)}, u32[]{:S(2)}, u32[]{:S(2)}) collective-permute-start(bf16[2,528,128]{2,1,0:T(8,128)(2,1)S(1)} %pad_maximum_fusion.1), channel_id=1, source_target_pairs={{0,64},{64,0},{128,192},{192,128},{256,320},{320,256},{384,448},{4... | collective-permute-start | bytes 811016 | tf_op jit(solution)/shard_map/ppermute | solution.py:62
  32.8 15.6 %collective-permute-start.6 = (bf16[4,528,128]{2,1,0:T(8,128)(2,1)S(1)}, bf16[4,528,128]{2,1,0:T(8,128)(2,1)S(1)}, u32[]{:S(2)}, u32[]{:S(2)}) collective-permute-start(bf16[4,528,128]{2,1,0:T(8,128)(2,1)S(1)} %pad_maximum_fusion.refs_6_), channel_id=1, source_target_pairs={{0,448},{64,128},{128,64},{192,256},{256,192},{320,384},{384,320},... | collective-permute-start | bytes 1622024 | tf_op jit(solution)/shard_map/ppermute | solution.py:62
  38.5 14.8 %collective-permute-start.1 = (bf16[8,256,128]{2,1,0:T(8,128)(2,1)S(1)}, bf16[8,256,128]{2,1,0:T(8,128)(2,1)S(1)}, u32[]{:S(2)}, u32[]{:S(2)}) collective-permute-start(bf16[8,256,128]{2,1,0:T(8,128)(2,1)S(1)} %all-to-all-done.refs_1_), channel_id=1, source_target_pairs={{0,24},{8,16},{16,8},{24,0},{1,25},{9,17},{17,9},{25,1},{2,26},{10... | collective-permute-start | bytes 1572872 | tf_op jit(solution)/shard_map/ppermute | solution.py:62
  42.0 15.7 %collective-permute-start = (bf16[8,256,128]{2,1,0:T(8,128)(2,1)S(1)}, bf16[8,256,128]{2,1,0:T(8,128)(2,1)S(1)}, u32[]{:S(2)}, u32[]{:S(2)}) collective-permute-start(bf16[8,256,128]{2,1,0:T(8,128)(2,1)S(1)} %all-to-all-done.refs_1_), channel_id=1, source_target_pairs={{0,8},{8,0},{16,24},{24,16},{1,9},{9,1},{17,25},{25,17},{2,10},{10... | collective-permute-start | bytes 1572872 | tf_op jit(solution)/shard_map/ppermute | solution.py:62
  45.7 17.0 %collective-permute-start.7 = (bf16[4,528,128]{2,1,0:T(8,128)(2,1)S(1)}, bf16[4,528,128]{2,1,0:T(8,128)(2,1)S(1)}, u32[]{:S(2)}, u32[]{:S(2)}) collective-permute-start(bf16[4,528,128]{2,1,0:T(8,128)(2,1)S(1)} %pad_maximum_fusion.refs_6_), channel_id=1, source_target_pairs={{0,32},{32,0},{1,33},{33,1},{2,34},{34,2},{3,35},{35,3},{4,36},{36... | collective-permute-start | bytes 1622024 | tf_op jit(solution)/shard_map/ppermute | solution.py:62
  48.4 15.1 %copy-start.1 = (bf16[4,528,128]{2,1,0:T(8,128)(2,1)}, bf16[4,528,128]{2,1,0:T(8,128)(2,1)S(1)}, u32[]{:S(2)}) copy-start(bf16[4,528,128]{2,1,0:T(8,128)(2,1)S(1)} %collective-permute-done.6.refs_7_) | copy-start | bytes 1622020
  48.4 15.1 %collective-permute-start.8 = (bf16[4,528,128]{2,1,0:T(8,128)(2,1)S(1)}, bf16[4,528,128]{2,1,0:T(8,128)(2,1)}, u32[]{:S(2)}, u32[]{:S(2)}) collective-permute-start(bf16[4,528,128]{2,1,0:T(8,128)(2,1)S(1)} %collective-permute-done.6.refs_7_), channel_id=1, source_target_pairs={{0,32},{32,0},{1,33},{33,1},{2,34},{34,2},{3,35},{35,3},{4,36},{36... | collective-permute-start | bytes 1622024 | tf_op jit(solution)/shard_map/ppermute | solution.py:62
  54.1 9.4 %collective-permute-start.3 = (bf16[4,256,128]{2,1,0:T(8,128)(2,1)}, bf16[4,256,128]{2,1,0:T(8,128)(2,1)}, u32[]{:S(2)}, u32[]{:S(2)}) collective-permute-start(bf16[4,256,128]{2,1,0:T(8,128)(2,1)} %slice.9), channel_id=1, source_target_pairs={{0,8},{8,0},{16,24},{24,16},{1,9},{9,1},{17,25},{25,17},{2,10},{10... | collective-permute-start | bytes 786440 | tf_op jit(solution)/shard_map/ppermute | solution.py:62
  58.4 8.8 %collective-permute-start.2 = (bf16[4,256,128]{2,1,0:T(8,128)(2,1)}, bf16[4,256,128]{2,1,0:T(8,128)(2,1)}, u32[]{:S(2)}, u32[]{:S(2)}) collective-permute-start(bf16[4,256,128]{2,1,0:T(8,128)(2,1)} %slice.8), channel_id=1, source_target_pairs={{0,24},{8,16},{16,8},{24,0},{1,25},{9,17},{17,9},{25,1},{2,26},{10... | collective-permute-start | bytes 786440 | tf_op jit(solution)/shard_map/ppermute | solution.py:62
  62.7 0.8 copy-start.3
  67.3 1.0 copy-start.2
  68.3 1.0 copy-start.4
  76.6 1.4 copy-start
  78.0 7.3 %collective-permute-start.9 = (bf16[8,512,128]{2,1,0:T(8,128)(2,1)}, bf16[8,512,128]{2,1,0:T(8,128)(2,1)}, u32[]{:S(2)}, u32[]{:S(2)}) collective-permute-start(bf16[8,512,128]{2,1,0:T(8,128)(2,1)} %get-tuple-element.23), channel_id=1, source_target_pairs={{0,32},{32,0},{1,33},{33,1},{2,34},{34,2},{3,35},{35,3},{4,36},{36... | collective-permute-start | bytes 3145736 | tf_op jit(solution)/shard_map/ppermute | solution.py:62
  79.9 33.3 %all-to-all-start.1 = ((bf16[4,8,256,128]{3,2,1,0:T(8,128)(2,1)}), bf16[4,8,256,128]{3,2,1,0:T(8,128)(2,1)S(1)}, u32[]{:S(2)}, u32[]{:S(2)}) async-start(bf16[4,8,256,128]{3,2,1,0:T(8,128)(2,1)} %copy-done), calls=%async_computation.1 | async-start | bytes 4194304 | tf_op jit(solution)/shard_map/all_to_all | solution.py:275
  86.7 17.0 %collective-permute-start.10 = (bf16[4,512,128]{2,1,0:T(8,128)(2,1)S(1)}, bf16[4,512,128]{2,1,0:T(8,128)(2,1)S(1)}, u32[]{:S(2)}, u32[]{:S(2)}) collective-permute-start(bf16[4,512,128]{2,1,0:T(8,128)(2,1)S(1)} %get-tuple-element.25), channel_id=1, source_target_pairs={{0,448},{64,128},{128,64},{192,256},{256,192},{320,384},{384,320},... | collective-permute-start | bytes 1572872 | tf_op jit(solution)/shard_map/ppermute | solution.py:62
  103.8 9.3 %collective-permute-start.11 = (bf16[2,512,128]{2,1,0:T(8,128)(2,1)S(1)}, bf16[2,512,128]{2,1,0:T(8,128)(2,1)S(1)}, u32[]{:S(2)}, u32[]{:S(2)}) collective-permute-start(bf16[2,512,128]{2,1,0:T(8,128)(2,1)S(1)} %get-tuple-element.27), channel_id=1, source_target_pairs={{0,64},{64,0},{128,192},{192,128},{256,320},{320,256},{384,448},{4... | collective-permute-start | bytes 786440 | tf_op jit(solution)/shard_map/ppermute | solution.py:62
  113.1 18.9 %copy-start.6 = (s32[2,4]{1,0:T(2,128)S(1)}, s32[2,4]{1,0:T(2,128)}, u32[]{:S(2)}) copy-start(s32[2,4]{1,0:T(2,128)} %gm_ref.3) | copy-start | bytes 100
  113.1 18.9 %copy-start.7 = (s32[2,4]{1,0:T(2,128)S(1)}, s32[2,4]{1,0:T(2,128)}, u32[]{:S(2)}) copy-start(s32[2,4]{1,0:T(2,128)} %um_ref.3) | copy-start | bytes 100
  114.3 21.7 %all-to-all-start.2 = ((bf16[8,256,128]{2,1,0:T(8,128)(2,1)}), bf16[8,256,128]{2,1,0:T(8,128)(2,1)S(1)}, u32[]{:S(2)}, u32[]{:S(2)}) async-start(bf16[8,256,128]{2,1,0:T(8,128)(2,1)} %shard_map.98), calls=%async_computation.2 | async-start | bytes 1048576 | tf_op jit(solution)/shard_map/all_to_all | solution.py:282
  119.8 12.2 %collective-permute-start.12 = (bf16[1,512,128]{2,1,0:T(8,128)(2,1)S(1)}, bf16[1,512,128]{2,1,0:T(8,128)(2,1)S(1)}, u32[]{:S(2)}, u32[]{:S(2)}) collective-permute-start(bf16[1,512,128]{2,1,0:T(8,128)(2,1)S(1)} %get-tuple-element.29), channel_id=1, source_target_pairs={{0,256},{64,320},{128,384},{192,448},{256,0},{320,64},{384,128},{4... | collective-permute-start | bytes 393224 | tf_op jit(solution)/shard_map/ppermute | solution.py:62

commit v6 on v5

--- a/solution.py
+++ b/solution.py
@@ -16,7 +16,7 @@
 HBM = pl.BlockSpec(memory_space=pltpu.HBM)
 
 
-def call(kernel, outs, in_specs, scratch=(), out_spec=VMEM, limit=24):
+def call(kernel, outs, in_specs, scratch=(), out_spec=VMEM, limit=17):
     return pl.pallas_call(
         kernel,
         out_shape=outs,
@@ -57,13 +57,16 @@
     return (["far"] if size > 4 else []) + ["one", "two"]
 
 
+ORDERS = (["far", "one", "two"], ["far", "two", "one"])
+
+
 def swap(x, axis, stage):
     size = lax.axis_size(axis)
     return lax.ppermute(x, axis, [(i, turn(i, stage, size)) for i in range(size)])
 
 
-def origin(i, j, size):
-    for bit, stage in reversed(list(enumerate(stages(size)))):
+def origin(i, j, size, order=None):
+    for bit, stage in reversed(list(enumerate(order or stages(size)))):
         if j >> bit & 1:
             i = turn(i, stage, size)
     return i
@@ -157,12 +160,12 @@
         gt[c] = gg.T.astype(BF)
         gt[blocks + c] = gu.T.astype(BF)
     for out_ref, core in ((send_ref, 1 - my_c), (keep_ref, my_c)):
-        for j in range(ys):
-            n = 2 * origin(my_y, j, ys) + core
-            for s in range(SLOTS):
+        for t, order in enumerate(ORDERS):
+            for j, s in ((j, s) for j in range(ys) for s in (2 * t, 2 * t + 1)):
+                n = 2 * origin(my_y, j, ys, order) + core
                 p = idx_ref[n, s]
-                a = p % blocks + (s // 2) * blocks
-                out_ref[j, pl.ds(s * BLK, BLK), :] = jnp.dot(
+                a = p % blocks + t * blocks
+                out_ref[t, j, pl.ds((s - 2 * t) * BLK, BLK), :] = jnp.dot(
                     gt[a], x_ref[2 * n + p // blocks], preferred_element_type=F32
                 ).astype(BF)
     for n in range(shards):
@@ -190,11 +193,26 @@
     return out
 
 
-def halves_kernel(a_ref, b_ref, lo_ref, hi_ref):
+def halves(a_ref, b_ref, lo_ref, hi_ref):
     half = lo_ref.shape[0]
     for i in range(half):
         lo_ref[i] = total([a_ref[i], b_ref[i]]).astype(BF)
         hi_ref[i] = total([a_ref[half + i], b_ref[half + i]]).astype(BF)
+
+
+def first_kernel(keep, other, lo_g, hi_g, lo_u, hi_u):
+    halves(keep.at[0], other.at[0], lo_g, hi_g)
+    halves(keep.at[1], other.at[1], lo_u, hi_u)
+
+
+def second_kernel(g, from_g, u, from_u, lo_g, hi_g, lo_u, hi_u):
+    halves(g, from_g, lo_g, hi_g)
+    halves(u, from_u, lo_u, hi_u)
+
+
+def third_kernel(g, from_g, u, from_u, lo, hi):
+    halves(g, from_g, lo.at[pl.ds(0, 1)], hi.at[pl.ds(0, 1)])
+    halves(u, from_u, lo.at[pl.ds(1, 1)], hi.at[pl.ds(1, 1)])
 
 
 def middle_kernel(t_ref, _, out_ref):
@@ -216,8 +234,8 @@
             @pl.when(on)
             def _(p=p, s=s):
                 r, c = block_of(o_ref, p, cols)
-                rows = pl.ds((2 * t + s) * BLK, BLK)
-                block = total([a_ref[0, rows, :], b_ref[0, rows, :]])
+                rows = pl.ds(s * BLK, BLK)
+                block = total([a_ref[t, rows, :], b_ref[t, rows, :]])
                 o_ref[pl.ds(r, BLK), pl.ds(c, BLK)] = block.T.astype(BF)
 
 
@@ -254,8 +272,8 @@
         lambda *refs: main_kernel(blocks, *refs),
         (
             shape((tok, width), BF),
-            shape((ys, META, BLK), BF),
-            shape((ys, META, BLK), BF),
+            shape((2, ys, META // 2, BLK), BF),
+            shape((2, ys, META // 2, BLK), BF),
             shape((xs, zs, tok, BLK), BF),
         ),
         [SMEM] + [VMEM] * 10,
@@ -273,13 +291,17 @@
     )(me, own, r1, r2, oa, ob, *w, cotangent)
     other = swap(send, "c", "one")
     terms = lax.all_to_all(terms, "x", 0, 0)
-    lo = keep
-    for stage in reversed(stages(ys)):
-        part = shape((lo.shape[0] // 2, *lo.shape[1:]), BF)
-        lo, hi = call(halves_kernel, (part, part), [VMEM] * 2)(lo, other)
-        other = swap(hi, "y", stage)
-    own = call(middle_kernel, shape(own.shape, BF), [VMEM, HBM])(terms, lo)
+    part = shape((ys // 2, META // 2, BLK), BF)
+    g, hi_g, u, hi_u = call(first_kernel, (part,) * 4, [VMEM] * 2)(keep, other)
+    from_g, from_u = swap(hi_g, "y", "two"), swap(hi_u, "y", "one")
+    part = shape((ys // 4, META // 2, BLK), BF)
+    g, hi_g, u, hi_u = call(second_kernel, (part,) * 4, [VMEM] * 4)(g, from_g, u, from_u)
+    own = call(middle_kernel, shape(own.shape, BF), [VMEM, HBM])(terms, g)
     own = lax.all_to_all(own, "z", 0, 0)
+    from_g, from_u = swap(hi_g, "y", "one"), swap(hi_u, "y", "two")
+    part = shape((2, META // 2, BLK), BF)
+    lo, hi = call(third_kernel, (part,) * 2, [VMEM] * 4)(g, from_g, u, from_u)
+    other = swap(hi, "y", "far")
     grad_tokens = call(last_kernel, shape(tokens.shape, BF), [VMEM])(own)
     grad_gate, grad_up = call(
         unpack_kernel,

time: 138 us -> 142 us (1.029)
  the two profiles are of different devices: /device:TPU:2 before, /device:TPU:24 now
where the time goes in v6:
time: 142 us; the launch traced here: 141 us
  starting transfers between devices  70.3 us (50%)
  waiting for transfers between devices  47.8 us (34%)
  Pallas kernels  13.3 us (9%)
  local copies, waits for them, and re-layouts  6.68 us (5%)
  other arithmetic  1.97 us (1%)
    ppermute x15, starting transfers between devices, swap(): lax.ppermute(x, axis, [(i, turn(i, stage, size)) for i in range(size)])  46.5 us
    ppermute x15, waiting for transfers between devices, swap(): lax.ppermute(x, axis, [(i, turn(i, stage, size)) for i in range(size)])  40.2 us
    all_to_all x2, starting transfers between devices, body(): own = lax.all_to_all(own, 'z', 0, 0)  20.1 us
    pallas_call x1, Pallas kernels, body(): call(lambda *refs: main_kernel(blocks, *refs), (shape((tok, width), BF),...  6.91 us
    unnamed x18, local copies, waits for them, and re-layouts  5.24 us
    all_to_all x1, waiting for transfers between devices, body(): terms = lax.all_to_all(terms, 'x', 0, 0)  5.01 us
    all_to_all x1, starting transfers between devices, body(): terms = lax.all_to_all(terms, 'x', 0, 0)  3.73 us
  transfers between devices with their start and end apart: 18, of which 14 were waited for; matrix products, arithmetic and copies ran while one was open for 2% of the time, Pallas kernels for 2%

profile of v6, /device:TPU:24, one launch (start us, length us, event | category | flops | bytes accessed | tf_op | source)
XLA Modules:
  0.0 140.9 jit_solution(13123153555231931835)
XLA Ops:
  0.6 0.0 copy-start.5
  0.6 2.6 %shard_map.93 = (bf16[528,128]{1,0:T(8,128)(2,1)}, bf16[8,256,128]{2,1,0:T(8,128)(2,1)}) custom-call(s32[2,4]{1,0:T(2,128)} %gm_ref.3, s32[2,4]{1,0:T(2,128)} %um_ref.3, bf16[256,128]{1,0:T(8,128)(2,1)} %tok_ref.1, bf16[256,512]{1,0:T(8,128)(2,1)} %gw_ref.1, bf16[256,512]{1,0:T(8,128)(2,1)} %uw_ref.1), custom_call_target="tpu_custom_call" | custom-call | tf_op jit(solution)/shard_map/pallas_call | solution.py:250
  3.2 5.0 %collective-permute-start.4 = (bf16[1,528,128]{2,1,0:T(8,128)(2,1)}, bf16[1,528,128]{2,1,0:T(8,128)(2,1)S(1)}, u32[]{:S(2)}, u32[]{:S(2)}) collective-permute-start(bf16[1,528,128]{2,1,0:T(8,128)(2,1)} %bitcast.4), channel_id=1, source_target_pairs={{0,256},{64,320},{128,384},{192,448},{256,0},{320,64},{384,128},{4... | collective-permute-start | bytes 405512 | tf_op jit(solution)/shard_map/ppermute | solution.py:65
  8.3 10.3 %all-to-all-start = ((bf16[8,256,128]{2,1,0:T(8,128)(2,1)}), bf16[8,256,128]{2,1,0:T(8,128)(2,1)S(1)}, u32[]{:S(2)}, u32[]{:S(2)}) async-start(bf16[8,256,128]{2,1,0:T(8,128)(2,1)} %get-tuple-element.22), calls=%async_computation | async-start | bytes 1048576 | tf_op jit(solution)/shard_map/all_to_all | solution.py:261
  18.6 0.0 collective-permute-done.4
  18.6 0.9 pad_maximum_fusion.1
  19.5 3.3 %collective-permute-start.5 = (bf16[2,528,128]{2,1,0:T(8,128)(2,1)S(1)}, bf16[2,528,128]{2,1,0:T(8,128)(2,1)S(1)}, u32[]{:S(2)}, u32[]{:S(2)}) collective-permute-start(bf16[2,528,128]{2,1,0:T(8,128)(2,1)S(1)} %pad_maximum_fusion.1), channel_id=1, source_target_pairs={{0,64},{64,0},{128,192},{192,128},{256,320},{320,256},{384,448},{4... | collective-permute-start | bytes 811016 | tf_op jit(solution)/shard_map/ppermute | solution.py:65
  22.9 6.2 %collective-permute-done.5 = bf16[2,528,128]{2,1,0:T(8,128)(2,1)S(1)} collective-permute-done((bf16[2,528,128]{2,1,0:T(8,128)(2,1)S(1)}, bf16[2,528,128]{2,1,0:T(8,128)(2,1)S(1)}, u32[]{:S(2)}, u32[]{:S(2)}) %collective-permute-start.5) | collective-permute-done | bytes 270368 | tf_op jit(solution)/shard_map/ppermute | solution.py:65
  29.1 1.0 pad_maximum_fusion.refs_6_
  30.0 3.2 %collective-permute-start.6 = (bf16[4,528,128]{2,1,0:T(8,128)(2,1)S(1)}, bf16[4,528,128]{2,1,0:T(8,128)(2,1)S(1)}, u32[]{:S(2)}, u32[]{:S(2)}) collective-permute-start(bf16[4,528,128]{2,1,0:T(8,128)(2,1)S(1)} %pad_maximum_fusion.refs_6_), channel_id=1, source_target_pairs={{0,448},{64,128},{128,64},{192,256},{256,192},{320,384},{384,320},... | collective-permute-start | bytes 1622024 | tf_op jit(solution)/shard_map/ppermute | solution.py:65
  33.3 2.5 %all-to-all-done.refs_1_ = bf16[8,256,128]{2,1,0:T(8,128)(2,1)S(1)} async-done(((bf16[8,256,128]{2,1,0:T(8,128)(2,1)}), bf16[8,256,128]{2,1,0:T(8,128)(2,1)S(1)}, u32[]{:S(2)}, u32[]{:S(2)}) %all-to-all-start) | async-done | bytes 524320 | tf_op jit(solution)/shard_map/all_to_all | solution.py:261
  35.8 4.7 %collective-permute-start.1 = (bf16[8,256,128]{2,1,0:T(8,128)(2,1)S(1)}, bf16[8,256,128]{2,1,0:T(8,128)(2,1)S(1)}, u32[]{:S(2)}, u32[]{:S(2)}) collective-permute-start(bf16[8,256,128]{2,1,0:T(8,128)(2,1)S(1)} %all-to-all-done.refs_1_), channel_id=1, source_target_pairs={{0,24},{8,16},{16,8},{24,0},{1,25},{9,17},{17,9},{25,1},{2,26},{10... | collective-permute-start | bytes 1572872 | tf_op jit(solution)/shard_map/ppermute | solution.py:65
  40.5 2.1 %collective-permute-start = (bf16[8,256,128]{2,1,0:T(8,128)(2,1)S(1)}, bf16[8,256,128]{2,1,0:T(8,128)(2,1)S(1)}, u32[]{:S(2)}, u32[]{:S(2)}) collective-permute-start(bf16[8,256,128]{2,1,0:T(8,128)(2,1)S(1)} %all-to-all-done.refs_1_), channel_id=1, source_target_pairs={{0,8},{8,0},{16,24},{24,16},{1,9},{9,1},{17,25},{25,17},{2,10},{10... | collective-permute-start | bytes 1572872 | tf_op jit(solution)/shard_map/ppermute | solution.py:65
  42.6 1.9 %collective-permute-start.7 = (bf16[4,528,128]{2,1,0:T(8,128)(2,1)S(1)}, bf16[4,528,128]{2,1,0:T(8,128)(2,1)S(1)}, u32[]{:S(2)}, u32[]{:S(2)}) collective-permute-start(bf16[4,528,128]{2,1,0:T(8,128)(2,1)S(1)} %pad_maximum_fusion.refs_6_), channel_id=1, source_target_pairs={{0,32},{32,0},{1,33},{33,1},{2,34},{34,2},{3,35},{35,3},{4,36},{36... | collective-permute-start | bytes 1622024 | tf_op jit(solution)/shard_map/ppermute | solution.py:65
  44.5 1.1 collective-permute-done.6.refs_7_
  45.7 0.0 copy-start.1
  45.7 1.9 %collective-permute-start.8 = (bf16[4,528,128]{2,1,0:T(8,128)(2,1)S(1)}, bf16[4,528,128]{2,1,0:T(8,128)(2,1)}, u32[]{:S(2)}, u32[]{:S(2)}) collective-permute-start(bf16[4,528,128]{2,1,0:T(8,128)(2,1)S(1)} %collective-permute-done.6.refs_7_), channel_id=1, source_target_pairs={{0,32},{32,0},{1,33},{33,1},{2,34},{34,2},{3,35},{35,3},{4,36},{36... | collective-permute-start | bytes 1622024 | tf_op jit(solution)/shard_map/ppermute | solution.py:65
  47.6 4.2 %collective-permute-done.1.refs_3_ = bf16[8,256,128]{2,1,0:T(8,128)(2,1)S(1)} collective-permute-done((bf16[8,256,128]{2,1,0:T(8,128)(2,1)S(1)}, bf16[8,256,128]{2,1,0:T(8,128)(2,1)S(1)}, u32[]{:S(2)}, u32[]{:S(2)}) %collective-permute-start.1) | collective-permute-done | bytes 524320 | tf_op jit(solution)/shard_map/ppermute | solution.py:65
  51.8 0.7 slice.9
  52.5 2.4 %collective-permute-start.3 = (bf16[4,256,128]{2,1,0:T(8,128)(2,1)}, bf16[4,256,128]{2,1,0:T(8,128)(2,1)}, u32[]{:S(2)}, u32[]{:S(2)}) collective-permute-start(bf16[4,256,128]{2,1,0:T(8,128)(2,1)} %slice.9), channel_id=1, source_target_pairs={{0,8},{8,0},{16,24},{24,16},{1,9},{9,1},{17,25},{25,17},{2,10},{10... | collective-permute-start | bytes 786440 | tf_op jit(solution)/shard_map/ppermute | solution.py:65
  55.0 0.1 collective-permute-done.refs_2_
  55.1 0.7 slice.8
  55.8 4.1 %collective-permute-start.2 = (bf16[4,256,128]{2,1,0:T(8,128)(2,1)}, bf16[4,256,128]{2,1,0:T(8,128)(2,1)}, u32[]{:S(2)}, u32[]{:S(2)}) collective-permute-start(bf16[4,256,128]{2,1,0:T(8,128)(2,1)} %slice.8), channel_id=1, source_target_pairs={{0,24},{8,16},{16,8},{24,0},{1,25},{9,17},{17,9},{25,1},{2,26},{10... | collective-permute-start | bytes 786440 | tf_op jit(solution)/shard_map/ppermute | solution.py:65
  59.9 0.1 pad_add_fusion.refs_0_
  60.0 0.0 collective-permute-done.7.refs_8_
  60.0 0.0 copy-start.3
  60.0 0.8 copy-done.3
  60.8 0.0 collective-permute-done.8.refs_9_
  60.8 0.3 collective-permute-done.3.refs_5_
  61.1 0.0 copy-done.1
  61.1 4.5 %collective-permute-done.2.refs_4_ = bf16[4,256,128]{2,1,0:T(8,128)(2,1)} collective-permute-done((bf16[4,256,128]{2,1,0:T(8,128)(2,1)}, bf16[4,256,128]{2,1,0:T(8,128)(2,1)}, u32[]{:S(2)}, u32[]{:S(2)}) %collective-permute-start.2) | collective-permute-done | bytes 262176 | tf_op jit(solution)/shard_map/ppermute | solution.py:65
  65.6 0.0 copy-done.5
  65.6 0.0 copy-start.2
  65.6 1.0 copy-done.2
  66.6 0.0 copy-start.4
  66.6 1.0 copy-done.4
  67.7 6.9 %shard_map.94 = (bf16[256,512]{1,0:T(8,128)(2,1)}, bf16[2,8,256,128]{3,2,1,0:T(8,128)(2,1)S(1)}, bf16[2,8,256,128]{3,2,1,0:T(8,128)(2,1)S(1)}, bf16[4,8,256,128]{3,2,1,0:T(8,128)(2,1)S(1)}) custom-call(s32[3]{0:T(128)S(1)} %pad_add_fusion.refs_0_, bf16[8,256,128]{2,1,0:T(8,128)(2,1)S(1)} %all-to-all-done.refs_1_, ...), custom_call_target="tpu_custom_call" | custom-call | tf_op jit(solution)/shard_map/pallas_call | solution.py:271
  74.6 0.0 copy-start
  74.6 1.3 copy-done
  75.9 1.0 copy-done.8
  76.9 3.7 %all-to-all-start.1 = ((bf16[4,8,256,128]{3,2,1,0:T(8,128)(2,1)}), bf16[4,8,256,128]{3,2,1,0:T(8,128)(2,1)S(1)}, u32[]{:S(2)}, u32[]{:S(2)}) async-start(bf16[4,8,256,128]{3,2,1,0:T(8,128)(2,1)} %copy-done), calls=%async_computation.1 | async-start | bytes 4194304 | tf_op jit(solution)/shard_map/all_to_all | solution.py:293
  80.7 1.9 %collective-permute-start.9 = (bf16[2,8,256,128]{3,2,1,0:T(8,128)(2,1)}, bf16[2,8,256,128]{3,2,1,0:T(8,128)(2,1)S(1)}, u32[]{:S(2)}, u32[]{:S(2)}) collective-permute-start(bf16[2,8,256,128]{3,2,1,0:T(8,128)(2,1)} %copy-done.8), channel_id=1, source_target_pairs={{0,32},{32,0},{1,33},{33,1},{2,34},{34,2},{3,35},{35,3},{4,36},{36... | collective-permute-start | bytes 3145736 | tf_op jit(solution)/shard_map/ppermute | solution.py:65
  82.6 2.8 %collective-permute-done.9.other = bf16[2,8,256,128]{3,2,1,0:T(8,128)(2,1)S(1)} collective-permute-done((bf16[2,8,256,128]{3,2,1,0:T(8,128)(2,1)}, bf16[2,8,256,128]{3,2,1,0:T(8,128)(2,1)S(1)}, u32[]{:S(2)}, u32[]{:S(2)}) %collective-permute-start.9) | collective-permute-done | bytes 1048608 | tf_op jit(solution)/shard_map/ppermute | solution.py:65
  85.4 0.2 shard_map.95
  85.7 3.4 %collective-permute-start.10 = (bf16[4,256,128]{2,1,0:T(8,128)(2,1)S(1)}, bf16[4,256,128]{2,1,0:T(8,128)(2,1)S(1)}, u32[]{:S(2)}, u32[]{:S(2)}) collective-permute-start(bf16[4,256,128]{2,1,0:T(8,128)(2,1)S(1)} %get-tuple-element.29), channel_id=1, source_target_pairs={{0,448},{64,128},{128,64},{192,256},{256,192},{320,384},{384,320},... | collective-permute-start | bytes 786440 | tf_op jit(solution)/shard_map/ppermute | solution.py:65
  89.1 3.1 %collective-permute-start.11 = (bf16[4,256,128]{2,1,0:T(8,128)(2,1)S(1)}, bf16[4,256,128]{2,1,0:T(8,128)(2,1)S(1)}, u32[]{:S(2)}, u32[]{:S(2)}) collective-permute-start(bf16[4,256,128]{2,1,0:T(8,128)(2,1)S(1)} %get-tuple-element.31), channel_id=1, source_target_pairs={{0,64},{64,0},{128,192},{192,128},{256,320},{320,256},{384,448},{4... | collective-permute-start | bytes 786440 | tf_op jit(solution)/shard_map/ppermute | solution.py:65
  92.2 4.9 %collective-permute-done.10.from_g = bf16[4,256,128]{2,1,0:T(8,128)(2,1)S(1)} collective-permute-done((bf16[4,256,128]{2,1,0:T(8,128)(2,1)S(1)}, bf16[4,256,128]{2,1,0:T(8,128)(2,1)S(1)}, u32[]{:S(2)}, u32[]{:S(2)}) %collective-permute-start.10) | collective-permute-done | bytes 262176 | tf_op jit(solution)/shard_map/ppermute | solution.py:65
  97.1 1.9 %collective-permute-done.11.from_u = bf16[4,256,128]{2,1,0:T(8,128)(2,1)S(1)} collective-permute-done((bf16[4,256,128]{2,1,0:T(8,128)(2,1)S(1)}, bf16[4,256,128]{2,1,0:T(8,128)(2,1)S(1)}, u32[]{:S(2)}, u32[]{:S(2)}) %collective-permute-start.11) | collective-permute-done | bytes 262176 | tf_op jit(solution)/shard_map/ppermute | solution.py:65
  99.0 0.1 shard_map.96
  99.2 5.0 %all-to-all-done.1.t_ref = bf16[4,8,256,128]{3,2,1,0:T(8,128)(2,1)S(1)} async-done(((bf16[4,8,256,128]{3,2,1,0:T(8,128)(2,1)}), bf16[4,8,256,128]{3,2,1,0:T(8,128)(2,1)S(1)}, u32[]{:S(2)}, u32[]{:S(2)}) %all-to-all-start.1) | async-done | bytes 2097184 | tf_op jit(solution)/shard_map/all_to_all | solution.py:293
  104.2 1.0 shard_map.97
  105.2 9.8 %all-to-all-start.2 = ((bf16[8,256,128]{2,1,0:T(8,128)(2,1)}), bf16[8,256,128]{2,1,0:T(8,128)(2,1)S(1)}, u32[]{:S(2)}, u32[]{:S(2)}) async-start(bf16[8,256,128]{2,1,0:T(8,128)(2,1)} %shard_map.97), calls=%async_computation.2 | async-start | bytes 1048576 | tf_op jit(solution)/shard_map/all_to_all | solution.py:300
  115.0 3.2 %collective-permute-start.12 = (bf16[2,256,128]{2,1,0:T(8,128)(2,1)S(1)}, bf16[2,256,128]{2,1,0:T(8,128)(2,1)S(1)}, u32[]{:S(2)}, u32[]{:S(2)}) collective-permute-start(bf16[2,256,128]{2,1,0:T(8,128)(2,1)S(1)} %get-tuple-element.33), channel_id=1, source_target_pairs={{0,64},{64,0},{128,192},{192,128},{256,320},{320,256},{384,448},{4... | collective-permute-start | bytes 393224 | tf_op jit(solution)/shard_map/ppermute | solution.py:65
  118.2 1.9 %collective-permute-start.13 = (bf16[2,256,128]{2,1,0:T(8,128)(2,1)S(1)}, bf16[2,256,128]{2,1,0:T(8,128)(2,1)S(1)}, u32[]{:S(2)}, u32[]{:S(2)}) collective-permute-start(bf16[2,256,128]{2,1,0:T(8,128)(2,1)S(1)} %get-tuple-element.35), channel_id=1, source_target_pairs={{0,448},{64,128},{128,64},{192,256},{256,192},{320,384},{384,320},... | collective-permute-start | bytes 393224 | tf_op jit(solution)/shard_map/ppermute | solution.py:65
  120.1 1.7 %collective-permute-done.12.from_g = bf16[2,256,128]{2,1,0:T(8,128)(2,1)S(1)} collective-permute-done((bf16[2,256,128]{2,1,0:T(8,128)(2,1)S(1)}, bf16[2,256,128]{2,1,0:T(8,128)(2,1)S(1)}, u32[]{:S(2)}, u32[]{:S(2)}) %collective-permute-start.12) | collective-permute-done | bytes 131104 | tf_op jit(solution)/shard_map/ppermute | solution.py:65
  121.8 4.4 %collective-permute-done.13.from_u = bf16[2,256,128]{2,1,0:T(8,128)(2,1)S(1)} collective-permute-done((bf16[2,256,128]{2,1,0:T(8,128)(2,1)S(1)}, bf16[2,256,128]{2,1,0:T(8,128)(2,1)S(1)}, u32[]{:S(2)}, u32[]{:S(2)}) %collective-permute-start.13) | collective-permute-done | bytes 131104 | tf_op jit(solution)/shard_map/ppermute | solution.py:65
  126.3 0.1 shard_map.99
  126.3 4.2 %collective-permute-start.14 = (bf16[2,256,128]{2,1,0:T(8,128)(2,1)S(1)}, bf16[2,256,128]{2,1,0:T(8,128)(2,1)S(1)}, u32[]{:S(2)}, u32[]{:S(2)}) collective-permute-start(bf16[2,256,128]{2,1,0:T(8,128)(2,1)S(1)} %get-tuple-element.37), channel_id=1, source_target_pairs={{0,256},{64,320},{128,384},{192,448},{256,0},{320,64},{384,128},{4... | collective-permute-start | bytes 393224 | tf_op jit(solution)/shard_map/ppermute | solution.py:65
  130.5 8.0 %collective-permute-done.14.b_ref = bf16[2,256,128]{2,1,0:T(8,128)(2,1)S(1)} collective-permute-done((bf16[2,256,128]{2,1,0:T(8,128)(2,1)S(1)}, bf16[2,256,128]{2,1,0:T(8,128)(2,1)S(1)}, u32[]{:S(2)}, u32[]{:S(2)}) %collective-permute-start.14) | collective-permute-done | bytes 131104 | tf_op jit(solution)/shard_map/ppermute | solution.py:65
  138.5 0.0 copy-done.6
  138.5 0.0 copy-done.7
  138.5 1.7 %shard_map.100 = (bf16[256,512]{1,0:T(8,128)(2,1)}, bf16[256,512]{1,0:T(8,128)(2,1)}) custom-call(s32[2,4]{1,0:T(2,128)S(1)} %copy-done.6, s32[2,4]{1,0:T(2,128)S(1)} %copy-done.7, bf16[2,256,128]{2,1,0:T(8,128)(2,1)S(1)} %get-tuple-element.36.a_ref, bf16[2,256,128]{2,1,0:T(8,128)(2,1)S(1)} %collective-permute-done.14.b_ref), custom_call_target="tpu_custom_call" | custom-call | tf_op jit(solution)/shard_map/pallas_call | solution.py:306
  140.2 0.0 all-to-all-done.2.a_ref
  140.2 0.7 shard_map.98
  (3 shorter events, 0.0 us)
Async XLA Ops:
  0.6 64.9 %copy-start.5 = (bf16[256,512]{1,0:T(8,128)(2,1)S(1)}, bf16[256,512]{1,0:T(8,128)(2,1)}, u32[]{:S(2)}) copy-start(bf16[256,512]{1,0:T(8,128)(2,1)} %refs_10_.1) | copy-start | bytes 786436
  3.2 15.4 %collective-permute-start.4 = (bf16[1,528,128]{2,1,0:T(8,128)(2,1)}, bf16[1,528,128]{2,1,0:T(8,128)(2,1)S(1)}, u32[]{:S(2)}, u32[]{:S(2)}) collective-permute-start(bf16[1,528,128]{2,1,0:T(8,128)(2,1)} %bitcast.4), channel_id=1, source_target_pairs={{0,256},{64,320},{128,384},{192,448},{256,0},{320,64},{384,128},{4... | collective-permute-start | bytes 405512 | tf_op jit(solution)/shard_map/ppermute | solution.py:65
  8.3 27.5 %all-to-all-start = ((bf16[8,256,128]{2,1,0:T(8,128)(2,1)}), bf16[8,256,128]{2,1,0:T(8,128)(2,1)S(1)}, u32[]{:S(2)}, u32[]{:S(2)}) async-start(bf16[8,256,128]{2,1,0:T(8,128)(2,1)} %get-tuple-element.22), calls=%async_computation | async-start | bytes 1048576 | tf_op jit(solution)/shard_map/all_to_all | solution.py:261
  19.5 9.6 %collective-permute-start.5 = (bf16[2,528,128]{2,1,0:T(8,128)(2,1)S(1)}, bf16[2,528,128]{2,1,0:T(8,128)(2,1)S(1)}, u32[]{:S(2)}, u32[]{:S(2)}) collective-permute-start(bf16[2,528,128]{2,1,0:T(8,128)(2,1)S(1)} %pad_maximum_fusion.1), channel_id=1, source_target_pairs={{0,64},{64,0},{128,192},{192,128},{256,320},{320,256},{384,448},{4... | collective-permute-start | bytes 811016 | tf_op jit(solution)/shard_map/ppermute | solution.py:65
  30.0 15.6 %collective-permute-start.6 = (bf16[4,528,128]{2,1,0:T(8,128)(2,1)S(1)}, bf16[4,528,128]{2,1,0:T(8,128)(2,1)S(1)}, u32[]{:S(2)}, u32[]{:S(2)}) collective-permute-start(bf16[4,528,128]{2,1,0:T(8,128)(2,1)S(1)} %pad_maximum_fusion.refs_6_), channel_id=1, source_target_pairs={{0,448},{64,128},{128,64},{192,256},{256,192},{320,384},{384,320},... | collective-permute-start | bytes 1622024 | tf_op jit(solution)/shard_map/ppermute | solution.py:65
  35.8 16.0 %collective-permute-start.1 = (bf16[8,256,128]{2,1,0:T(8,128)(2,1)S(1)}, bf16[8,256,128]{2,1,0:T(8,128)(2,1)S(1)}, u32[]{:S(2)}, u32[]{:S(2)}) collective-permute-start(bf16[8,256,128]{2,1,0:T(8,128)(2,1)S(1)} %all-to-all-done.refs_1_), channel_id=1, source_target_pairs={{0,24},{8,16},{16,8},{24,0},{1,25},{9,17},{17,9},{25,1},{2,26},{10... | collective-permute-start | bytes 1572872 | tf_op jit(solution)/shard_map/ppermute | solution.py:65
  40.5 14.6 %collective-permute-start = (bf16[8,256,128]{2,1,0:T(8,128)(2,1)S(1)}, bf16[8,256,128]{2,1,0:T(8,128)(2,1)S(1)}, u32[]{:S(2)}, u32[]{:S(2)}) collective-permute-start(bf16[8,256,128]{2,1,0:T(8,128)(2,1)S(1)} %all-to-all-done.refs_1_), channel_id=1, source_target_pairs={{0,8},{8,0},{16,24},{24,16},{1,9},{9,1},{17,25},{25,17},{2,10},{10... | collective-permute-start | bytes 1572872 | tf_op jit(solution)/shard_map/ppermute | solution.py:65
  42.6 17.4 %collective-permute-start.7 = (bf16[4,528,128]{2,1,0:T(8,128)(2,1)S(1)}, bf16[4,528,128]{2,1,0:T(8,128)(2,1)S(1)}, u32[]{:S(2)}, u32[]{:S(2)}) collective-permute-start(bf16[4,528,128]{2,1,0:T(8,128)(2,1)S(1)} %pad_maximum_fusion.refs_6_), channel_id=1, source_target_pairs={{0,32},{32,0},{1,33},{33,1},{2,34},{34,2},{3,35},{35,3},{4,36},{36... | collective-permute-start | bytes 1622024 | tf_op jit(solution)/shard_map/ppermute | solution.py:65
  45.7 15.4 %copy-start.1 = (bf16[4,528,128]{2,1,0:T(8,128)(2,1)}, bf16[4,528,128]{2,1,0:T(8,128)(2,1)S(1)}, u32[]{:S(2)}) copy-start(bf16[4,528,128]{2,1,0:T(8,128)(2,1)S(1)} %collective-permute-done.6.refs_7_) | copy-start | bytes 1622020
  45.7 15.1 %collective-permute-start.8 = (bf16[4,528,128]{2,1,0:T(8,128)(2,1)S(1)}, bf16[4,528,128]{2,1,0:T(8,128)(2,1)}, u32[]{:S(2)}, u32[]{:S(2)}) collective-permute-start(bf16[4,528,128]{2,1,0:T(8,128)(2,1)S(1)} %collective-permute-done.6.refs_7_), channel_id=1, source_target_pairs={{0,32},{32,0},{1,33},{33,1},{2,34},{34,2},{3,35},{35,3},{4,36},{36... | collective-permute-start | bytes 1622024 | tf_op jit(solution)/shard_map/ppermute | solution.py:65
  52.5 8.6 %collective-permute-start.3 = (bf16[4,256,128]{2,1,0:T(8,128)(2,1)}, bf16[4,256,128]{2,1,0:T(8,128)(2,1)}, u32[]{:S(2)}, u32[]{:S(2)}) collective-permute-start(bf16[4,256,128]{2,1,0:T(8,128)(2,1)} %slice.9), channel_id=1, source_target_pairs={{0,8},{8,0},{16,24},{24,16},{1,9},{9,1},{17,25},{25,17},{2,10},{10... | collective-permute-start | bytes 786440 | tf_op jit(solution)/shard_map/ppermute | solution.py:65
  55.8 9.8 %collective-permute-start.2 = (bf16[4,256,128]{2,1,0:T(8,128)(2,1)}, bf16[4,256,128]{2,1,0:T(8,128)(2,1)}, u32[]{:S(2)}, u32[]{:S(2)}) collective-permute-start(bf16[4,256,128]{2,1,0:T(8,128)(2,1)} %slice.8), channel_id=1, source_target_pairs={{0,24},{8,16},{16,8},{24,0},{1,25},{9,17},{17,9},{25,1},{2,26},{10... | collective-permute-start | bytes 786440 | tf_op jit(solution)/shard_map/ppermute | solution.py:65
  60.0 0.8 copy-start.3
  65.6 1.0 copy-start.2
  66.6 1.0 copy-start.4
  74.6 1.3 copy-start
  75.9 1.0 copy-start.8
  76.9 27.2 %all-to-all-start.1 = ((bf16[4,8,256,128]{3,2,1,0:T(8,128)(2,1)}), bf16[4,8,256,128]{3,2,1,0:T(8,128)(2,1)S(1)}, u32[]{:S(2)}, u32[]{:S(2)}) async-start(bf16[4,8,256,128]{3,2,1,0:T(8,128)(2,1)} %copy-done), calls=%async_computation.1 | async-start | bytes 4194304 | tf_op jit(solution)/shard_map/all_to_all | solution.py:293
  80.7 4.8 %collective-permute-start.9 = (bf16[2,8,256,128]{3,2,1,0:T(8,128)(2,1)}, bf16[2,8,256,128]{3,2,1,0:T(8,128)(2,1)S(1)}, u32[]{:S(2)}, u32[]{:S(2)}) collective-permute-start(bf16[2,8,256,128]{3,2,1,0:T(8,128)(2,1)} %copy-done.8), channel_id=1, source_target_pairs={{0,32},{32,0},{1,33},{33,1},{2,34},{34,2},{3,35},{35,3},{4,36},{36... | collective-permute-start | bytes 3145736 | tf_op jit(solution)/shard_map/ppermute | solution.py:65
  85.7 11.5 %collective-permute-start.10 = (bf16[4,256,128]{2,1,0:T(8,128)(2,1)S(1)}, bf16[4,256,128]{2,1,0:T(8,128)(2,1)S(1)}, u32[]{:S(2)}, u32[]{:S(2)}) collective-permute-start(bf16[4,256,128]{2,1,0:T(8,128)(2,1)S(1)} %get-tuple-element.29), channel_id=1, source_target_pairs={{0,448},{64,128},{128,64},{192,256},{256,192},{320,384},{384,320},... | collective-permute-start | bytes 786440 | tf_op jit(solution)/shard_map/ppermute | solution.py:65
  89.1 10.0 %collective-permute-start.11 = (bf16[4,256,128]{2,1,0:T(8,128)(2,1)S(1)}, bf16[4,256,128]{2,1,0:T(8,128)(2,1)S(1)}, u32[]{:S(2)}, u32[]{:S(2)}) collective-permute-start(bf16[4,256,128]{2,1,0:T(8,128)(2,1)S(1)} %get-tuple-element.31), channel_id=1, source_target_pairs={{0,64},{64,0},{128,192},{192,128},{256,320},{320,256},{384,448},{4... | collective-permute-start | bytes 786440 | tf_op jit(solution)/shard_map/ppermute | solution.py:65
  104.2 34.3 %copy-start.6 = (s32[2,4]{1,0:T(2,128)S(1)}, s32[2,4]{1,0:T(2,128)}, u32[]{:S(2)}) copy-start(s32[2,4]{1,0:T(2,128)} %gm_ref.3) | copy-start | bytes 100
  104.2 34.3 %copy-start.7 = (s32[2,4]{1,0:T(2,128)S(1)}, s32[2,4]{1,0:T(2,128)}, u32[]{:S(2)}) copy-start(s32[2,4]{1,0:T(2,128)} %um_ref.3) | copy-start | bytes 100
  105.2 34.9 %all-to-all-start.2 = ((bf16[8,256,128]{2,1,0:T(8,128)(2,1)}), bf16[8,256,128]{2,1,0:T(8,128)(2,1)S(1)}, u32[]{:S(2)}, u32[]{:S(2)}) async-start(bf16[8,256,128]{2,1,0:T(8,128)(2,1)} %shard_map.97), calls=%async_computation.2 | async-start | bytes 1048576 | tf_op jit(solution)/shard_map/all_to_all | solution.py:300
  115.0 6.8 %collective-permute-start.12 = (bf16[2,256,128]{2,1,0:T(8,128)(2,1)S(1)}, bf16[2,256,128]{2,1,0:T(8,128)(2,1)S(1)}, u32[]{:S(2)}, u32[]{:S(2)}) collective-permute-start(bf16[2,256,128]{2,1,0:T(8,128)(2,1)S(1)} %get-tuple-element.33), channel_id=1, source_target_pairs={{0,64},{64,0},{128,192},{192,128},{256,320},{320,256},{384,448},{4... | collective-permute-start | bytes 393224 | tf_op jit(solution)/shard_map/ppermute | solution.py:65
  118.2 8.1 %collective-permute-start.13 = (bf16[2,256,128]{2,1,0:T(8,128)(2,1)S(1)}, bf16[2,256,128]{2,1,0:T(8,128)(2,1)S(1)}, u32[]{:S(2)}, u32[]{:S(2)}) collective-permute-start(bf16[2,256,128]{2,1,0:T(8,128)(2,1)S(1)} %get-tuple-element.35), channel_id=1, source_target_pairs={{0,448},{64,128},{128,64},{192,256},{256,192},{320,384},{384,320},... | collective-permute-start | bytes 393224 | tf_op jit(solution)/shard_map/ppermute | solution.py:65
  126.3 12.1 %collective-permute-start.14 = (bf16[2,256,128]{2,1,0:T(8,128)(2,1)S(1)}, bf16[2,256,128]{2,1,0:T(8,128)(2,1)S(1)}, u32[]{:S(2)}, u32[]{:S(2)}) collective-permute-start(bf16[2,256,128]{2,1,0:T(8,128)(2,1)S(1)} %get-tuple-element.37), channel_id=1, source_target_pairs={{0,256},{64,320},{128,384},{192,448},{256,0},{320,64},{384,128},{4... | collective-permute-start | bytes 393224 | tf_op jit(solution)/shard_map/ppermute | solution.py:65

commit v7 on v6

--- a/solution.py
+++ b/solution.py
@@ -112,30 +112,40 @@
 
 def main_kernel(blocks, me_ref, own, r1, r2, oa, ob, w0, w1, w2, w3, cot_ref, *rest):
     hid_ref, keep_ref, send_ref, t_ref = rest[:4]
-    x_ref, w_ref, at_vec, at_ref, idx_ref, acc, g_ref, gt, sem = rest[4:]
-    count = w0.shape[0]
-    for g, part in enumerate((w0, w1, w2, w3)):
-        for i in range(count):
-            meta = part[i, pl.ds(META, 16), :].astype(F32).astype(jnp.int32)
-            at_vec[pl.ds(g * count + i, 1), :] = meta[:1]
-    scalars = pltpu.make_async_copy(at_vec, at_ref, sem)
-    scalars.start()
+    x_ref, w_ref, metas, at_vec, at_ref, idx_ref, acc, g_ref, gt, sem, sems = rest[4:]
     my_x, my_c, my_y = me_ref[0], me_ref[1], me_ref[2]
     shards = w_ref.shape[0]
     ys, zs, half = shards // 2, own.shape[0], oa.shape[0]
+    count = w0.shape[0]
+    places, small, large = [], [], []
+    for g, part in enumerate((w0, w1, w2, w3)):
+        for i in range(count):
+            k = g * count + i
+            places.append(2 * origin(my_y, k % ys, ys) + (my_c if g < 2 else 1 - my_c))
+            meta = part.at[i, pl.ds(META, 16)]
+            small.append(pltpu.make_async_copy(meta, metas.at[k], sems.at[0, k]))
+            data = part.at[i, pl.ds(0, META)]
+            large.append(pltpu.make_async_copy(data, w_ref.at[places[k]], sems.at[1, k]))
+    for copy in small + large:
+        copy.start()
     xs = 2 * shards // zs
     far, one, two = ((turn(my_x, stage, xs)) for stage in ("far", "one", "two"))
-    for part, x, z in ((own, my_x, 0), (r1, one, 0), (r2, two, 0), (oa, far, 0), (ob, far, half)):
-        for i in range(part.shape[0]):
-            x_ref[x * zs + z + i] = part[i]
+    parts = ((own, my_x, 0), (r1, one, 0), (r2, two, 0), (oa, far, 0), (ob, far, half))
+    for k, (part, x, z) in enumerate(parts):
+        place = x_ref.at[pl.ds(x * zs + z, part.shape[0])]
+        large.append(pltpu.make_async_copy(part, place, sems.at[2, k]))
+        large[-1].start()
+    for k, copy in enumerate(small):
+        copy.wait()
+        at_vec[pl.ds(k, 1), :] = metas[k].astype(F32).astype(jnp.int32)[:1]
+    scalars = pltpu.make_async_copy(at_vec, at_ref, sem)
+    scalars.start()
     scalars.wait()
-    for g, part in enumerate((w0, w1, w2, w3)):
-        for i in range(count):
-            y = origin(my_y, (g % 2) * count + i, ys)
-            n = 2 * y + (my_c if g < 2 else 1 - my_c)
-            w_ref[n] = part[i, pl.ds(0, META), :]
-            for s in range(SLOTS):
-                idx_ref[n, s] = at_ref[g * count + i, s]
+    for k, n in enumerate(places):
+        for s in range(SLOTS):
+            idx_ref[n, s] = at_ref[k, s]
+    for copy in large:
+        copy.wait()
 
     acc[...] = jnp.zeros_like(acc)
     for n in range(shards):
@@ -276,10 +286,11 @@
             shape((2, ys, META // 2, BLK), BF),
             shape((xs, zs, tok, BLK), BF),
         ),
-        [SMEM] + [VMEM] * 10,
+        [SMEM] + [HBM] * 9 + [VMEM],
         [
             pltpu.VMEM((xs * zs, tok, BLK), BF),
             pltpu.VMEM((2 * ys, META, BLK), BF),
+            pltpu.VMEM((2 * ys, 16, BLK), BF),
             pltpu.VMEM((2 * ys, BLK), jnp.int32),
             pltpu.SMEM((2 * ys, BLK), jnp.int32),
             pltpu.SMEM((2 * ys, SLOTS), jnp.int32),
@@ -287,7 +298,9 @@
             pltpu.VMEM((2 * blocks, tok, BLK), BF),
             pltpu.VMEM((2 * blocks, BLK, tok), BF),
             pltpu.SemaphoreType.DMA(()),
+            pltpu.SemaphoreType.DMA((3, 2 * ys)),
         ],
+        limit=58,
     )(me, own, r1, r2, oa, ob, *w, cotangent)
     other = swap(send, "c", "one")
     terms = lax.all_to_all(terms, "x", 0, 0)
@@ -296,11 +309,11 @@
     from_g, from_u = swap(hi_g, "y", "two"), swap(hi_u, "y", "one")
     part = shape((ys // 4, META // 2, BLK), BF)
     g, hi_g, u, hi_u = call(second_kernel, (part,) * 4, [VMEM] * 4)(g, from_g, u, from_u)
-    own = call(middle_kernel, shape(own.shape, BF), [VMEM, HBM])(terms, g)
-    own = lax.all_to_all(own, "z", 0, 0)
     from_g, from_u = swap(hi_g, "y", "one"), swap(hi_u, "y", "two")
     part = shape((2, META // 2, BLK), BF)
     lo, hi = call(third_kernel, (part,) * 2, [VMEM] * 4)(g, from_g, u, from_u)
+    own = call(middle_kernel, shape(own.shape, BF), [VMEM, HBM])(terms, lo)
+    own = lax.all_to_all(own, "z", 0, 0)
     other = swap(hi, "y", "far")
     grad_tokens = call(last_kernel, shape(tokens.shape, BF), [VMEM])(own)
     grad_gate, grad_up = call(

time: 142 us -> 136 us (0.958)
  the two profiles are of different devices: /device:TPU:24 before, /device:TPU:2 now
where the time goes in v7:
time: 136 us
  starting transfers between devices  72.8 us (54%)
  waiting for transfers between devices  41.7 us (31%)
  Pallas kernels  16.1 us (12%)
  other arithmetic  2.48 us (2%)
  local copies, waits for them, and re-layouts  1.58 us (1%)
    ppermute x15, starting transfers between devices, swap(): lax.ppermute(x, axis, [(i, turn(i, stage, size)) for i in range(size)])  49.7 us
    ppermute x15, waiting for transfers between devices, swap(): lax.ppermute(x, axis, [(i, turn(i, stage, size)) for i in range(size)])  36.3 us
    all_to_all x2, starting transfers between devices, body(): own = lax.all_to_all(own, 'z', 0, 0)  17.7 us
    pallas_call x1, Pallas kernels, body(): call(lambda *refs: main_kernel(blocks, *refs), (shape((tok, width), BF),...  9.91 us
    all_to_all x1, starting transfers between devices, body(): terms = lax.all_to_all(terms, 'x', 0, 0)  5.47 us
    all_to_all x2, waiting for transfers between devices, body(): own = lax.all_to_all(own, 'z', 0, 0)  5.38 us
  transfers between devices with their start and end apart: 18, of which 11 were waited for; matrix products, arithmetic and copies ran while one was open for 3% of the time, Pallas kernels for 1%

profile of v7, /device:TPU:2, one launch (start us, length us, event | category | flops | bytes accessed | tf_op | source)
XLA Modules:
  0.0 135.6 jit_solution(17059653704796959945)
XLA Ops:
  0.6 2.5 %shard_map.93 = (bf16[528,128]{1,0:T(8,128)(2,1)}, bf16[8,256,128]{2,1,0:T(8,128)(2,1)}) custom-call(s32[2,4]{1,0:T(2,128)} %gm_ref.3, s32[2,4]{1,0:T(2,128)} %um_ref.3, bf16[256,128]{1,0:T(8,128)(2,1)} %tok_ref.1, bf16[256,512]{1,0:T(8,128)(2,1)} %gw_ref.1, bf16[256,512]{1,0:T(8,128)(2,1)} %uw_ref.1), custom_call_target="tpu_custom_call" | custom-call | tf_op jit(solution)/shard_map/pallas_call | solution.py:260
  3.1 7.7 %collective-permute-start.4 = (bf16[1,528,128]{2,1,0:T(8,128)(2,1)}, bf16[1,528,128]{2,1,0:T(8,128)(2,1)S(1)}, u32[]{:S(2)}, u32[]{:S(2)}) collective-permute-start(bf16[1,528,128]{2,1,0:T(8,128)(2,1)} %bitcast.4), channel_id=1, source_target_pairs={{0,256},{64,320},{128,384},{192,448},{256,0},{320,64},{384,128},{4... | collective-permute-start | bytes 405512 | tf_op jit(solution)/shard_map/ppermute | solution.py:65
  10.8 10.3 %all-to-all-start = ((bf16[8,256,128]{2,1,0:T(8,128)(2,1)}), bf16[8,256,128]{2,1,0:T(8,128)(2,1)S(1)}, u32[]{:S(2)}, u32[]{:S(2)}) async-start(bf16[8,256,128]{2,1,0:T(8,128)(2,1)} %get-tuple-element.22), calls=%async_computation | async-start | bytes 1048576 | tf_op jit(solution)/shard_map/all_to_all | solution.py:271
  21.2 0.0 collective-permute-done.4
  21.2 0.9 pad_maximum_fusion.1
  22.1 2.6 %collective-permute-start.5 = (bf16[2,528,128]{2,1,0:T(8,128)(2,1)S(1)}, bf16[2,528,128]{2,1,0:T(8,128)(2,1)S(1)}, u32[]{:S(2)}, u32[]{:S(2)}) collective-permute-start(bf16[2,528,128]{2,1,0:T(8,128)(2,1)S(1)} %pad_maximum_fusion.1), channel_id=1, source_target_pairs={{0,64},{64,0},{128,192},{192,128},{256,320},{320,256},{384,448},{4... | collective-permute-start | bytes 811016 | tf_op jit(solution)/shard_map/ppermute | solution.py:65
  24.7 7.0 %collective-permute-done.5 = bf16[2,528,128]{2,1,0:T(8,128)(2,1)S(1)} collective-permute-done((bf16[2,528,128]{2,1,0:T(8,128)(2,1)S(1)}, bf16[2,528,128]{2,1,0:T(8,128)(2,1)S(1)}, u32[]{:S(2)}, u32[]{:S(2)}) %collective-permute-start.5) | collective-permute-done | bytes 270368 | tf_op jit(solution)/shard_map/ppermute | solution.py:65
  31.7 1.0 pad_maximum_fusion.refs_6_
  32.6 0.0 copy-start.3
  32.6 2.4 %collective-permute-start.6 = (bf16[4,528,128]{2,1,0:T(8,128)(2,1)S(1)}, bf16[4,528,128]{2,1,0:T(8,128)(2,1)S(1)}, u32[]{:S(2)}, u32[]{:S(2)}) collective-permute-start(bf16[4,528,128]{2,1,0:T(8,128)(2,1)S(1)} %pad_maximum_fusion.refs_6_), channel_id=1, source_target_pairs={{0,448},{64,128},{128,64},{192,256},{256,192},{320,384},{384,320},... | collective-permute-start | bytes 1622024 | tf_op jit(solution)/shard_map/ppermute | solution.py:65
  35.1 3.3 %all-to-all-done.refs_1_ = bf16[8,256,128]{2,1,0:T(8,128)(2,1)S(1)} async-done(((bf16[8,256,128]{2,1,0:T(8,128)(2,1)}), bf16[8,256,128]{2,1,0:T(8,128)(2,1)S(1)}, u32[]{:S(2)}, u32[]{:S(2)}) %all-to-all-start) | async-done | bytes 524320 | tf_op jit(solution)/shard_map/all_to_all | solution.py:271
  38.4 0.0 copy-start.4
  38.4 3.4 %collective-permute-start.1 = (bf16[8,256,128]{2,1,0:T(8,128)(2,1)S(1)}, bf16[8,256,128]{2,1,0:T(8,128)(2,1)S(1)}, u32[]{:S(2)}, u32[]{:S(2)}) collective-permute-start(bf16[8,256,128]{2,1,0:T(8,128)(2,1)S(1)} %all-to-all-done.refs_1_), channel_id=1, source_target_pairs={{0,24},{8,16},{16,8},{24,0},{1,25},{9,17},{17,9},{25,1},{2,26},{10... | collective-permute-start | bytes 1572872 | tf_op jit(solution)/shard_map/ppermute | solution.py:65
  41.8 3.7 %collective-permute-start = (bf16[8,256,128]{2,1,0:T(8,128)(2,1)S(1)}, bf16[8,256,128]{2,1,0:T(8,128)(2,1)S(1)}, u32[]{:S(2)}, u32[]{:S(2)}) collective-permute-start(bf16[8,256,128]{2,1,0:T(8,128)(2,1)S(1)} %all-to-all-done.refs_1_), channel_id=1, source_target_pairs={{0,8},{8,0},{16,24},{24,16},{1,9},{9,1},{17,25},{25,17},{2,10},{10... | collective-permute-start | bytes 1572872 | tf_op jit(solution)/shard_map/ppermute | solution.py:65
  45.6 1.9 %collective-permute-start.7 = (bf16[4,528,128]{2,1,0:T(8,128)(2,1)S(1)}, bf16[4,528,128]{2,1,0:T(8,128)(2,1)S(1)}, u32[]{:S(2)}, u32[]{:S(2)}) collective-permute-start(bf16[4,528,128]{2,1,0:T(8,128)(2,1)S(1)} %pad_maximum_fusion.refs_6_), channel_id=1, source_target_pairs={{0,32},{32,0},{1,33},{33,1},{2,34},{34,2},{3,35},{35,3},{4,36},{36... | collective-permute-start | bytes 1622024 | tf_op jit(solution)/shard_map/ppermute | solution.py:65
  47.5 0.8 collective-permute-done.6.refs_7_
  48.3 1.9 %collective-permute-start.8 = (bf16[4,528,128]{2,1,0:T(8,128)(2,1)S(1)}, bf16[4,528,128]{2,1,0:T(8,128)(2,1)}, u32[]{:S(2)}, u32[]{:S(2)}) collective-permute-start(bf16[4,528,128]{2,1,0:T(8,128)(2,1)S(1)} %collective-permute-done.6.refs_7_), channel_id=1, source_target_pairs={{0,32},{32,0},{1,33},{33,1},{2,34},{34,2},{3,35},{35,3},{4,36},{36... | collective-permute-start | bytes 1622024 | tf_op jit(solution)/shard_map/ppermute | solution.py:65
  50.2 3.0 %collective-permute-done.1.refs_3_ = bf16[8,256,128]{2,1,0:T(8,128)(2,1)S(1)} collective-permute-done((bf16[8,256,128]{2,1,0:T(8,128)(2,1)S(1)}, bf16[8,256,128]{2,1,0:T(8,128)(2,1)S(1)}, u32[]{:S(2)}, u32[]{:S(2)}) %collective-permute-start.1) | collective-permute-done | bytes 524320 | tf_op jit(solution)/shard_map/ppermute | solution.py:65
  53.2 0.8 slice.9
  53.9 3.6 %collective-permute-start.3 = (bf16[4,256,128]{2,1,0:T(8,128)(2,1)}, bf16[4,256,128]{2,1,0:T(8,128)(2,1)S(1)}, u32[]{:S(2)}, u32[]{:S(2)}) collective-permute-start(bf16[4,256,128]{2,1,0:T(8,128)(2,1)} %slice.9), channel_id=1, source_target_pairs={{0,8},{8,0},{16,24},{24,16},{1,9},{9,1},{17,25},{25,17},{2,10},{10... | collective-permute-start | bytes 786440 | tf_op jit(solution)/shard_map/ppermute | solution.py:65
  57.6 0.0 collective-permute-done.refs_2_
  57.6 0.0 copy-start.6
  57.6 0.8 slice.8
  58.4 4.2 %collective-permute-start.2 = (bf16[4,256,128]{2,1,0:T(8,128)(2,1)}, bf16[4,256,128]{2,1,0:T(8,128)(2,1)}, u32[]{:S(2)}, u32[]{:S(2)}) collective-permute-start(bf16[4,256,128]{2,1,0:T(8,128)(2,1)} %slice.8), channel_id=1, source_target_pairs={{0,24},{8,16},{16,8},{24,0},{1,25},{9,17},{17,9},{25,1},{2,26},{10... | collective-permute-start | bytes 786440 | tf_op jit(solution)/shard_map/ppermute | solution.py:65
  62.5 0.6 pad_add_fusion.refs_0_
  63.1 0.0 collective-permute-done.7.refs_8_
  63.1 0.0 collective-permute-done.8.refs_9_
  63.1 0.0 collective-permute-done.3.refs_5_
  63.1 0.0 copy-start.9
  63.2 4.1 %collective-permute-done.2.refs_4_ = bf16[4,256,128]{2,1,0:T(8,128)(2,1)} collective-permute-done((bf16[4,256,128]{2,1,0:T(8,128)(2,1)}, bf16[4,256,128]{2,1,0:T(8,128)(2,1)}, u32[]{:S(2)}, u32[]{:S(2)}) %collective-permute-start.2) | collective-permute-done | bytes 262176 | tf_op jit(solution)/shard_map/ppermute | solution.py:65
  67.2 0.0 copy-done.3
  67.2 0.0 copy-done.4
  67.2 0.0 copy-done.7
  67.2 0.0 copy-done.5
  67.2 0.0 copy-done.6
  67.3 0.0 copy-done.8
  67.3 0.0 copy-done.9
  67.3 9.9 %shard_map.94 = (bf16[256,512]{1,0:T(8,128)(2,1)}, bf16[2,8,256,128]{3,2,1,0:T(8,128)(2,1)}, bf16[2,8,256,128]{3,2,1,0:T(8,128)(2,1)}, bf16[4,8,256,128]{3,2,1,0:T(8,128)(2,1)}) custom-call(s32[3]{0:T(128)} %pad_add_fusion.refs_0_, bf16[8,256,128]{2,1,0:T(8,128)(2,1)} %copy-done.4, bf16[8,256,128]{2,1,0:T(8,128)(2,1)} %copy-done.6, ...), custom_call_target="tpu_custom_call" | custom-call | tf_op jit(solution)/shard_map/pallas_call | solution.py:281
  77.2 0.0 copy-start
  77.2 5.5 %all-to-all-start.1 = ((bf16[4,8,256,128]{3,2,1,0:T(8,128)(2,1)}), bf16[4,8,256,128]{3,2,1,0:T(8,128)(2,1)S(1)}, u32[]{:S(2)}, u32[]{:S(2)}) async-start(bf16[4,8,256,128]{3,2,1,0:T(8,128)(2,1)} %get-tuple-element.25), calls=%async_computation.1 | async-start | bytes 4194304 | tf_op jit(solution)/shard_map/all_to_all | solution.py:306
  82.7 1.9 %collective-permute-start.9 = (bf16[2,8,256,128]{3,2,1,0:T(8,128)(2,1)}, bf16[2,8,256,128]{3,2,1,0:T(8,128)(2,1)S(1)}, u32[]{:S(2)}, u32[]{:S(2)}) collective-permute-start(bf16[2,8,256,128]{3,2,1,0:T(8,128)(2,1)} %get-tuple-element.27), channel_id=1, source_target_pairs={{0,32},{32,0},{1,33},{33,1},{2,34},{34,2},{3,35},{35,3},{4,36},{36... | collective-permute-start | bytes 3145736 | tf_op jit(solution)/shard_map/ppermute | solution.py:65
  84.6 2.8 %collective-permute-done.9.other = bf16[2,8,256,128]{3,2,1,0:T(8,128)(2,1)S(1)} collective-permute-done((bf16[2,8,256,128]{3,2,1,0:T(8,128)(2,1)}, bf16[2,8,256,128]{3,2,1,0:T(8,128)(2,1)S(1)}, u32[]{:S(2)}, u32[]{:S(2)}) %collective-permute-start.9) | collective-permute-done | bytes 1048608 | tf_op jit(solution)/shard_map/ppermute | solution.py:65
  87.4 0.0 copy-done
  87.4 0.2 shard_map.95
  87.7 2.3 %collective-permute-start.10 = (bf16[4,256,128]{2,1,0:T(8,128)(2,1)S(1)}, bf16[4,256,128]{2,1,0:T(8,128)(2,1)S(1)}, u32[]{:S(2)}, u32[]{:S(2)}) collective-permute-start(bf16[4,256,128]{2,1,0:T(8,128)(2,1)S(1)} %get-tuple-element.29), channel_id=1, source_target_pairs={{0,448},{64,128},{128,64},{192,256},{256,192},{320,384},{384,320},... | collective-permute-start | bytes 786440 | tf_op jit(solution)/shard_map/ppermute | solution.py:65
  90.0 2.8 %collective-permute-start.11 = (bf16[4,256,128]{2,1,0:T(8,128)(2,1)S(1)}, bf16[4,256,128]{2,1,0:T(8,128)(2,1)S(1)}, u32[]{:S(2)}, u32[]{:S(2)}) collective-permute-start(bf16[4,256,128]{2,1,0:T(8,128)(2,1)S(1)} %get-tuple-element.31), channel_id=1, source_target_pairs={{0,64},{64,0},{128,192},{192,128},{256,320},{320,256},{384,448},{4... | collective-permute-start | bytes 786440 | tf_op jit(solution)/shard_map/ppermute | solution.py:65
  92.8 6.4 %collective-permute-done.10.from_g = bf16[4,256,128]{2,1,0:T(8,128)(2,1)S(1)} collective-permute-done((bf16[4,256,128]{2,1,0:T(8,128)(2,1)S(1)}, bf16[4,256,128]{2,1,0:T(8,128)(2,1)S(1)}, u32[]{:S(2)}, u32[]{:S(2)}) %collective-permute-start.10) | collective-permute-done | bytes 262176 | tf_op jit(solution)/shard_map/ppermute | solution.py:65
  99.1 0.8 collective-permute-done.11.from_u
  100.0 0.1 shard_map.96
  100.1 2.8 %collective-permute-start.12 = (bf16[2,256,128]{2,1,0:T(8,128)(2,1)S(1)}, bf16[2,256,128]{2,1,0:T(8,128)(2,1)S(1)}, u32[]{:S(2)}, u32[]{:S(2)}) collective-permute-start(bf16[2,256,128]{2,1,0:T(8,128)(2,1)S(1)} %get-tuple-element.33), channel_id=1, source_target_pairs={{0,64},{64,0},{128,192},{192,128},{256,320},{320,256},{384,448},{4... | collective-permute-start | bytes 393224 | tf_op jit(solution)/shard_map/ppermute | solution.py:65
  102.8 4.2 %collective-permute-start.13 = (bf16[2,256,128]{2,1,0:T(8,128)(2,1)S(1)}, bf16[2,256,128]{2,1,0:T(8,128)(2,1)S(1)}, u32[]{:S(2)}, u32[]{:S(2)}) collective-permute-start(bf16[2,256,128]{2,1,0:T(8,128)(2,1)S(1)} %get-tuple-element.35), channel_id=1, source_target_pairs={{0,448},{64,128},{128,64},{192,256},{256,192},{320,384},{384,320},... | collective-permute-start | bytes 393224 | tf_op jit(solution)/shard_map/ppermute | solution.py:65
  107.0 0.0 collective-permute-done.12.from_g
  107.0 3.9 %collective-permute-done.13.from_u = bf16[2,256,128]{2,1,0:T(8,128)(2,1)S(1)} collective-permute-done((bf16[2,256,128]{2,1,0:T(8,128)(2,1)S(1)}, bf16[2,256,128]{2,1,0:T(8,128)(2,1)S(1)}, u32[]{:S(2)}, u32[]{:S(2)}) %collective-permute-start.13) | collective-permute-done | bytes 131104 | tf_op jit(solution)/shard_map/ppermute | solution.py:65
  110.9 0.1 shard_map.97
  111.0 0.0 all-to-all-done.1.t_ref
  111.0 1.1 shard_map.98
  112.0 7.4 %all-to-all-start.2 = ((bf16[8,256,128]{2,1,0:T(8,128)(2,1)}), bf16[8,256,128]{2,1,0:T(8,128)(2,1)S(1)}, u32[]{:S(2)}, u32[]{:S(2)}) async-start(bf16[8,256,128]{2,1,0:T(8,128)(2,1)} %shard_map.98), calls=%async_computation.2 | async-start | bytes 1048576 | tf_op jit(solution)/shard_map/all_to_all | solution.py:316
  119.4 4.3 %collective-permute-start.14 = (bf16[2,256,128]{2,1,0:T(8,128)(2,1)S(1)}, bf16[2,256,128]{2,1,0:T(8,128)(2,1)S(1)}, u32[]{:S(2)}, u32[]{:S(2)}) collective-permute-start(bf16[2,256,128]{2,1,0:T(8,128)(2,1)S(1)} %get-tuple-element.37), channel_id=1, source_target_pairs={{0,256},{64,320},{128,384},{192,448},{256,0},{320,64},{384,128},{4... | collective-permute-start | bytes 393224 | tf_op jit(solution)/shard_map/ppermute | solution.py:65
  123.7 7.6 %collective-permute-done.14.b_ref = bf16[2,256,128]{2,1,0:T(8,128)(2,1)S(1)} collective-permute-done((bf16[2,256,128]{2,1,0:T(8,128)(2,1)S(1)}, bf16[2,256,128]{2,1,0:T(8,128)(2,1)S(1)}, u32[]{:S(2)}, u32[]{:S(2)}) %collective-permute-start.14) | collective-permute-done | bytes 131104 | tf_op jit(solution)/shard_map/ppermute | solution.py:65
  131.3 0.0 copy-done.1
  131.3 0.0 copy-done.2
  131.3 1.6 %shard_map.100 = (bf16[256,512]{1,0:T(8,128)(2,1)}, bf16[256,512]{1,0:T(8,128)(2,1)}) custom-call(s32[2,4]{1,0:T(2,128)S(1)} %copy-done.1, s32[2,4]{1,0:T(2,128)S(1)} %copy-done.2, bf16[2,256,128]{2,1,0:T(8,128)(2,1)S(1)} %get-tuple-element.36._.a_ref, bf16[2,256,128]{2,1,0:T(8,128)(2,1)S(1)} %collective-permute-done.14.b_ref), custom_call_target="tpu_custom_call" | custom-call | tf_op jit(solution)/shard_map/pallas_call | solution.py:319
  132.9 2.1 %all-to-all-done.2.a_ref = bf16[8,256,128]{2,1,0:T(8,128)(2,1)S(1)} async-done(((bf16[8,256,128]{2,1,0:T(8,128)(2,1)}), bf16[8,256,128]{2,1,0:T(8,128)(2,1)S(1)}, u32[]{:S(2)}, u32[]{:S(2)}) %all-to-all-start.2) | async-done | bytes 524320 | tf_op jit(solution)/shard_map/all_to_all | solution.py:316
  134.9 0.7 shard_map.99
  (5 shorter events, 0.0 us)
Async XLA Ops:
  3.1 18.1 %collective-permute-start.4 = (bf16[1,528,128]{2,1,0:T(8,128)(2,1)}, bf16[1,528,128]{2,1,0:T(8,128)(2,1)S(1)}, u32[]{:S(2)}, u32[]{:S(2)}) collective-permute-start(bf16[1,528,128]{2,1,0:T(8,128)(2,1)} %bitcast.4), channel_id=1, source_target_pairs={{0,256},{64,320},{128,384},{192,448},{256,0},{320,64},{384,128},{4... | collective-permute-start | bytes 405512 | tf_op jit(solution)/shard_map/ppermute | solution.py:65
  10.8 27.5 %all-to-all-start = ((bf16[8,256,128]{2,1,0:T(8,128)(2,1)}), bf16[8,256,128]{2,1,0:T(8,128)(2,1)S(1)}, u32[]{:S(2)}, u32[]{:S(2)}) async-start(bf16[8,256,128]{2,1,0:T(8,128)(2,1)} %get-tuple-element.22), calls=%async_computation | async-start | bytes 1048576 | tf_op jit(solution)/shard_map/all_to_all | solution.py:271
  22.1 9.5 %collective-permute-start.5 = (bf16[2,528,128]{2,1,0:T(8,128)(2,1)S(1)}, bf16[2,528,128]{2,1,0:T(8,128)(2,1)S(1)}, u32[]{:S(2)}, u32[]{:S(2)}) collective-permute-start(bf16[2,528,128]{2,1,0:T(8,128)(2,1)S(1)} %pad_maximum_fusion.1), channel_id=1, source_target_pairs={{0,64},{64,0},{128,192},{192,128},{256,320},{320,256},{384,448},{4... | collective-permute-start | bytes 811016 | tf_op jit(solution)/shard_map/ppermute | solution.py:65
  32.6 34.6 %copy-start.3 = (bf16[4,528,128]{2,1,0:T(8,128)(2,1)}, bf16[4,528,128]{2,1,0:T(8,128)(2,1)S(1)}, u32[]{:S(2)}) copy-start(bf16[4,528,128]{2,1,0:T(8,128)(2,1)S(1)} %pad_maximum_fusion.refs_6_) | copy-start | bytes 1622020
  32.6 15.6 %collective-permute-start.6 = (bf16[4,528,128]{2,1,0:T(8,128)(2,1)S(1)}, bf16[4,528,128]{2,1,0:T(8,128)(2,1)S(1)}, u32[]{:S(2)}, u32[]{:S(2)}) collective-permute-start(bf16[4,528,128]{2,1,0:T(8,128)(2,1)S(1)} %pad_maximum_fusion.refs_6_), channel_id=1, source_target_pairs={{0,448},{64,128},{128,64},{192,256},{256,192},{320,384},{384,320},... | collective-permute-start | bytes 1622024 | tf_op jit(solution)/shard_map/ppermute | solution.py:65
  38.4 28.9 %copy-start.4 = (bf16[8,256,128]{2,1,0:T(8,128)(2,1)}, bf16[8,256,128]{2,1,0:T(8,128)(2,1)S(1)}, u32[]{:S(2)}) copy-start(bf16[8,256,128]{2,1,0:T(8,128)(2,1)S(1)} %all-to-all-done.refs_1_) | copy-start | bytes 1572868
  38.4 14.8 %collective-permute-start.1 = (bf16[8,256,128]{2,1,0:T(8,128)(2,1)S(1)}, bf16[8,256,128]{2,1,0:T(8,128)(2,1)S(1)}, u32[]{:S(2)}, u32[]{:S(2)}) collective-permute-start(bf16[8,256,128]{2,1,0:T(8,128)(2,1)S(1)} %all-to-all-done.refs_1_), channel_id=1, source_target_pairs={{0,24},{8,16},{16,8},{24,0},{1,25},{9,17},{17,9},{25,1},{2,26},{10... | collective-permute-start | bytes 1572872 | tf_op jit(solution)/shard_map/ppermute | solution.py:65
  41.8 15.7 %collective-permute-start = (bf16[8,256,128]{2,1,0:T(8,128)(2,1)S(1)}, bf16[8,256,128]{2,1,0:T(8,128)(2,1)S(1)}, u32[]{:S(2)}, u32[]{:S(2)}) collective-permute-start(bf16[8,256,128]{2,1,0:T(8,128)(2,1)S(1)} %all-to-all-done.refs_1_), channel_id=1, source_target_pairs={{0,8},{8,0},{16,24},{24,16},{1,9},{9,1},{17,25},{25,17},{2,10},{10... | collective-permute-start | bytes 1572872 | tf_op jit(solution)/shard_map/ppermute | solution.py:65
  45.6 17.6 %collective-permute-start.7 = (bf16[4,528,128]{2,1,0:T(8,128)(2,1)S(1)}, bf16[4,528,128]{2,1,0:T(8,128)(2,1)S(1)}, u32[]{:S(2)}, u32[]{:S(2)}) collective-permute-start(bf16[4,528,128]{2,1,0:T(8,128)(2,1)S(1)} %pad_maximum_fusion.refs_6_), channel_id=1, source_target_pairs={{0,32},{32,0},{1,33},{33,1},{2,34},{34,2},{3,35},{35,3},{4,36},{36... | collective-permute-start | bytes 1622024 | tf_op jit(solution)/shard_map/ppermute | solution.py:65
  48.3 19.0 %copy-start.7 = (bf16[4,528,128]{2,1,0:T(8,128)(2,1)}, bf16[4,528,128]{2,1,0:T(8,128)(2,1)S(1)}, u32[]{:S(2)}) copy-start(bf16[4,528,128]{2,1,0:T(8,128)(2,1)S(1)} %collective-permute-done.6.refs_7_) | copy-start | bytes 1622020
  48.3 14.9 %collective-permute-start.8 = (bf16[4,528,128]{2,1,0:T(8,128)(2,1)S(1)}, bf16[4,528,128]{2,1,0:T(8,128)(2,1)}, u32[]{:S(2)}, u32[]{:S(2)}) collective-permute-start(bf16[4,528,128]{2,1,0:T(8,128)(2,1)S(1)} %collective-permute-done.6.refs_7_), channel_id=1, source_target_pairs={{0,32},{32,0},{1,33},{33,1},{2,34},{34,2},{3,35},{35,3},{4,36},{36... | collective-permute-start | bytes 1622024 | tf_op jit(solution)/shard_map/ppermute | solution.py:65
  53.2 14.1 %copy-start.5 = (bf16[8,256,128]{2,1,0:T(8,128)(2,1)}, bf16[8,256,128]{2,1,0:T(8,128)(2,1)S(1)}, u32[]{:S(2)}) copy-start(bf16[8,256,128]{2,1,0:T(8,128)(2,1)S(1)} %collective-permute-done.1.refs_3_) | copy-start | bytes 1572868
  53.9 9.2 %collective-permute-start.3 = (bf16[4,256,128]{2,1,0:T(8,128)(2,1)}, bf16[4,256,128]{2,1,0:T(8,128)(2,1)S(1)}, u32[]{:S(2)}, u32[]{:S(2)}) collective-permute-start(bf16[4,256,128]{2,1,0:T(8,128)(2,1)} %slice.9), channel_id=1, source_target_pairs={{0,8},{8,0},{16,24},{24,16},{1,9},{9,1},{17,25},{25,17},{2,10},{10... | collective-permute-start | bytes 786440 | tf_op jit(solution)/shard_map/ppermute | solution.py:65
  57.6 9.7 %copy-start.6 = (bf16[8,256,128]{2,1,0:T(8,128)(2,1)}, bf16[8,256,128]{2,1,0:T(8,128)(2,1)S(1)}, u32[]{:S(2)}) copy-start(bf16[8,256,128]{2,1,0:T(8,128)(2,1)S(1)} %collective-permute-done.refs_2_) | copy-start | bytes 1572868
  58.4 8.9 %collective-permute-start.2 = (bf16[4,256,128]{2,1,0:T(8,128)(2,1)}, bf16[4,256,128]{2,1,0:T(8,128)(2,1)}, u32[]{:S(2)}, u32[]{:S(2)}) collective-permute-start(bf16[4,256,128]{2,1,0:T(8,128)(2,1)} %slice.8), channel_id=1, source_target_pairs={{0,24},{8,16},{16,8},{24,0},{1,25},{9,17},{17,9},{25,1},{2,26},{10... | collective-permute-start | bytes 786440 | tf_op jit(solution)/shard_map/ppermute | solution.py:65
  63.1 4.1 %copy-start.8 = (bf16[4,528,128]{2,1,0:T(8,128)(2,1)}, bf16[4,528,128]{2,1,0:T(8,128)(2,1)S(1)}, u32[]{:S(2)}) copy-start(bf16[4,528,128]{2,1,0:T(8,128)(2,1)S(1)} %collective-permute-done.7.refs_8_) | copy-start | bytes 1622020
  63.1 4.1 %copy-start.9 = (bf16[4,256,128]{2,1,0:T(8,128)(2,1)}, bf16[4,256,128]{2,1,0:T(8,128)(2,1)S(1)}, u32[]{:S(2)}) copy-start(bf16[4,256,128]{2,1,0:T(8,128)(2,1)S(1)} %collective-permute-done.3.refs_5_) | copy-start | bytes 786436
  77.2 10.2 %copy-start = (bf16[2,8,256,128]{3,2,1,0:T(8,128)(2,1)S(1)}, bf16[2,8,256,128]{3,2,1,0:T(8,128)(2,1)}, u32[]{:S(2)}) copy-start(bf16[2,8,256,128]{3,2,1,0:T(8,128)(2,1)} %get-tuple-element.26.keep) | copy-start | bytes 3145732
  77.2 33.8 %all-to-all-start.1 = ((bf16[4,8,256,128]{3,2,1,0:T(8,128)(2,1)}), bf16[4,8,256,128]{3,2,1,0:T(8,128)(2,1)S(1)}, u32[]{:S(2)}, u32[]{:S(2)}) async-start(bf16[4,8,256,128]{3,2,1,0:T(8,128)(2,1)} %get-tuple-element.25), calls=%async_computation.1 | async-start | bytes 4194304 | tf_op jit(solution)/shard_map/all_to_all | solution.py:306
  82.7 4.8 %collective-permute-start.9 = (bf16[2,8,256,128]{3,2,1,0:T(8,128)(2,1)}, bf16[2,8,256,128]{3,2,1,0:T(8,128)(2,1)S(1)}, u32[]{:S(2)}, u32[]{:S(2)}) collective-permute-start(bf16[2,8,256,128]{3,2,1,0:T(8,128)(2,1)} %get-tuple-element.27), channel_id=1, source_target_pairs={{0,32},{32,0},{1,33},{33,1},{2,34},{34,2},{3,35},{35,3},{4,36},{36... | collective-permute-start | bytes 3145736 | tf_op jit(solution)/shard_map/ppermute | solution.py:65
  87.7 11.5 %collective-permute-start.10 = (bf16[4,256,128]{2,1,0:T(8,128)(2,1)S(1)}, bf16[4,256,128]{2,1,0:T(8,128)(2,1)S(1)}, u32[]{:S(2)}, u32[]{:S(2)}) collective-permute-start(bf16[4,256,128]{2,1,0:T(8,128)(2,1)S(1)} %get-tuple-element.29), channel_id=1, source_target_pairs={{0,448},{64,128},{128,64},{192,256},{256,192},{320,384},{384,320},... | collective-permute-start | bytes 786440 | tf_op jit(solution)/shard_map/ppermute | solution.py:65
  90.0 10.0 %collective-permute-start.11 = (bf16[4,256,128]{2,1,0:T(8,128)(2,1)S(1)}, bf16[4,256,128]{2,1,0:T(8,128)(2,1)S(1)}, u32[]{:S(2)}, u32[]{:S(2)}) collective-permute-start(bf16[4,256,128]{2,1,0:T(8,128)(2,1)S(1)} %get-tuple-element.31), channel_id=1, source_target_pairs={{0,64},{64,0},{128,192},{192,128},{256,320},{320,256},{384,448},{4... | collective-permute-start | bytes 786440 | tf_op jit(solution)/shard_map/ppermute | solution.py:65
  100.1 7.0 %collective-permute-start.12 = (bf16[2,256,128]{2,1,0:T(8,128)(2,1)S(1)}, bf16[2,256,128]{2,1,0:T(8,128)(2,1)S(1)}, u32[]{:S(2)}, u32[]{:S(2)}) collective-permute-start(bf16[2,256,128]{2,1,0:T(8,128)(2,1)S(1)} %get-tuple-element.33), channel_id=1, source_target_pairs={{0,64},{64,0},{128,192},{192,128},{256,320},{320,256},{384,448},{4... | collective-permute-start | bytes 393224 | tf_op jit(solution)/shard_map/ppermute | solution.py:65
  102.8 8.1 %collective-permute-start.13 = (bf16[2,256,128]{2,1,0:T(8,128)(2,1)S(1)}, bf16[2,256,128]{2,1,0:T(8,128)(2,1)S(1)}, u32[]{:S(2)}, u32[]{:S(2)}) collective-permute-start(bf16[2,256,128]{2,1,0:T(8,128)(2,1)S(1)} %get-tuple-element.35), channel_id=1, source_target_pairs={{0,448},{64,128},{128,64},{192,256},{256,192},{320,384},{384,320},... | collective-permute-start | bytes 393224 | tf_op jit(solution)/shard_map/ppermute | solution.py:65
  110.9 20.3 %copy-start.1 = (s32[2,4]{1,0:T(2,128)S(1)}, s32[2,4]{1,0:T(2,128)}, u32[]{:S(2)}) copy-start(s32[2,4]{1,0:T(2,128)} %gm_ref.3) | copy-start | bytes 100
  110.9 20.3 %copy-start.2 = (s32[2,4]{1,0:T(2,128)S(1)}, s32[2,4]{1,0:T(2,128)}, u32[]{:S(2)}) copy-start(s32[2,4]{1,0:T(2,128)} %um_ref.3) | copy-start | bytes 100
  112.0 22.9 %all-to-all-start.2 = ((bf16[8,256,128]{2,1,0:T(8,128)(2,1)}), bf16[8,256,128]{2,1,0:T(8,128)(2,1)S(1)}, u32[]{:S(2)}, u32[]{:S(2)}) async-start(bf16[8,256,128]{2,1,0:T(8,128)(2,1)} %shard_map.98), calls=%async_computation.2 | async-start | bytes 1048576 | tf_op jit(solution)/shard_map/all_to_all | solution.py:316
  119.4 11.8 %collective-permute-start.14 = (bf16[2,256,128]{2,1,0:T(8,128)(2,1)S(1)}, bf16[2,256,128]{2,1,0:T(8,128)(2,1)S(1)}, u32[]{:S(2)}, u32[]{:S(2)}) collective-permute-start(bf16[2,256,128]{2,1,0:T(8,128)(2,1)S(1)} %get-tuple-element.37), channel_id=1, source_target_pairs={{0,256},{64,320},{128,384},{192,448},{256,0},{320,64},{384,128},{4... | collective-permute-start | bytes 393224 | tf_op jit(solution)/shard_map/ppermute | solution.py:65

commit v8 on v7

--- a/solution.py
+++ b/solution.py
@@ -72,14 +72,13 @@
     return i
 
 
-def pack_kernel(gm_ref, um_ref, tok_ref, gw_ref, uw_ref, out_ref, all_ref, gm, um, sems):
+def pack_kernel(gm_ref, um_ref, gw_ref, uw_ref, out_ref, gm, um, sems):
     cols = gm.shape[1]
-    tokens = pltpu.make_async_copy(tok_ref, all_ref.at[0], sems.at[0])
     masks = [
-        pltpu.make_async_copy(a, b, sems.at[1 + t])
+        pltpu.make_async_copy(a, b, sems.at[t])
         for t, (a, b) in enumerate(((gm_ref, gm), (um_ref, um)))
     ]
-    for copy in masks + [tokens]:
+    for copy in masks:
         copy.start()
     for copy in masks:
         copy.wait()
@@ -90,7 +89,7 @@
             r, c = block_of(w_ref, p, cols)
             place = pl.ds((2 * t + s) * BLK, BLK)
             copy = pltpu.make_async_copy(
-                w_ref.at[pl.ds(r, BLK), pl.ds(c, BLK)], out_ref.at[place], sems.at[3 + 2 * t + s]
+                w_ref.at[pl.ds(r, BLK), pl.ds(c, BLK)], out_ref.at[place], sems.at[2 + 2 * t + s]
             )
             copy.start()
             chosen.append((p, on, place, copy))
@@ -99,9 +98,6 @@
     for s, (p, _, _, _) in enumerate(chosen):
         meta = jnp.where(lane == s, p, meta)
     out_ref[pl.ds(META, lane.shape[0]), :] = meta.astype(F32).astype(BF)
-    tokens.wait()
-    for z in range(1, all_ref.shape[0]):
-        all_ref[z] = all_ref[0]
     for _, on, place, copy in chosen:
         copy.wait()
 
@@ -113,7 +109,7 @@
 def main_kernel(blocks, me_ref, own, r1, r2, oa, ob, w0, w1, w2, w3, cot_ref, *rest):
     hid_ref, keep_ref, send_ref, t_ref = rest[:4]
     x_ref, w_ref, metas, at_vec, at_ref, idx_ref, acc, g_ref, gt, sem, sems = rest[4:]
-    my_x, my_c, my_y = me_ref[0], me_ref[1], me_ref[2]
+    my_x, my_c, my_y, my_z = (me_ref[i] for i in range(4))
     shards = w_ref.shape[0]
     ys, zs, half = shards // 2, own.shape[0], oa.shape[0]
     count = w0.shape[0]
@@ -131,9 +127,11 @@
     xs = 2 * shards // zs
     far, one, two = ((turn(my_x, stage, xs)) for stage in ("far", "one", "two"))
     parts = ((own, my_x, 0), (r1, one, 0), (r2, two, 0), (oa, far, 0), (ob, far, half))
-    for k, (part, x, z) in enumerate(parts):
-        place = x_ref.at[pl.ds(x * zs + z, part.shape[0])]
-        large.append(pltpu.make_async_copy(part, place, sems.at[2, k]))
+    moves = [(part, i, x, z + i) for part, x, z in parts for i in range(part.shape[0])]
+    for k, (part, i, x, j) in enumerate(moves):
+        place = x_ref.at[x * zs + origin(my_z, j, zs)]
+        sem_k = sems.at[2 + k // shards, k % shards]
+        large.append(pltpu.make_async_copy(part.at[i], place, sem_k))
         large[-1].start()
     for k, copy in enumerate(small):
         copy.wait()
@@ -255,20 +253,22 @@
     blocks = gate_mask.shape[1]
     half = zs // 2
     shape = jax.ShapeDtypeStruct
-    me = jnp.stack([lax.axis_index(a) for a in ("x", "c", "y")]).astype(jnp.int32)
-
-    packed, own = call(
+    me = jnp.stack([lax.axis_index(a) for a in ("x", "c", "y", "z")]).astype(jnp.int32)
+
+    packed = call(
         pack_kernel,
-        (shape((META + 16, BLK), BF), shape((zs, tok, BLK), BF)),
-        [HBM] * 5,
+        shape((META + 16, BLK), BF),
+        [HBM] * 4,
         [
             pltpu.SMEM(gate_mask.shape, jnp.int32),
             pltpu.SMEM(up_mask.shape, jnp.int32),
-            pltpu.SemaphoreType.DMA((3 + SLOTS,)),
+            pltpu.SemaphoreType.DMA((2 + SLOTS,)),
         ],
         limit=60,
-    )(gate_mask, up_mask, tokens, gate_weight, up_weight)
-    own = lax.all_to_all(own, "z", 0, 0)
+    )(gate_mask, up_mask, gate_weight, up_weight)
+    own = tokens[None]
+    for stage in stages(zs):
+        own = jnp.concatenate([own, swap(own, "z", stage)])
     w = packed[None]
     *early, late = stages(ys)
     for stage in early:
@@ -298,7 +298,7 @@
             pltpu.VMEM((2 * blocks, tok, BLK), BF),
             pltpu.VMEM((2 * blocks, BLK, tok), BF),
             pltpu.SemaphoreType.DMA(()),
-            pltpu.SemaphoreType.DMA((3, 2 * ys)),
+            pltpu.SemaphoreType.DMA((4, 2 * ys)),
         ],
         limit=58,
     )(me, own, r1, r2, oa, ob, *w, cotangent)

time: 136 us -> 143 us (1.051)
  starting transfers between devices: 72.8 us -> 83.2 us
  waiting for transfers between devices: 41.7 us -> 35.2 us
  other arithmetic: 2.48 us -> 4.33 us
    ppermute x15 -> x18, starting transfers between devices: 49.7 us -> 73.7 us  [swap(): lax.ppermute(x, axis, [(i, turn(i, stage, size)) for i in range(size)])]
    all_to_all x2 -> x1, starting transfers between devices: 17.7 us -> 3.49 us  [body(): own = lax.all_to_all(own, 'z', 0, 0)]
    ppermute x15 -> x18, waiting for transfers between devices: 36.3 us -> 32.7 us  [swap(): lax.ppermute(x, axis, [(i, turn(i, stage, size)) for i in range(size)])]
    all_to_all x2 -> x1, waiting for transfers between devices: 5.38 us -> 2.55 us  [body(): own = lax.all_to_all(own, 'z', 0, 0)]
    concatenate x0 -> x3, other arithmetic: none -> 1.78 us  [body(): own = jnp.concatenate([own, swap(own, 'z', stage)])]
  transfers between devices with their start and end apart: 18 -> 20, of which waited for: 11 -> 12; matrix products, arithmetic and copies ran while one was open for 3% -> 4% of each run, Pallas kernels for 1% -> 1%
where the time goes in v8:
time: 143 us; the launch traced here: 142 us
  starting transfers between devices  83.2 us (58%)
  waiting for transfers between devices  35.2 us (25%)
  Pallas kernels  16.3 us (11%)
  other arithmetic  4.33 us (3%)
  local copies, waits for them, and re-layouts  1.58 us (1%)
    ppermute x18, starting transfers between devices, swap(): lax.ppermute(x, axis, [(i, turn(i, stage, size)) for i in range(size)])  73.7 us
    ppermute x18, waiting for transfers between devices, swap(): lax.ppermute(x, axis, [(i, turn(i, stage, size)) for i in range(size)])  32.7 us
    pallas_call x1, Pallas kernels, body(): call(lambda *refs: main_kernel(blocks, *refs), (shape((tok, width), BF),...  10 us
    all_to_all x1, starting transfers between devices, body(): terms = lax.all_to_all(terms, 'x', 0, 0)  6.01 us
    all_to_all x1, starting transfers between devices, body(): own = lax.all_to_all(own, 'z', 0, 0)  3.49 us
  transfers between devices with their start and end apart: 20, of which 12 were waited for; matrix products, arithmetic and copies ran while one was open for 4% of the time, Pallas kernels for 1%

profile of v8, /device:TPU:2, one launch (start us, length us, event | category | flops | bytes accessed | tf_op | source)
XLA Modules:
  0.0 141.6 jit_solution(3960522694366772835)
XLA Ops:
  0.6 0.0 copy-start.7
  0.6 2.4 %shard_map.93 = bf16[528,128]{1,0:T(8,128)(2,1)} custom-call(s32[2,4]{1,0:T(2,128)} %gm_ref.3, s32[2,4]{1,0:T(2,128)} %um_ref.3, bf16[256,512]{1,0:T(8,128)(2,1)} %gw_ref.1, bf16[256,512]{1,0:T(8,128)(2,1)} %uw_ref.1), custom_call_target="tpu_custom_call" | custom-call | tf_op jit(solution)/shard_map/pallas_call | solution.py:258
  3.0 7.7 %collective-permute-start.7 = (bf16[1,528,128]{2,1,0:T(8,128)(2,1)}, bf16[1,528,128]{2,1,0:T(8,128)(2,1)S(1)}, u32[]{:S(2)}, u32[]{:S(2)}) collective-permute-start(bf16[1,528,128]{2,1,0:T(8,128)(2,1)} %bitcast.6), channel_id=1, source_target_pairs={{0,256},{64,320},{128,384},{192,448},{256,0},{320,64},{384,128},{4... | collective-permute-start | bytes 405512 | tf_op jit(solution)/shard_map/ppermute | solution.py:65
  10.8 10.9 %collective-permute-start = (bf16[1,256,128]{2,1,0:T(8,128)(2,1)}, bf16[1,256,128]{2,1,0:T(8,128)(2,1)S(1)}, u32[]{:S(2)}, u32[]{:S(2)}) collective-permute-start(bf16[1,256,128]{2,1,0:T(8,128)(2,1)} %bitcast.9), channel_id=1, source_target_pairs={{0,4},{1,5},{2,6},{3,7},{4,0},{5,1},{6,2},{7,3},{8,12},{9,13},{10,... | collective-permute-start | bytes 196616 | tf_op jit(solution)/shard_map/ppermute | solution.py:65
  21.7 0.0 collective-permute-done.7
  21.7 0.9 pad_maximum_fusion.2
  22.7 2.6 %collective-permute-start.8 = (bf16[2,528,128]{2,1,0:T(8,128)(2,1)S(1)}, bf16[2,528,128]{2,1,0:T(8,128)(2,1)S(1)}, u32[]{:S(2)}, u32[]{:S(2)}) collective-permute-start(bf16[2,528,128]{2,1,0:T(8,128)(2,1)S(1)} %pad_maximum_fusion.2), channel_id=1, source_target_pairs={{0,64},{64,0},{128,192},{192,128},{256,320},{320,256},{384,448},{4... | collective-permute-start | bytes 811016 | tf_op jit(solution)/shard_map/ppermute | solution.py:65
  25.2 0.0 collective-permute-done
  25.3 0.9 pad_maximum_fusion.4
  26.1 3.4 %collective-permute-start.1 = (bf16[2,256,128]{2,1,0:T(8,128)(2,1)S(1)}, bf16[2,256,128]{2,1,0:T(8,128)(2,1)S(1)}, u32[]{:S(2)}, u32[]{:S(2)}) collective-permute-start(bf16[2,256,128]{2,1,0:T(8,128)(2,1)S(1)} %pad_maximum_fusion.4), channel_id=1, source_target_pairs={{0,1},{1,0},{2,3},{3,2},{4,5},{5,4},{6,7},{7,6},{8,9},{9,8},{10,11... | collective-permute-start | bytes 393224 | tf_op jit(solution)/shard_map/ppermute | solution.py:65
  29.5 3.5 %collective-permute-done.1 = bf16[2,256,128]{2,1,0:T(8,128)(2,1)S(1)} collective-permute-done((bf16[2,256,128]{2,1,0:T(8,128)(2,1)S(1)}, bf16[2,256,128]{2,1,0:T(8,128)(2,1)S(1)}, u32[]{:S(2)}, u32[]{:S(2)}) %collective-permute-start.1) | collective-permute-done | bytes 131104 | tf_op jit(solution)/shard_map/ppermute | solution.py:65
  33.0 0.9 pad_maximum_fusion.3
  33.8 7.3 %collective-permute-start.2 = (bf16[4,256,128]{2,1,0:T(8,128)(2,1)S(1)}, bf16[4,256,128]{2,1,0:T(8,128)(2,1)S(1)}, u32[]{:S(2)}, u32[]{:S(2)}) collective-permute-start(bf16[4,256,128]{2,1,0:T(8,128)(2,1)S(1)} %pad_maximum_fusion.3), channel_id=1, source_target_pairs={{0,7},{1,2},{2,1},{3,4},{4,3},{5,6},{6,5},{7,0},{8,15},{9,10},{10,... | collective-permute-start | bytes 786440 | tf_op jit(solution)/shard_map/ppermute | solution.py:65
  41.1 0.0 collective-permute-done.8
  41.1 1.0 pad_maximum_fusion.refs_6_
  42.1 0.0 copy-start.3
  42.1 5.1 %collective-permute-start.9 = (bf16[4,528,128]{2,1,0:T(8,128)(2,1)S(1)}, bf16[4,528,128]{2,1,0:T(8,128)(2,1)S(1)}, u32[]{:S(2)}, u32[]{:S(2)}) collective-permute-start(bf16[4,528,128]{2,1,0:T(8,128)(2,1)S(1)} %pad_maximum_fusion.refs_6_), channel_id=1, source_target_pairs={{0,448},{64,128},{128,64},{192,256},{256,192},{320,384},{384,320},... | collective-permute-start | bytes 1622024 | tf_op jit(solution)/shard_map/ppermute | solution.py:65
  47.3 0.0 collective-permute-done.2
  47.3 0.0 copy-done.7
  47.3 0.1 pad_maximum_fusion.1.refs_1_
  47.3 0.0 copy-start.4
  47.3 3.4 %collective-permute-start.4 = (bf16[8,256,128]{2,1,0:T(8,128)(2,1)S(1)}, bf16[8,256,128]{2,1,0:T(8,128)(2,1)S(1)}, u32[]{:S(2)}, u32[]{:S(2)}) collective-permute-start(bf16[8,256,128]{2,1,0:T(8,128)(2,1)S(1)} %pad_maximum_fusion.1.refs_1_), channel_id=1, source_target_pairs={{0,24},{8,16},{16,8},{24,0},{1,25},{9,17},{17,9},{25,1},{2,26},{10... | collective-permute-start | bytes 1572872 | tf_op jit(solution)/shard_map/ppermute | solution.py:65
  50.7 3.7 %collective-permute-start.3 = (bf16[8,256,128]{2,1,0:T(8,128)(2,1)S(1)}, bf16[8,256,128]{2,1,0:T(8,128)(2,1)S(1)}, u32[]{:S(2)}, u32[]{:S(2)}) collective-permute-start(bf16[8,256,128]{2,1,0:T(8,128)(2,1)S(1)} %pad_maximum_fusion.1.refs_1_), channel_id=1, source_target_pairs={{0,8},{8,0},{16,24},{24,16},{1,9},{9,1},{17,25},{25,17},{2,10},{10... | collective-permute-start | bytes 1572872 | tf_op jit(solution)/shard_map/ppermute | solution.py:65
  54.5 1.9 %collective-permute-start.10 = (bf16[4,528,128]{2,1,0:T(8,128)(2,1)S(1)}, bf16[4,528,128]{2,1,0:T(8,128)(2,1)S(1)}, u32[]{:S(2)}, u32[]{:S(2)}) collective-permute-start(bf16[4,528,128]{2,1,0:T(8,128)(2,1)S(1)} %pad_maximum_fusion.refs_6_), channel_id=1, source_target_pairs={{0,32},{32,0},{1,33},{33,1},{2,34},{34,2},{3,35},{35,3},{4,36},{36... | collective-permute-start | bytes 1622024 | tf_op jit(solution)/shard_map/ppermute | solution.py:65
  56.4 0.8 collective-permute-done.9.refs_7_
  57.2 1.9 %collective-permute-start.11 = (bf16[4,528,128]{2,1,0:T(8,128)(2,1)S(1)}, bf16[4,528,128]{2,1,0:T(8,128)(2,1)}, u32[]{:S(2)}, u32[]{:S(2)}) collective-permute-start(bf16[4,528,128]{2,1,0:T(8,128)(2,1)S(1)} %collective-permute-done.9.refs_7_), channel_id=1, source_target_pairs={{0,32},{32,0},{1,33},{33,1},{2,34},{34,2},{3,35},{35,3},{4,36},{36... | collective-permute-start | bytes 1622024 | tf_op jit(solution)/shard_map/ppermute | solution.py:65
  59.1 1.2 collective-permute-done.4.refs_3_
  60.3 0.8 slice.9
  61.1 3.6 %collective-permute-start.6 = (bf16[4,256,128]{2,1,0:T(8,128)(2,1)}, bf16[4,256,128]{2,1,0:T(8,128)(2,1)S(1)}, u32[]{:S(2)}, u32[]{:S(2)}) collective-permute-start(bf16[4,256,128]{2,1,0:T(8,128)(2,1)} %slice.9), channel_id=1, source_target_pairs={{0,8},{8,0},{16,24},{24,16},{1,9},{9,1},{17,25},{25,17},{2,10},{10... | collective-permute-start | bytes 786440 | tf_op jit(solution)/shard_map/ppermute | solution.py:65
  64.7 0.0 collective-permute-done.3.refs_2_
  64.8 0.0 copy-start.6
  64.8 0.8 slice.8
  65.5 4.0 %collective-permute-start.5 = (bf16[4,256,128]{2,1,0:T(8,128)(2,1)}, bf16[4,256,128]{2,1,0:T(8,128)(2,1)}, u32[]{:S(2)}, u32[]{:S(2)}) collective-permute-start(bf16[4,256,128]{2,1,0:T(8,128)(2,1)} %slice.8), channel_id=1, source_target_pairs={{0,24},{8,16},{16,8},{24,0},{1,25},{9,17},{17,9},{25,1},{2,26},{10... | collective-permute-start | bytes 786440 | tf_op jit(solution)/shard_map/ppermute | solution.py:65
  69.6 0.7 pad_add_fusion.refs_0_
  70.2 0.0 collective-permute-done.10.refs_8_
  70.2 0.5 collective-permute-done.6.refs_5_
  70.7 3.5 %collective-permute-done.5.refs_4_ = bf16[4,256,128]{2,1,0:T(8,128)(2,1)} collective-permute-done((bf16[4,256,128]{2,1,0:T(8,128)(2,1)}, bf16[4,256,128]{2,1,0:T(8,128)(2,1)}, u32[]{:S(2)}, u32[]{:S(2)}) %collective-permute-start.5) | collective-permute-done | bytes 262176 | tf_op jit(solution)/shard_map/ppermute | solution.py:65
  74.2 0.0 collective-permute-done.11.refs_9_
  74.2 0.0 copy-done.3
  74.2 0.0 copy-done.4
  74.3 10.0 %shard_map.94 = (bf16[256,512]{1,0:T(8,128)(2,1)}, bf16[2,8,256,128]{3,2,1,0:T(8,128)(2,1)}, bf16[2,8,256,128]{3,2,1,0:T(8,128)(2,1)}, bf16[4,8,256,128]{3,2,1,0:T(8,128)(2,1)}) custom-call(s32[4]{0:T(128)} %pad_add_fusion.refs_0_, bf16[8,256,128]{2,1,0:T(8,128)(2,1)} %copy-done.4, bf16[8,256,128]{2,1,0:T(8,128)(2,1)} %copy-done.6, ...), custom_call_target="tpu_custom_call" | custom-call | tf_op jit(solution)/shard_map/pallas_call | solution.py:281
  84.3 6.0 %all-to-all-start = ((bf16[4,8,256,128]{3,2,1,0:T(8,128)(2,1)}), bf16[4,8,256,128]{3,2,1,0:T(8,128)(2,1)S(1)}, u32[]{:S(2)}, u32[]{:S(2)}) async-start(bf16[4,8,256,128]{3,2,1,0:T(8,128)(2,1)} %get-tuple-element.21), calls=%async_computation | async-start | bytes 4194304 | tf_op jit(solution)/shard_map/all_to_all | solution.py:306
  90.3 1.9 %collective-permute-start.12 = (bf16[2,8,256,128]{3,2,1,0:T(8,128)(2,1)}, bf16[2,8,256,128]{3,2,1,0:T(8,128)(2,1)S(1)}, u32[]{:S(2)}, u32[]{:S(2)}) collective-permute-start(bf16[2,8,256,128]{3,2,1,0:T(8,128)(2,1)} %get-tuple-element.23), channel_id=1, source_target_pairs={{0,32},{32,0},{1,33},{33,1},{2,34},{34,2},{3,35},{35,3},{4,36},{36... | collective-permute-start | bytes 3145736 | tf_op jit(solution)/shard_map/ppermute | solution.py:65
  92.2 2.8 %collective-permute-done.12.other = bf16[2,8,256,128]{3,2,1,0:T(8,128)(2,1)S(1)} collective-permute-done((bf16[2,8,256,128]{3,2,1,0:T(8,128)(2,1)}, bf16[2,8,256,128]{3,2,1,0:T(8,128)(2,1)S(1)}, u32[]{:S(2)}, u32[]{:S(2)}) %collective-permute-start.12) | collective-permute-done | bytes 1048608 | tf_op jit(solution)/shard_map/ppermute | solution.py:65
  95.1 0.2 shard_map.95
  95.3 4.8 %collective-permute-start.13 = (bf16[4,256,128]{2,1,0:T(8,128)(2,1)S(1)}, bf16[4,256,128]{2,1,0:T(8,128)(2,1)S(1)}, u32[]{:S(2)}, u32[]{:S(2)}) collective-permute-start(bf16[4,256,128]{2,1,0:T(8,128)(2,1)S(1)} %get-tuple-element.25), channel_id=1, source_target_pairs={{0,448},{64,128},{128,64},{192,256},{256,192},{320,384},{384,320},... | collective-permute-start | bytes 786440 | tf_op jit(solution)/shard_map/ppermute | solution.py:65
  100.2 1.9 %collective-permute-start.14 = (bf16[4,256,128]{2,1,0:T(8,128)(2,1)S(1)}, bf16[4,256,128]{2,1,0:T(8,128)(2,1)S(1)}, u32[]{:S(2)}, u32[]{:S(2)}) collective-permute-start(bf16[4,256,128]{2,1,0:T(8,128)(2,1)S(1)} %get-tuple-element.27), channel_id=1, source_target_pairs={{0,64},{64,0},{128,192},{192,128},{256,320},{320,256},{384,448},{4... | collective-permute-start | bytes 786440 | tf_op jit(solution)/shard_map/ppermute | solution.py:65
  102.1 4.7 %collective-permute-done.13.from_g = bf16[4,256,128]{2,1,0:T(8,128)(2,1)S(1)} collective-permute-done((bf16[4,256,128]{2,1,0:T(8,128)(2,1)S(1)}, bf16[4,256,128]{2,1,0:T(8,128)(2,1)S(1)}, u32[]{:S(2)}, u32[]{:S(2)}) %collective-permute-start.13) | collective-permute-done | bytes 262176 | tf_op jit(solution)/shard_map/ppermute | solution.py:65
  106.8 3.4 %collective-permute-done.14.from_u = bf16[4,256,128]{2,1,0:T(8,128)(2,1)S(1)} collective-permute-done((bf16[4,256,128]{2,1,0:T(8,128)(2,1)S(1)}, bf16[4,256,128]{2,1,0:T(8,128)(2,1)S(1)}, u32[]{:S(2)}, u32[]{:S(2)}) %collective-permute-start.14) | collective-permute-done | bytes 262176 | tf_op jit(solution)/shard_map/ppermute | solution.py:65
  110.1 0.1 shard_map.96
  110.2 2.2 %collective-permute-start.15 = (bf16[2,256,128]{2,1,0:T(8,128)(2,1)S(1)}, bf16[2,256,128]{2,1,0:T(8,128)(2,1)S(1)}, u32[]{:S(2)}, u32[]{:S(2)}) collective-permute-start(bf16[2,256,128]{2,1,0:T(8,128)(2,1)S(1)} %get-tuple-element.29), channel_id=1, source_target_pairs={{0,64},{64,0},{128,192},{192,128},{256,320},{320,256},{384,448},{4... | collective-permute-start | bytes 393224 | tf_op jit(solution)/shard_map/ppermute | solution.py:65
  112.5 2.2 %collective-permute-start.16 = (bf16[2,256,128]{2,1,0:T(8,128)(2,1)S(1)}, bf16[2,256,128]{2,1,0:T(8,128)(2,1)S(1)}, u32[]{:S(2)}, u32[]{:S(2)}) collective-permute-start(bf16[2,256,128]{2,1,0:T(8,128)(2,1)S(1)} %get-tuple-element.31), channel_id=1, source_target_pairs={{0,448},{64,128},{128,64},{192,256},{256,192},{320,384},{384,320},... | collective-permute-start | bytes 393224 | tf_op jit(solution)/shard_map/ppermute | solution.py:65
  114.7 2.4 %collective-permute-done.15.from_g = bf16[2,256,128]{2,1,0:T(8,128)(2,1)S(1)} collective-permute-done((bf16[2,256,128]{2,1,0:T(8,128)(2,1)S(1)}, bf16[2,256,128]{2,1,0:T(8,128)(2,1)S(1)}, u32[]{:S(2)}, u32[]{:S(2)}) %collective-permute-start.15) | collective-permute-done | bytes 131104 | tf_op jit(solution)/shard_map/ppermute | solution.py:65
  117.1 3.4 %collective-permute-done.16.from_u = bf16[2,256,128]{2,1,0:T(8,128)(2,1)S(1)} collective-permute-done((bf16[2,256,128]{2,1,0:T(8,128)(2,1)S(1)}, bf16[2,256,128]{2,1,0:T(8,128)(2,1)S(1)}, u32[]{:S(2)}, u32[]{:S(2)}) %collective-permute-start.16) | collective-permute-done | bytes 131104 | tf_op jit(solution)/shard_map/ppermute | solution.py:65
  120.5 0.1 shard_map.97
  120.6 0.0 all-to-all-done.t_ref
  120.6 1.1 shard_map.98
  121.7 3.5 %all-to-all-start.1 = ((bf16[8,256,128]{2,1,0:T(8,128)(2,1)}), bf16[8,256,128]{2,1,0:T(8,128)(2,1)S(1)}, u32[]{:S(2)}, u32[]{:S(2)}) async-start(bf16[8,256,128]{2,1,0:T(8,128)(2,1)} %shard_map.98), calls=%async_computation.1 | async-start | bytes 1048576 | tf_op jit(solution)/shard_map/all_to_all | solution.py:316
  125.2 5.0 %collective-permute-start.17 = (bf16[2,256,128]{2,1,0:T(8,128)(2,1)S(1)}, bf16[2,256,128]{2,1,0:T(8,128)(2,1)S(1)}, u32[]{:S(2)}, u32[]{:S(2)}) collective-permute-start(bf16[2,256,128]{2,1,0:T(8,128)(2,1)S(1)} %get-tuple-element.33), channel_id=1, source_target_pairs={{0,256},{64,320},{128,384},{192,448},{256,0},{320,64},{384,128},{4... | collective-permute-start | bytes 393224 | tf_op jit(solution)/shard_map/ppermute | solution.py:65
  130.2 6.5 %collective-permute-done.17.b_ref = bf16[2,256,128]{2,1,0:T(8,128)(2,1)S(1)} collective-permute-done((bf16[2,256,128]{2,1,0:T(8,128)(2,1)S(1)}, bf16[2,256,128]{2,1,0:T(8,128)(2,1)S(1)}, u32[]{:S(2)}, u32[]{:S(2)}) %collective-permute-start.17) | collective-permute-done | bytes 131104 | tf_op jit(solution)/shard_map/ppermute | solution.py:65
  136.6 0.0 copy-done.1
  136.6 1.7 %shard_map.100 = (bf16[256,512]{1,0:T(8,128)(2,1)}, bf16[256,512]{1,0:T(8,128)(2,1)}) custom-call(s32[2,4]{1,0:T(2,128)S(1)} %copy-done.1, s32[2,4]{1,0:T(2,128)S(1)} %copy-done.2, bf16[2,256,128]{2,1,0:T(8,128)(2,1)S(1)} %get-tuple-element.32._.a_ref, bf16[2,256,128]{2,1,0:T(8,128)(2,1)S(1)} %collective-permute-done.17.b_ref), custom_call_target="tpu_custom_call" | custom-call | tf_op jit(solution)/shard_map/pallas_call | solution.py:319
  138.3 2.5 %all-to-all-done.1.a_ref = bf16[8,256,128]{2,1,0:T(8,128)(2,1)S(1)} async-done(((bf16[8,256,128]{2,1,0:T(8,128)(2,1)}), bf16[8,256,128]{2,1,0:T(8,128)(2,1)S(1)}, u32[]{:S(2)}, u32[]{:S(2)}) %all-to-all-start.1) | async-done | bytes 524320 | tf_op jit(solution)/shard_map/all_to_all | solution.py:316
  140.9 0.7 shard_map.99
  (14 shorter events, 0.0 us)
Async XLA Ops:
  0.6 46.6 %copy-start.7 = (bf16[256,128]{1,0:T(8,128)(2,1)S(1)}, bf16[256,128]{1,0:T(8,128)(2,1)}, u32[]{:S(2)}) copy-start(bf16[256,128]{1,0:T(8,128)(2,1)} %param.6) | copy-start | bytes 196612
  3.0 18.7 %collective-permute-start.7 = (bf16[1,528,128]{2,1,0:T(8,128)(2,1)}, bf16[1,528,128]{2,1,0:T(8,128)(2,1)S(1)}, u32[]{:S(2)}, u32[]{:S(2)}) collective-permute-start(bf16[1,528,128]{2,1,0:T(8,128)(2,1)} %bitcast.6), channel_id=1, source_target_pairs={{0,256},{64,320},{128,384},{192,448},{256,0},{320,64},{384,128},{4... | collective-permute-start | bytes 405512 | tf_op jit(solution)/shard_map/ppermute | solution.py:65
  10.8 14.5 %collective-permute-start = (bf16[1,256,128]{2,1,0:T(8,128)(2,1)}, bf16[1,256,128]{2,1,0:T(8,128)(2,1)S(1)}, u32[]{:S(2)}, u32[]{:S(2)}) collective-permute-start(bf16[1,256,128]{2,1,0:T(8,128)(2,1)} %bitcast.9), channel_id=1, source_target_pairs={{0,4},{1,5},{2,6},{3,7},{4,0},{5,1},{6,2},{7,3},{8,12},{9,13},{10,... | collective-permute-start | bytes 196616 | tf_op jit(solution)/shard_map/ppermute | solution.py:65
  22.7 18.4 %collective-permute-start.8 = (bf16[2,528,128]{2,1,0:T(8,128)(2,1)S(1)}, bf16[2,528,128]{2,1,0:T(8,128)(2,1)S(1)}, u32[]{:S(2)}, u32[]{:S(2)}) collective-permute-start(bf16[2,528,128]{2,1,0:T(8,128)(2,1)S(1)} %pad_maximum_fusion.2), channel_id=1, source_target_pairs={{0,64},{64,0},{128,192},{192,128},{256,320},{320,256},{384,448},{4... | collective-permute-start | bytes 811016 | tf_op jit(solution)/shard_map/ppermute | solution.py:65
  26.1 6.9 %collective-permute-start.1 = (bf16[2,256,128]{2,1,0:T(8,128)(2,1)S(1)}, bf16[2,256,128]{2,1,0:T(8,128)(2,1)S(1)}, u32[]{:S(2)}, u32[]{:S(2)}) collective-permute-start(bf16[2,256,128]{2,1,0:T(8,128)(2,1)S(1)} %pad_maximum_fusion.4), channel_id=1, source_target_pairs={{0,1},{1,0},{2,3},{3,2},{4,5},{5,4},{6,7},{7,6},{8,9},{9,8},{10,11... | collective-permute-start | bytes 393224 | tf_op jit(solution)/shard_map/ppermute | solution.py:65
  33.8 13.4 %collective-permute-start.2 = (bf16[4,256,128]{2,1,0:T(8,128)(2,1)S(1)}, bf16[4,256,128]{2,1,0:T(8,128)(2,1)S(1)}, u32[]{:S(2)}, u32[]{:S(2)}) collective-permute-start(bf16[4,256,128]{2,1,0:T(8,128)(2,1)S(1)} %pad_maximum_fusion.3), channel_id=1, source_target_pairs={{0,7},{1,2},{2,1},{3,4},{4,3},{5,6},{6,5},{7,0},{8,15},{9,10},{10,... | collective-permute-start | bytes 786440 | tf_op jit(solution)/shard_map/ppermute | solution.py:65
  42.1 32.1 %copy-start.3 = (bf16[4,528,128]{2,1,0:T(8,128)(2,1)}, bf16[4,528,128]{2,1,0:T(8,128)(2,1)S(1)}, u32[]{:S(2)}) copy-start(bf16[4,528,128]{2,1,0:T(8,128)(2,1)S(1)} %pad_maximum_fusion.refs_6_) | copy-start | bytes 1622020
  42.1 15.1 %collective-permute-start.9 = (bf16[4,528,128]{2,1,0:T(8,128)(2,1)S(1)}, bf16[4,528,128]{2,1,0:T(8,128)(2,1)S(1)}, u32[]{:S(2)}, u32[]{:S(2)}) collective-permute-start(bf16[4,528,128]{2,1,0:T(8,128)(2,1)S(1)} %pad_maximum_fusion.refs_6_), channel_id=1, source_target_pairs={{0,448},{64,128},{128,64},{192,256},{256,192},{320,384},{384,320},... | collective-permute-start | bytes 1622024 | tf_op jit(solution)/shard_map/ppermute | solution.py:65
  47.3 26.9 %copy-start.4 = (bf16[8,256,128]{2,1,0:T(8,128)(2,1)}, bf16[8,256,128]{2,1,0:T(8,128)(2,1)S(1)}, u32[]{:S(2)}) copy-start(bf16[8,256,128]{2,1,0:T(8,128)(2,1)S(1)} %pad_maximum_fusion.1.refs_1_) | copy-start | bytes 1572868
  47.3 13.0 %collective-permute-start.4 = (bf16[8,256,128]{2,1,0:T(8,128)(2,1)S(1)}, bf16[8,256,128]{2,1,0:T(8,128)(2,1)S(1)}, u32[]{:S(2)}, u32[]{:S(2)}) collective-permute-start(bf16[8,256,128]{2,1,0:T(8,128)(2,1)S(1)} %pad_maximum_fusion.1.refs_1_), channel_id=1, source_target_pairs={{0,24},{8,16},{16,8},{24,0},{1,25},{9,17},{17,9},{25,1},{2,26},{10... | collective-permute-start | bytes 1572872 | tf_op jit(solution)/shard_map/ppermute | solution.py:65
  50.7 14.0 %collective-permute-start.3 = (bf16[8,256,128]{2,1,0:T(8,128)(2,1)S(1)}, bf16[8,256,128]{2,1,0:T(8,128)(2,1)S(1)}, u32[]{:S(2)}, u32[]{:S(2)}) collective-permute-start(bf16[8,256,128]{2,1,0:T(8,128)(2,1)S(1)} %pad_maximum_fusion.1.refs_1_), channel_id=1, source_target_pairs={{0,8},{8,0},{16,24},{24,16},{1,9},{9,1},{17,25},{25,17},{2,10},{10... | collective-permute-start | bytes 1572872 | tf_op jit(solution)/shard_map/ppermute | solution.py:65
  54.5 15.8 %collective-permute-start.10 = (bf16[4,528,128]{2,1,0:T(8,128)(2,1)S(1)}, bf16[4,528,128]{2,1,0:T(8,128)(2,1)S(1)}, u32[]{:S(2)}, u32[]{:S(2)}) collective-permute-start(bf16[4,528,128]{2,1,0:T(8,128)(2,1)S(1)} %pad_maximum_fusion.refs_6_), channel_id=1, source_target_pairs={{0,32},{32,0},{1,33},{33,1},{2,34},{34,2},{3,35},{35,3},{4,36},{36... | collective-permute-start | bytes 1622024 | tf_op jit(solution)/shard_map/ppermute | solution.py:65
  57.2 17.0 %copy-start.8 = (bf16[4,528,128]{2,1,0:T(8,128)(2,1)}, bf16[4,528,128]{2,1,0:T(8,128)(2,1)S(1)}, u32[]{:S(2)}) copy-start(bf16[4,528,128]{2,1,0:T(8,128)(2,1)S(1)} %collective-permute-done.9.refs_7_) | copy-start | bytes 1622020
  57.2 17.0 %collective-permute-start.11 = (bf16[4,528,128]{2,1,0:T(8,128)(2,1)S(1)}, bf16[4,528,128]{2,1,0:T(8,128)(2,1)}, u32[]{:S(2)}, u32[]{:S(2)}) collective-permute-start(bf16[4,528,128]{2,1,0:T(8,128)(2,1)S(1)} %collective-permute-done.9.refs_7_), channel_id=1, source_target_pairs={{0,32},{32,0},{1,33},{33,1},{2,34},{34,2},{3,35},{35,3},{4,36},{36... | collective-permute-start | bytes 1622024 | tf_op jit(solution)/shard_map/ppermute | solution.py:65
  60.3 13.9 %copy-start.5 = (bf16[8,256,128]{2,1,0:T(8,128)(2,1)}, bf16[8,256,128]{2,1,0:T(8,128)(2,1)S(1)}, u32[]{:S(2)}) copy-start(bf16[8,256,128]{2,1,0:T(8,128)(2,1)S(1)} %collective-permute-done.4.refs_3_) | copy-start | bytes 1572868
  61.1 9.6 %collective-permute-start.6 = (bf16[4,256,128]{2,1,0:T(8,128)(2,1)}, bf16[4,256,128]{2,1,0:T(8,128)(2,1)S(1)}, u32[]{:S(2)}, u32[]{:S(2)}) collective-permute-start(bf16[4,256,128]{2,1,0:T(8,128)(2,1)} %slice.9), channel_id=1, source_target_pairs={{0,8},{8,0},{16,24},{24,16},{1,9},{9,1},{17,25},{25,17},{2,10},{10... | collective-permute-start | bytes 786440 | tf_op jit(solution)/shard_map/ppermute | solution.py:65
  64.8 9.5 %copy-start.6 = (bf16[8,256,128]{2,1,0:T(8,128)(2,1)}, bf16[8,256,128]{2,1,0:T(8,128)(2,1)S(1)}, u32[]{:S(2)}) copy-start(bf16[8,256,128]{2,1,0:T(8,128)(2,1)S(1)} %collective-permute-done.3.refs_2_) | copy-start | bytes 1572868
  65.5 8.7 %collective-permute-start.5 = (bf16[4,256,128]{2,1,0:T(8,128)(2,1)}, bf16[4,256,128]{2,1,0:T(8,128)(2,1)}, u32[]{:S(2)}, u32[]{:S(2)}) collective-permute-start(bf16[4,256,128]{2,1,0:T(8,128)(2,1)} %slice.8), channel_id=1, source_target_pairs={{0,24},{8,16},{16,8},{24,0},{1,25},{9,17},{17,9},{25,1},{2,26},{10... | collective-permute-start | bytes 786440 | tf_op jit(solution)/shard_map/ppermute | solution.py:65
  70.2 4.0 %copy-start.9 = (bf16[4,528,128]{2,1,0:T(8,128)(2,1)}, bf16[4,528,128]{2,1,0:T(8,128)(2,1)S(1)}, u32[]{:S(2)}) copy-start(bf16[4,528,128]{2,1,0:T(8,128)(2,1)S(1)} %collective-permute-done.10.refs_8_) | copy-start | bytes 1622020
  70.7 3.5 %copy-start.10 = (bf16[4,256,128]{2,1,0:T(8,128)(2,1)}, bf16[4,256,128]{2,1,0:T(8,128)(2,1)S(1)}, u32[]{:S(2)}) copy-start(bf16[4,256,128]{2,1,0:T(8,128)(2,1)S(1)} %collective-permute-done.6.refs_5_) | copy-start | bytes 786436
  84.3 10.8 %copy-start = (bf16[2,8,256,128]{3,2,1,0:T(8,128)(2,1)S(1)}, bf16[2,8,256,128]{3,2,1,0:T(8,128)(2,1)}, u32[]{:S(2)}) copy-start(bf16[2,8,256,128]{3,2,1,0:T(8,128)(2,1)} %get-tuple-element.22.keep) | copy-start | bytes 3145732
  84.3 36.3 %all-to-all-start = ((bf16[4,8,256,128]{3,2,1,0:T(8,128)(2,1)}), bf16[4,8,256,128]{3,2,1,0:T(8,128)(2,1)S(1)}, u32[]{:S(2)}, u32[]{:S(2)}) async-start(bf16[4,8,256,128]{3,2,1,0:T(8,128)(2,1)} %get-tuple-element.21), calls=%async_computation | async-start | bytes 4194304 | tf_op jit(solution)/shard_map/all_to_all | solution.py:306
  90.3 4.8 %collective-permute-start.12 = (bf16[2,8,256,128]{3,2,1,0:T(8,128)(2,1)}, bf16[2,8,256,128]{3,2,1,0:T(8,128)(2,1)S(1)}, u32[]{:S(2)}, u32[]{:S(2)}) collective-permute-start(bf16[2,8,256,128]{3,2,1,0:T(8,128)(2,1)} %get-tuple-element.23), channel_id=1, source_target_pairs={{0,32},{32,0},{1,33},{33,1},{2,34},{34,2},{3,35},{35,3},{4,36},{36... | collective-permute-start | bytes 3145736 | tf_op jit(solution)/shard_map/ppermute | solution.py:65
  95.3 11.5 %collective-permute-start.13 = (bf16[4,256,128]{2,1,0:T(8,128)(2,1)S(1)}, bf16[4,256,128]{2,1,0:T(8,128)(2,1)S(1)}, u32[]{:S(2)}, u32[]{:S(2)}) collective-permute-start(bf16[4,256,128]{2,1,0:T(8,128)(2,1)S(1)} %get-tuple-element.25), channel_id=1, source_target_pairs={{0,448},{64,128},{128,64},{192,256},{256,192},{320,384},{384,320},... | collective-permute-start | bytes 786440 | tf_op jit(solution)/shard_map/ppermute | solution.py:65
  100.2 10.0 %collective-permute-start.14 = (bf16[4,256,128]{2,1,0:T(8,128)(2,1)S(1)}, bf16[4,256,128]{2,1,0:T(8,128)(2,1)S(1)}, u32[]{:S(2)}, u32[]{:S(2)}) collective-permute-start(bf16[4,256,128]{2,1,0:T(8,128)(2,1)S(1)} %get-tuple-element.27), channel_id=1, source_target_pairs={{0,64},{64,0},{128,192},{192,128},{256,320},{320,256},{384,448},{4... | collective-permute-start | bytes 786440 | tf_op jit(solution)/shard_map/ppermute | solution.py:65
  110.2 6.9 %collective-permute-start.15 = (bf16[2,256,128]{2,1,0:T(8,128)(2,1)S(1)}, bf16[2,256,128]{2,1,0:T(8,128)(2,1)S(1)}, u32[]{:S(2)}, u32[]{:S(2)}) collective-permute-start(bf16[2,256,128]{2,1,0:T(8,128)(2,1)S(1)} %get-tuple-element.29), channel_id=1, source_target_pairs={{0,64},{64,0},{128,192},{192,128},{256,320},{320,256},{384,448},{4... | collective-permute-start | bytes 393224 | tf_op jit(solution)/shard_map/ppermute | solution.py:65
  112.5 8.1 %collective-permute-start.16 = (bf16[2,256,128]{2,1,0:T(8,128)(2,1)S(1)}, bf16[2,256,128]{2,1,0:T(8,128)(2,1)S(1)}, u32[]{:S(2)}, u32[]{:S(2)}) collective-permute-start(bf16[2,256,128]{2,1,0:T(8,128)(2,1)S(1)} %get-tuple-element.31), channel_id=1, source_target_pairs={{0,448},{64,128},{128,64},{192,256},{256,192},{320,384},{384,320},... | collective-permute-start | bytes 393224 | tf_op jit(solution)/shard_map/ppermute | solution.py:65
  120.5 16.1 %copy-start.1 = (s32[2,4]{1,0:T(2,128)S(1)}, s32[2,4]{1,0:T(2,128)}, u32[]{:S(2)}) copy-start(s32[2,4]{1,0:T(2,128)} %gm_ref.3) | copy-start | bytes 100
  120.5 16.1 %copy-start.2 = (s32[2,4]{1,0:T(2,128)S(1)}, s32[2,4]{1,0:T(2,128)}, u32[]{:S(2)}) copy-start(s32[2,4]{1,0:T(2,128)} %um_ref.3) | copy-start | bytes 100
  121.7 19.2 %all-to-all-start.1 = ((bf16[8,256,128]{2,1,0:T(8,128)(2,1)}), bf16[8,256,128]{2,1,0:T(8,128)(2,1)S(1)}, u32[]{:S(2)}, u32[]{:S(2)}) async-start(bf16[8,256,128]{2,1,0:T(8,128)(2,1)} %shard_map.98), calls=%async_computation.1 | async-start | bytes 1048576 | tf_op jit(solution)/shard_map/all_to_all | solution.py:316
  125.2 11.5 %collective-permute-start.17 = (bf16[2,256,128]{2,1,0:T(8,128)(2,1)S(1)}, bf16[2,256,128]{2,1,0:T(8,128)(2,1)S(1)}, u32[]{:S(2)}, u32[]{:S(2)}) collective-permute-start(bf16[2,256,128]{2,1,0:T(8,128)(2,1)S(1)} %get-tuple-element.33), channel_id=1, source_target_pairs={{0,256},{64,320},{128,384},{192,448},{256,0},{320,64},{384,128},{4... | collective-permute-start | bytes 393224 | tf_op jit(solution)/shard_map/ppermute | solution.py:65

commit v9 on v7

--- a/solution.py
+++ b/solution.py
@@ -144,13 +144,13 @@
     for k, n in enumerate(places):
         for s in range(SLOTS):
             idx_ref[n, s] = at_ref[k, s]
-    for copy in large:
+    acc[...] = jnp.zeros_like(acc)
+    for copy in large[shards:]:
         copy.wait()
-
-    acc[...] = jnp.zeros_like(acc)
-    for n in range(shards):
+    for k, n in enumerate(places):
+        large[k].wait()
         for s in range(SLOTS):
-            p = idx_ref[n, s]
+            p = at_ref[k, s]
             a = p % blocks + (s // 2) * blocks
             acc[a] += jnp.dot(
                 x_ref[2 * n + p // blocks],

time: 136 us -> 139 us (1.022)
  Pallas kernels: 16.1 us -> 18.4 us
    pallas_call x1, Pallas kernels: 9.91 us -> 12.2 us  [body(): call(lambda *refs: main_kernel(blocks, *refs), (shape((tok, width), BF),...]
where the time goes in v9:
time: 139 us; the launch traced here: 138 us
  starting transfers between devices  72.8 us (52%)
  waiting for transfers between devices  41.9 us (30%)
  Pallas kernels  18.4 us (13%)
  other arithmetic  2.48 us (2%)
  local copies, waits for them, and re-layouts  1.58 us (1%)
    ppermute x15, starting transfers between devices, swap(): lax.ppermute(x, axis, [(i, turn(i, stage, size)) for i in range(size)])  49.5 us
    ppermute x15, waiting for transfers between devices, swap(): lax.ppermute(x, axis, [(i, turn(i, stage, size)) for i in range(size)])  36.5 us
    all_to_all x2, starting transfers between devices, body(): own = lax.all_to_all(own, 'z', 0, 0)  17.9 us
    pallas_call x1, Pallas kernels, body(): call(lambda *refs: main_kernel(blocks, *refs), (shape((tok, width), BF),...  12.2 us
    all_to_all x1, starting transfers between devices, body(): terms = lax.all_to_all(terms, 'x', 0, 0)  5.48 us
    all_to_all x2, waiting for transfers between devices, body(): own = lax.all_to_all(own, 'z', 0, 0)  5.4 us
  transfers between devices with their start and end apart: 18, of which 11 were waited for; matrix products, arithmetic and copies ran while one was open for 3% of the time, Pallas kernels for 1%

profile of v9, /device:TPU:2, one launch (start us, length us, event | category | flops | bytes accessed | tf_op | source)
XLA Modules:
  0.0 138.1 jit_solution(1575838221733343786)
XLA Ops:
  0.6 2.5 %shard_map.93 = (bf16[528,128]{1,0:T(8,128)(2,1)}, bf16[8,256,128]{2,1,0:T(8,128)(2,1)}) custom-call(s32[2,4]{1,0:T(2,128)} %gm_ref.3, s32[2,4]{1,0:T(2,128)} %um_ref.3, bf16[256,128]{1,0:T(8,128)(2,1)} %tok_ref.1, bf16[256,512]{1,0:T(8,128)(2,1)} %gw_ref.1, bf16[256,512]{1,0:T(8,128)(2,1)} %uw_ref.1), custom_call_target="tpu_custom_call" | custom-call | tf_op jit(solution)/shard_map/pallas_call | solution.py:260
  3.1 7.7 %collective-permute-start.4 = (bf16[1,528,128]{2,1,0:T(8,128)(2,1)}, bf16[1,528,128]{2,1,0:T(8,128)(2,1)S(1)}, u32[]{:S(2)}, u32[]{:S(2)}) collective-permute-start(bf16[1,528,128]{2,1,0:T(8,128)(2,1)} %bitcast.4), channel_id=1, source_target_pairs={{0,256},{64,320},{128,384},{192,448},{256,0},{320,64},{384,128},{4... | collective-permute-start | bytes 405512 | tf_op jit(solution)/shard_map/ppermute | solution.py:65
  10.8 10.3 %all-to-all-start = ((bf16[8,256,128]{2,1,0:T(8,128)(2,1)}), bf16[8,256,128]{2,1,0:T(8,128)(2,1)S(1)}, u32[]{:S(2)}, u32[]{:S(2)}) async-start(bf16[8,256,128]{2,1,0:T(8,128)(2,1)} %get-tuple-element.22), calls=%async_computation | async-start | bytes 1048576 | tf_op jit(solution)/shard_map/all_to_all | solution.py:271
  21.2 0.0 collective-permute-done.4
  21.2 0.9 pad_maximum_fusion.1
  22.1 2.6 %collective-permute-start.5 = (bf16[2,528,128]{2,1,0:T(8,128)(2,1)S(1)}, bf16[2,528,128]{2,1,0:T(8,128)(2,1)S(1)}, u32[]{:S(2)}, u32[]{:S(2)}) collective-permute-start(bf16[2,528,128]{2,1,0:T(8,128)(2,1)S(1)} %pad_maximum_fusion.1), channel_id=1, source_target_pairs={{0,64},{64,0},{128,192},{192,128},{256,320},{320,256},{384,448},{4... | collective-permute-start | bytes 811016 | tf_op jit(solution)/shard_map/ppermute | solution.py:65
  24.8 6.9 %collective-permute-done.5 = bf16[2,528,128]{2,1,0:T(8,128)(2,1)S(1)} collective-permute-done((bf16[2,528,128]{2,1,0:T(8,128)(2,1)S(1)}, bf16[2,528,128]{2,1,0:T(8,128)(2,1)S(1)}, u32[]{:S(2)}, u32[]{:S(2)}) %collective-permute-start.5) | collective-permute-done | bytes 270368 | tf_op jit(solution)/shard_map/ppermute | solution.py:65
  31.7 1.0 pad_maximum_fusion.refs_6_
  32.6 0.0 copy-start.3
  32.6 2.4 %collective-permute-start.6 = (bf16[4,528,128]{2,1,0:T(8,128)(2,1)S(1)}, bf16[4,528,128]{2,1,0:T(8,128)(2,1)S(1)}, u32[]{:S(2)}, u32[]{:S(2)}) collective-permute-start(bf16[4,528,128]{2,1,0:T(8,128)(2,1)S(1)} %pad_maximum_fusion.refs_6_), channel_id=1, source_target_pairs={{0,448},{64,128},{128,64},{192,256},{256,192},{320,384},{384,320},... | collective-permute-start | bytes 1622024 | tf_op jit(solution)/shard_map/ppermute | solution.py:65
  35.1 3.3 %all-to-all-done.refs_1_ = bf16[8,256,128]{2,1,0:T(8,128)(2,1)S(1)} async-done(((bf16[8,256,128]{2,1,0:T(8,128)(2,1)}), bf16[8,256,128]{2,1,0:T(8,128)(2,1)S(1)}, u32[]{:S(2)}, u32[]{:S(2)}) %all-to-all-start) | async-done | bytes 524320 | tf_op jit(solution)/shard_map/all_to_all | solution.py:271
  38.4 0.0 copy-start.4
  38.4 3.4 %collective-permute-start.1 = (bf16[8,256,128]{2,1,0:T(8,128)(2,1)S(1)}, bf16[8,256,128]{2,1,0:T(8,128)(2,1)S(1)}, u32[]{:S(2)}, u32[]{:S(2)}) collective-permute-start(bf16[8,256,128]{2,1,0:T(8,128)(2,1)S(1)} %all-to-all-done.refs_1_), channel_id=1, source_target_pairs={{0,24},{8,16},{16,8},{24,0},{1,25},{9,17},{17,9},{25,1},{2,26},{10... | collective-permute-start | bytes 1572872 | tf_op jit(solution)/shard_map/ppermute | solution.py:65
  41.8 3.7 %collective-permute-start = (bf16[8,256,128]{2,1,0:T(8,128)(2,1)S(1)}, bf16[8,256,128]{2,1,0:T(8,128)(2,1)S(1)}, u32[]{:S(2)}, u32[]{:S(2)}) collective-permute-start(bf16[8,256,128]{2,1,0:T(8,128)(2,1)S(1)} %all-to-all-done.refs_1_), channel_id=1, source_target_pairs={{0,8},{8,0},{16,24},{24,16},{1,9},{9,1},{17,25},{25,17},{2,10},{10... | collective-permute-start | bytes 1572872 | tf_op jit(solution)/shard_map/ppermute | solution.py:65
  45.5 1.9 %collective-permute-start.7 = (bf16[4,528,128]{2,1,0:T(8,128)(2,1)S(1)}, bf16[4,528,128]{2,1,0:T(8,128)(2,1)S(1)}, u32[]{:S(2)}, u32[]{:S(2)}) collective-permute-start(bf16[4,528,128]{2,1,0:T(8,128)(2,1)S(1)} %pad_maximum_fusion.refs_6_), channel_id=1, source_target_pairs={{0,32},{32,0},{1,33},{33,1},{2,34},{34,2},{3,35},{35,3},{4,36},{36... | collective-permute-start | bytes 1622024 | tf_op jit(solution)/shard_map/ppermute | solution.py:65
  47.4 0.8 collective-permute-done.6.refs_7_
  48.3 1.9 %collective-permute-start.8 = (bf16[4,528,128]{2,1,0:T(8,128)(2,1)S(1)}, bf16[4,528,128]{2,1,0:T(8,128)(2,1)}, u32[]{:S(2)}, u32[]{:S(2)}) collective-permute-start(bf16[4,528,128]{2,1,0:T(8,128)(2,1)S(1)} %collective-permute-done.6.refs_7_), channel_id=1, source_target_pairs={{0,32},{32,0},{1,33},{33,1},{2,34},{34,2},{3,35},{35,3},{4,36},{36... | collective-permute-start | bytes 1622024 | tf_op jit(solution)/shard_map/ppermute | solution.py:65
  50.2 3.0 %collective-permute-done.1.refs_3_ = bf16[8,256,128]{2,1,0:T(8,128)(2,1)S(1)} collective-permute-done((bf16[8,256,128]{2,1,0:T(8,128)(2,1)S(1)}, bf16[8,256,128]{2,1,0:T(8,128)(2,1)S(1)}, u32[]{:S(2)}, u32[]{:S(2)}) %collective-permute-start.1) | collective-permute-done | bytes 524320 | tf_op jit(solution)/shard_map/ppermute | solution.py:65
  53.2 0.8 slice.9
  54.0 3.7 %collective-permute-start.3 = (bf16[4,256,128]{2,1,0:T(8,128)(2,1)}, bf16[4,256,128]{2,1,0:T(8,128)(2,1)S(1)}, u32[]{:S(2)}, u32[]{:S(2)}) collective-permute-start(bf16[4,256,128]{2,1,0:T(8,128)(2,1)} %slice.9), channel_id=1, source_target_pairs={{0,8},{8,0},{16,24},{24,16},{1,9},{9,1},{17,25},{25,17},{2,10},{10... | collective-permute-start | bytes 786440 | tf_op jit(solution)/shard_map/ppermute | solution.py:65
  57.6 0.0 collective-permute-done.refs_2_
  57.6 0.0 copy-start.6
  57.6 0.8 slice.8
  58.4 4.0 %collective-permute-start.2 = (bf16[4,256,128]{2,1,0:T(8,128)(2,1)}, bf16[4,256,128]{2,1,0:T(8,128)(2,1)}, u32[]{:S(2)}, u32[]{:S(2)}) collective-permute-start(bf16[4,256,128]{2,1,0:T(8,128)(2,1)} %slice.8), channel_id=1, source_target_pairs={{0,24},{8,16},{16,8},{24,0},{1,25},{9,17},{17,9},{25,1},{2,26},{10... | collective-permute-start | bytes 786440 | tf_op jit(solution)/shard_map/ppermute | solution.py:65
  62.5 0.6 pad_add_fusion.refs_0_
  63.0 0.0 collective-permute-done.7.refs_8_
  63.0 0.0 collective-permute-done.8.refs_9_
  63.1 0.0 collective-permute-done.3.refs_5_
  63.1 0.0 copy-start.9
  63.1 4.0 %collective-permute-done.2.refs_4_ = bf16[4,256,128]{2,1,0:T(8,128)(2,1)} collective-permute-done((bf16[4,256,128]{2,1,0:T(8,128)(2,1)}, bf16[4,256,128]{2,1,0:T(8,128)(2,1)}, u32[]{:S(2)}, u32[]{:S(2)}) %collective-permute-start.2) | collective-permute-done | bytes 262176 | tf_op jit(solution)/shard_map/ppermute | solution.py:65
  67.1 0.0 copy-done.3
  67.1 0.0 copy-done.4
  67.1 0.0 copy-done.7
  67.1 0.0 copy-done.5
  67.1 0.0 copy-done.6
  67.2 0.0 copy-done.8
  67.2 0.0 copy-done.9
  67.2 12.2 %shard_map.94 = (bf16[256,512]{1,0:T(8,128)(2,1)}, bf16[2,8,256,128]{3,2,1,0:T(8,128)(2,1)}, bf16[2,8,256,128]{3,2,1,0:T(8,128)(2,1)}, bf16[4,8,256,128]{3,2,1,0:T(8,128)(2,1)}) custom-call(s32[3]{0:T(128)} %pad_add_fusion.refs_0_, bf16[8,256,128]{2,1,0:T(8,128)(2,1)} %copy-done.4, bf16[8,256,128]{2,1,0:T(8,128)(2,1)} %copy-done.6, ...), custom_call_target="tpu_custom_call" | custom-call | tf_op jit(solution)/shard_map/pallas_call | solution.py:281
  79.4 0.0 copy-start
  79.4 5.5 %all-to-all-start.1 = ((bf16[4,8,256,128]{3,2,1,0:T(8,128)(2,1)}), bf16[4,8,256,128]{3,2,1,0:T(8,128)(2,1)S(1)}, u32[]{:S(2)}, u32[]{:S(2)}) async-start(bf16[4,8,256,128]{3,2,1,0:T(8,128)(2,1)} %get-tuple-element.25), calls=%async_computation.1 | async-start | bytes 4194304 | tf_op jit(solution)/shard_map/all_to_all | solution.py:306
  84.9 1.9 %collective-permute-start.9 = (bf16[2,8,256,128]{3,2,1,0:T(8,128)(2,1)}, bf16[2,8,256,128]{3,2,1,0:T(8,128)(2,1)S(1)}, u32[]{:S(2)}, u32[]{:S(2)}) collective-permute-start(bf16[2,8,256,128]{3,2,1,0:T(8,128)(2,1)} %get-tuple-element.27), channel_id=1, source_target_pairs={{0,32},{32,0},{1,33},{33,1},{2,34},{34,2},{3,35},{35,3},{4,36},{36... | collective-permute-start | bytes 3145736 | tf_op jit(solution)/shard_map/ppermute | solution.py:65
  86.8 2.8 %collective-permute-done.9.other = bf16[2,8,256,128]{3,2,1,0:T(8,128)(2,1)S(1)} collective-permute-done((bf16[2,8,256,128]{3,2,1,0:T(8,128)(2,1)}, bf16[2,8,256,128]{3,2,1,0:T(8,128)(2,1)S(1)}, u32[]{:S(2)}, u32[]{:S(2)}) %collective-permute-start.9) | collective-permute-done | bytes 1048608 | tf_op jit(solution)/shard_map/ppermute | solution.py:65
  89.6 0.0 copy-done
  89.6 0.2 shard_map.95
  89.9 2.3 %collective-permute-start.10 = (bf16[4,256,128]{2,1,0:T(8,128)(2,1)S(1)}, bf16[4,256,128]{2,1,0:T(8,128)(2,1)S(1)}, u32[]{:S(2)}, u32[]{:S(2)}) collective-permute-start(bf16[4,256,128]{2,1,0:T(8,128)(2,1)S(1)} %get-tuple-element.29), channel_id=1, source_target_pairs={{0,448},{64,128},{128,64},{192,256},{256,192},{320,384},{384,320},... | collective-permute-start | bytes 786440 | tf_op jit(solution)/shard_map/ppermute | solution.py:65
  92.2 2.8 %collective-permute-start.11 = (bf16[4,256,128]{2,1,0:T(8,128)(2,1)S(1)}, bf16[4,256,128]{2,1,0:T(8,128)(2,1)S(1)}, u32[]{:S(2)}, u32[]{:S(2)}) collective-permute-start(bf16[4,256,128]{2,1,0:T(8,128)(2,1)S(1)} %get-tuple-element.31), channel_id=1, source_target_pairs={{0,64},{64,0},{128,192},{192,128},{256,320},{320,256},{384,448},{4... | collective-permute-start | bytes 786440 | tf_op jit(solution)/shard_map/ppermute | solution.py:65
  95.0 6.3 %collective-permute-done.10.from_g = bf16[4,256,128]{2,1,0:T(8,128)(2,1)S(1)} collective-permute-done((bf16[4,256,128]{2,1,0:T(8,128)(2,1)S(1)}, bf16[4,256,128]{2,1,0:T(8,128)(2,1)S(1)}, u32[]{:S(2)}, u32[]{:S(2)}) %collective-permute-start.10) | collective-permute-done | bytes 262176 | tf_op jit(solution)/shard_map/ppermute | solution.py:65
  101.3 0.9 collective-permute-done.11.from_u
  102.2 0.1 shard_map.96
  102.3 2.8 %collective-permute-start.12 = (bf16[2,256,128]{2,1,0:T(8,128)(2,1)S(1)}, bf16[2,256,128]{2,1,0:T(8,128)(2,1)S(1)}, u32[]{:S(2)}, u32[]{:S(2)}) collective-permute-start(bf16[2,256,128]{2,1,0:T(8,128)(2,1)S(1)} %get-tuple-element.33), channel_id=1, source_target_pairs={{0,64},{64,0},{128,192},{192,128},{256,320},{320,256},{384,448},{4... | collective-permute-start | bytes 393224 | tf_op jit(solution)/shard_map/ppermute | solution.py:65
  105.1 4.1 %collective-permute-start.13 = (bf16[2,256,128]{2,1,0:T(8,128)(2,1)S(1)}, bf16[2,256,128]{2,1,0:T(8,128)(2,1)S(1)}, u32[]{:S(2)}, u32[]{:S(2)}) collective-permute-start(bf16[2,256,128]{2,1,0:T(8,128)(2,1)S(1)} %get-tuple-element.35), channel_id=1, source_target_pairs={{0,448},{64,128},{128,64},{192,256},{256,192},{320,384},{384,320},... | collective-permute-start | bytes 393224 | tf_op jit(solution)/shard_map/ppermute | solution.py:65
  109.2 0.0 collective-permute-done.12.from_g
  109.2 4.0 %collective-permute-done.13.from_u = bf16[2,256,128]{2,1,0:T(8,128)(2,1)S(1)} collective-permute-done((bf16[2,256,128]{2,1,0:T(8,128)(2,1)S(1)}, bf16[2,256,128]{2,1,0:T(8,128)(2,1)S(1)}, u32[]{:S(2)}, u32[]{:S(2)}) %collective-permute-start.13) | collective-permute-done | bytes 131104 | tf_op jit(solution)/shard_map/ppermute | solution.py:65
  113.2 0.1 shard_map.97
  113.3 0.0 all-to-all-done.1.t_ref
  113.3 1.1 shard_map.98
  114.3 7.5 %all-to-all-start.2 = ((bf16[8,256,128]{2,1,0:T(8,128)(2,1)}), bf16[8,256,128]{2,1,0:T(8,128)(2,1)S(1)}, u32[]{:S(2)}, u32[]{:S(2)}) async-start(bf16[8,256,128]{2,1,0:T(8,128)(2,1)} %shard_map.98), calls=%async_computation.2 | async-start | bytes 1048576 | tf_op jit(solution)/shard_map/all_to_all | solution.py:316
  121.9 4.1 %collective-permute-start.14 = (bf16[2,256,128]{2,1,0:T(8,128)(2,1)S(1)}, bf16[2,256,128]{2,1,0:T(8,128)(2,1)S(1)}, u32[]{:S(2)}, u32[]{:S(2)}) collective-permute-start(bf16[2,256,128]{2,1,0:T(8,128)(2,1)S(1)} %get-tuple-element.37), channel_id=1, source_target_pairs={{0,256},{64,320},{128,384},{192,448},{256,0},{320,64},{384,128},{4... | collective-permute-start | bytes 393224 | tf_op jit(solution)/shard_map/ppermute | solution.py:65
  126.0 7.8 %collective-permute-done.14.b_ref = bf16[2,256,128]{2,1,0:T(8,128)(2,1)S(1)} collective-permute-done((bf16[2,256,128]{2,1,0:T(8,128)(2,1)S(1)}, bf16[2,256,128]{2,1,0:T(8,128)(2,1)S(1)}, u32[]{:S(2)}, u32[]{:S(2)}) %collective-permute-start.14) | collective-permute-done | bytes 131104 | tf_op jit(solution)/shard_map/ppermute | solution.py:65
  133.7 0.0 copy-done.1
  133.7 0.0 copy-done.2
  133.7 1.6 %shard_map.100 = (bf16[256,512]{1,0:T(8,128)(2,1)}, bf16[256,512]{1,0:T(8,128)(2,1)}) custom-call(s32[2,4]{1,0:T(2,128)S(1)} %copy-done.1, s32[2,4]{1,0:T(2,128)S(1)} %copy-done.2, bf16[2,256,128]{2,1,0:T(8,128)(2,1)S(1)} %get-tuple-element.36._.a_ref, bf16[2,256,128]{2,1,0:T(8,128)(2,1)S(1)} %collective-permute-done.14.b_ref), custom_call_target="tpu_custom_call" | custom-call | tf_op jit(solution)/shard_map/pallas_call | solution.py:319
  135.3 2.1 %all-to-all-done.2.a_ref = bf16[8,256,128]{2,1,0:T(8,128)(2,1)S(1)} async-done(((bf16[8,256,128]{2,1,0:T(8,128)(2,1)}), bf16[8,256,128]{2,1,0:T(8,128)(2,1)S(1)}, u32[]{:S(2)}, u32[]{:S(2)}) %all-to-all-start.2) | async-done | bytes 524320 | tf_op jit(solution)/shard_map/all_to_all | solution.py:316
  137.4 0.7 shard_map.99
  (5 shorter events, 0.0 us)
Async XLA Ops:
  3.1 18.1 %collective-permute-start.4 = (bf16[1,528,128]{2,1,0:T(8,128)(2,1)}, bf16[1,528,128]{2,1,0:T(8,128)(2,1)S(1)}, u32[]{:S(2)}, u32[]{:S(2)}) collective-permute-start(bf16[1,528,128]{2,1,0:T(8,128)(2,1)} %bitcast.4), channel_id=1, source_target_pairs={{0,256},{64,320},{128,384},{192,448},{256,0},{320,64},{384,128},{4... | collective-permute-start | bytes 405512 | tf_op jit(solution)/shard_map/ppermute | solution.py:65
  10.8 27.5 %all-to-all-start = ((bf16[8,256,128]{2,1,0:T(8,128)(2,1)}), bf16[8,256,128]{2,1,0:T(8,128)(2,1)S(1)}, u32[]{:S(2)}, u32[]{:S(2)}) async-start(bf16[8,256,128]{2,1,0:T(8,128)(2,1)} %get-tuple-element.22), calls=%async_computation | async-start | bytes 1048576 | tf_op jit(solution)/shard_map/all_to_all | solution.py:271
  22.1 9.6 %collective-permute-start.5 = (bf16[2,528,128]{2,1,0:T(8,128)(2,1)S(1)}, bf16[2,528,128]{2,1,0:T(8,128)(2,1)S(1)}, u32[]{:S(2)}, u32[]{:S(2)}) collective-permute-start(bf16[2,528,128]{2,1,0:T(8,128)(2,1)S(1)} %pad_maximum_fusion.1), channel_id=1, source_target_pairs={{0,64},{64,0},{128,192},{192,128},{256,320},{320,256},{384,448},{4... | collective-permute-start | bytes 811016 | tf_op jit(solution)/shard_map/ppermute | solution.py:65
  32.6 34.5 %copy-start.3 = (bf16[4,528,128]{2,1,0:T(8,128)(2,1)}, bf16[4,528,128]{2,1,0:T(8,128)(2,1)S(1)}, u32[]{:S(2)}) copy-start(bf16[4,528,128]{2,1,0:T(8,128)(2,1)S(1)} %pad_maximum_fusion.refs_6_) | copy-start | bytes 1622020
  32.6 15.6 %collective-permute-start.6 = (bf16[4,528,128]{2,1,0:T(8,128)(2,1)S(1)}, bf16[4,528,128]{2,1,0:T(8,128)(2,1)S(1)}, u32[]{:S(2)}, u32[]{:S(2)}) collective-permute-start(bf16[4,528,128]{2,1,0:T(8,128)(2,1)S(1)} %pad_maximum_fusion.refs_6_), channel_id=1, source_target_pairs={{0,448},{64,128},{128,64},{192,256},{256,192},{320,384},{384,320},... | collective-permute-start | bytes 1622024 | tf_op jit(solution)/shard_map/ppermute | solution.py:65
  38.4 28.7 %copy-start.4 = (bf16[8,256,128]{2,1,0:T(8,128)(2,1)}, bf16[8,256,128]{2,1,0:T(8,128)(2,1)S(1)}, u32[]{:S(2)}) copy-start(bf16[8,256,128]{2,1,0:T(8,128)(2,1)S(1)} %all-to-all-done.refs_1_) | copy-start | bytes 1572868
  38.4 14.8 %collective-permute-start.1 = (bf16[8,256,128]{2,1,0:T(8,128)(2,1)S(1)}, bf16[8,256,128]{2,1,0:T(8,128)(2,1)S(1)}, u32[]{:S(2)}, u32[]{:S(2)}) collective-permute-start(bf16[8,256,128]{2,1,0:T(8,128)(2,1)S(1)} %all-to-all-done.refs_1_), channel_id=1, source_target_pairs={{0,24},{8,16},{16,8},{24,0},{1,25},{9,17},{17,9},{25,1},{2,26},{10... | collective-permute-start | bytes 1572872 | tf_op jit(solution)/shard_map/ppermute | solution.py:65
  41.8 15.8 %collective-permute-start = (bf16[8,256,128]{2,1,0:T(8,128)(2,1)S(1)}, bf16[8,256,128]{2,1,0:T(8,128)(2,1)S(1)}, u32[]{:S(2)}, u32[]{:S(2)}) collective-permute-start(bf16[8,256,128]{2,1,0:T(8,128)(2,1)S(1)} %all-to-all-done.refs_1_), channel_id=1, source_target_pairs={{0,8},{8,0},{16,24},{24,16},{1,9},{9,1},{17,25},{25,17},{2,10},{10... | collective-permute-start | bytes 1572872 | tf_op jit(solution)/shard_map/ppermute | solution.py:65
  45.5 17.6 %collective-permute-start.7 = (bf16[4,528,128]{2,1,0:T(8,128)(2,1)S(1)}, bf16[4,528,128]{2,1,0:T(8,128)(2,1)S(1)}, u32[]{:S(2)}, u32[]{:S(2)}) collective-permute-start(bf16[4,528,128]{2,1,0:T(8,128)(2,1)S(1)} %pad_maximum_fusion.refs_6_), channel_id=1, source_target_pairs={{0,32},{32,0},{1,33},{33,1},{2,34},{34,2},{3,35},{35,3},{4,36},{36... | collective-permute-start | bytes 1622024 | tf_op jit(solution)/shard_map/ppermute | solution.py:65
  48.3 18.9 %copy-start.7 = (bf16[4,528,128]{2,1,0:T(8,128)(2,1)}, bf16[4,528,128]{2,1,0:T(8,128)(2,1)S(1)}, u32[]{:S(2)}) copy-start(bf16[4,528,128]{2,1,0:T(8,128)(2,1)S(1)} %collective-permute-done.6.refs_7_) | copy-start | bytes 1622020
  48.3 14.8 %collective-permute-start.8 = (bf16[4,528,128]{2,1,0:T(8,128)(2,1)S(1)}, bf16[4,528,128]{2,1,0:T(8,128)(2,1)}, u32[]{:S(2)}, u32[]{:S(2)}) collective-permute-start(bf16[4,528,128]{2,1,0:T(8,128)(2,1)S(1)} %collective-permute-done.6.refs_7_), channel_id=1, source_target_pairs={{0,32},{32,0},{1,33},{33,1},{2,34},{34,2},{3,35},{35,3},{4,36},{36... | collective-permute-start | bytes 1622024 | tf_op jit(solution)/shard_map/ppermute | solution.py:65
  53.2 13.9 %copy-start.5 = (bf16[8,256,128]{2,1,0:T(8,128)(2,1)}, bf16[8,256,128]{2,1,0:T(8,128)(2,1)S(1)}, u32[]{:S(2)}) copy-start(bf16[8,256,128]{2,1,0:T(8,128)(2,1)S(1)} %collective-permute-done.1.refs_3_) | copy-start | bytes 1572868
  54.0 9.1 %collective-permute-start.3 = (bf16[4,256,128]{2,1,0:T(8,128)(2,1)}, bf16[4,256,128]{2,1,0:T(8,128)(2,1)S(1)}, u32[]{:S(2)}, u32[]{:S(2)}) collective-permute-start(bf16[4,256,128]{2,1,0:T(8,128)(2,1)} %slice.9), channel_id=1, source_target_pairs={{0,8},{8,0},{16,24},{24,16},{1,9},{9,1},{17,25},{25,17},{2,10},{10... | collective-permute-start | bytes 786440 | tf_op jit(solution)/shard_map/ppermute | solution.py:65
  57.6 9.5 %copy-start.6 = (bf16[8,256,128]{2,1,0:T(8,128)(2,1)}, bf16[8,256,128]{2,1,0:T(8,128)(2,1)S(1)}, u32[]{:S(2)}) copy-start(bf16[8,256,128]{2,1,0:T(8,128)(2,1)S(1)} %collective-permute-done.refs_2_) | copy-start | bytes 1572868
  58.4 8.7 %collective-permute-start.2 = (bf16[4,256,128]{2,1,0:T(8,128)(2,1)}, bf16[4,256,128]{2,1,0:T(8,128)(2,1)}, u32[]{:S(2)}, u32[]{:S(2)}) collective-permute-start(bf16[4,256,128]{2,1,0:T(8,128)(2,1)} %slice.8), channel_id=1, source_target_pairs={{0,24},{8,16},{16,8},{24,0},{1,25},{9,17},{17,9},{25,1},{2,26},{10... | collective-permute-start | bytes 786440 | tf_op jit(solution)/shard_map/ppermute | solution.py:65
  63.0 4.1 %copy-start.8 = (bf16[4,528,128]{2,1,0:T(8,128)(2,1)}, bf16[4,528,128]{2,1,0:T(8,128)(2,1)S(1)}, u32[]{:S(2)}) copy-start(bf16[4,528,128]{2,1,0:T(8,128)(2,1)S(1)} %collective-permute-done.7.refs_8_) | copy-start | bytes 1622020
  63.1 4.1 %copy-start.9 = (bf16[4,256,128]{2,1,0:T(8,128)(2,1)}, bf16[4,256,128]{2,1,0:T(8,128)(2,1)S(1)}, u32[]{:S(2)}) copy-start(bf16[4,256,128]{2,1,0:T(8,128)(2,1)S(1)} %collective-permute-done.3.refs_5_) | copy-start | bytes 786436
  79.4 10.2 %copy-start = (bf16[2,8,256,128]{3,2,1,0:T(8,128)(2,1)S(1)}, bf16[2,8,256,128]{3,2,1,0:T(8,128)(2,1)}, u32[]{:S(2)}) copy-start(bf16[2,8,256,128]{3,2,1,0:T(8,128)(2,1)} %get-tuple-element.26.keep) | copy-start | bytes 3145732
  79.4 33.9 %all-to-all-start.1 = ((bf16[4,8,256,128]{3,2,1,0:T(8,128)(2,1)}), bf16[4,8,256,128]{3,2,1,0:T(8,128)(2,1)S(1)}, u32[]{:S(2)}, u32[]{:S(2)}) async-start(bf16[4,8,256,128]{3,2,1,0:T(8,128)(2,1)} %get-tuple-element.25), calls=%async_computation.1 | async-start | bytes 4194304 | tf_op jit(solution)/shard_map/all_to_all | solution.py:306
  84.9 4.8 %collective-permute-start.9 = (bf16[2,8,256,128]{3,2,1,0:T(8,128)(2,1)}, bf16[2,8,256,128]{3,2,1,0:T(8,128)(2,1)S(1)}, u32[]{:S(2)}, u32[]{:S(2)}) collective-permute-start(bf16[2,8,256,128]{3,2,1,0:T(8,128)(2,1)} %get-tuple-element.27), channel_id=1, source_target_pairs={{0,32},{32,0},{1,33},{33,1},{2,34},{34,2},{3,35},{35,3},{4,36},{36... | collective-permute-start | bytes 3145736 | tf_op jit(solution)/shard_map/ppermute | solution.py:65
  89.9 11.5 %collective-permute-start.10 = (bf16[4,256,128]{2,1,0:T(8,128)(2,1)S(1)}, bf16[4,256,128]{2,1,0:T(8,128)(2,1)S(1)}, u32[]{:S(2)}, u32[]{:S(2)}) collective-permute-start(bf16[4,256,128]{2,1,0:T(8,128)(2,1)S(1)} %get-tuple-element.29), channel_id=1, source_target_pairs={{0,448},{64,128},{128,64},{192,256},{256,192},{320,384},{384,320},... | collective-permute-start | bytes 786440 | tf_op jit(solution)/shard_map/ppermute | solution.py:65
  92.2 10.0 %collective-permute-start.11 = (bf16[4,256,128]{2,1,0:T(8,128)(2,1)S(1)}, bf16[4,256,128]{2,1,0:T(8,128)(2,1)S(1)}, u32[]{:S(2)}, u32[]{:S(2)}) collective-permute-start(bf16[4,256,128]{2,1,0:T(8,128)(2,1)S(1)} %get-tuple-element.31), channel_id=1, source_target_pairs={{0,64},{64,0},{128,192},{192,128},{256,320},{320,256},{384,448},{4... | collective-permute-start | bytes 786440 | tf_op jit(solution)/shard_map/ppermute | solution.py:65
  102.3 6.9 %collective-permute-start.12 = (bf16[2,256,128]{2,1,0:T(8,128)(2,1)S(1)}, bf16[2,256,128]{2,1,0:T(8,128)(2,1)S(1)}, u32[]{:S(2)}, u32[]{:S(2)}) collective-permute-start(bf16[2,256,128]{2,1,0:T(8,128)(2,1)S(1)} %get-tuple-element.33), channel_id=1, source_target_pairs={{0,64},{64,0},{128,192},{192,128},{256,320},{320,256},{384,448},{4... | collective-permute-start | bytes 393224 | tf_op jit(solution)/shard_map/ppermute | solution.py:65
  105.1 8.1 %collective-permute-start.13 = (bf16[2,256,128]{2,1,0:T(8,128)(2,1)S(1)}, bf16[2,256,128]{2,1,0:T(8,128)(2,1)S(1)}, u32[]{:S(2)}, u32[]{:S(2)}) collective-permute-start(bf16[2,256,128]{2,1,0:T(8,128)(2,1)S(1)} %get-tuple-element.35), channel_id=1, source_target_pairs={{0,448},{64,128},{128,64},{192,256},{256,192},{320,384},{384,320},... | collective-permute-start | bytes 393224 | tf_op jit(solution)/shard_map/ppermute | solution.py:65
  113.2 20.5 %copy-start.1 = (s32[2,4]{1,0:T(2,128)S(1)}, s32[2,4]{1,0:T(2,128)}, u32[]{:S(2)}) copy-start(s32[2,4]{1,0:T(2,128)} %gm_ref.3) | copy-start | bytes 100
  113.2 20.5 %copy-start.2 = (s32[2,4]{1,0:T(2,128)S(1)}, s32[2,4]{1,0:T(2,128)}, u32[]{:S(2)}) copy-start(s32[2,4]{1,0:T(2,128)} %um_ref.3) | copy-start | bytes 100
  114.3 23.1 %all-to-all-start.2 = ((bf16[8,256,128]{2,1,0:T(8,128)(2,1)}), bf16[8,256,128]{2,1,0:T(8,128)(2,1)S(1)}, u32[]{:S(2)}, u32[]{:S(2)}) async-start(bf16[8,256,128]{2,1,0:T(8,128)(2,1)} %shard_map.98), calls=%async_computation.2 | async-start | bytes 1048576 | tf_op jit(solution)/shard_map/all_to_all | solution.py:316
  121.9 11.9 %collective-permute-start.14 = (bf16[2,256,128]{2,1,0:T(8,128)(2,1)S(1)}, bf16[2,256,128]{2,1,0:T(8,128)(2,1)S(1)}, u32[]{:S(2)}, u32[]{:S(2)}) collective-permute-start(bf16[2,256,128]{2,1,0:T(8,128)(2,1)S(1)} %get-tuple-element.37), channel_id=1, source_target_pairs={{0,256},{64,320},{128,384},{192,448},{256,0},{320,64},{384,128},{4... | collective-permute-start | bytes 393224 | tf_op jit(solution)/shard_map/ppermute | solution.py:65
